TPU v7x, 32 devices: a whole 2x2x4 slice. The times are simulated.
32 devices in a mesh: groups: 2 (over y), tensor: 4 (over z), pool: 2 (over x), inner: 2 (over core).
Axes of the slice: x: 2, y: 2, z: 4, core: 2. Of those that a mesh axis runs over, the one named last changes fastest.
Arguments:
- tokens: bfloat16 [3072, 8192], P(('groups', 'pool', 'inner'), 'tensor'), parts along dimension 0, may hold values from -6 to 6
- token_adapter_ids: int32 [3072], P(('groups', 'pool', 'inner')), parts along dimension 0, may hold values from 0 to 7, as said below
- adapter_pool_slot: int32 [16], P('groups'), parts along dimension 0, may hold values from 0 to 7, as said below
- adapter_rank_blocks: int32 [16], P('groups'), parts along dimension 0, may hold values from 1 to 8
- query_weight: bfloat16 [8192, 4096], P(None, 'tensor'), may hold values from -0.0625 to 0.0625
- pool_down_factors: bfloat16 [16, 128, 8192], P(('groups', 'pool', 'inner'), None, 'tensor'), parts along dimension 0, may hold values from -0.0625 to 0.0625
- pool_up_factors: bfloat16 [16, 128, 4096], P(('groups', 'pool', 'inner'), None, 'tensor'), parts along dimension 0, may hold values from -0.5 to 0.5
Outputs:
- query: bfloat16 [3072, 4096], P(('groups', 'pool', 'inner'), 'tensor'), parts along dimension 0
There are 2 independent parts, one for each index of `groups`. A program takes and returns all parts, laid end to end along the dimension named above; an argument that names none is the same for every part. Nothing has to cross between parts.
Inputs may be any that keep to these rules, and one draw needn't show every extreme that they name: `token_adapter_ids`: of the 384 tokens of one device (aligned blocks of the token order), at most 192 have adapters whose slots lie in one aligned group of 2 slots (slots g * 2 to (g + 1) * 2 - 1); in every draw one such group receives exactly 192 tokens from every device. `adapter_pool_slot`: A permutation of the adapters over the slots.
All inputs are finite; a program needn't handle non-finite values.
Results may differ from a plain program's by a relative error of at most 0.0046.
Values may be sent and summed in bfloat16 or wider, within the bound.
No kernel may reach another device: no remote copies, remote signals or barrier semaphores. Data moves between devices by JAX's collectives and lax.ppermute only.
A program may use at most 128 MiB of HBM per device.

v0:
```python
import jax
import jax.numpy as jnp
from jax import lax
from jax.sharding import PartitionSpec as P

MAXIMUM_RANK = 128
RBLK = 16


def lookup(indices, table):
    count = table.shape[0]
    match = indices[..., None] == jnp.arange(count, dtype=jnp.int32)
    return jnp.sum(jnp.where(match, table, 0), axis=-1)


def rank_mask(local, blocks, adapters):
    which = local[:, None, None] == jnp.arange(adapters, dtype=jnp.int32)[None, :, None]
    within = (
        jnp.arange(MAXIMUM_RANK, dtype=jnp.int32)[None, None, :] < (RBLK * blocks)[:, None, None]
    )
    return jnp.logical_and(which, within)


def project_down(rows, factors, mask):
    flat = factors.reshape(-1, factors.shape[2])
    coords = lax.dot_general(
        rows, flat, (((1,), (1,)), ((), ())), preferred_element_type=jnp.float32
    )
    coords = coords.reshape(rows.shape[0], factors.shape[0], MAXIMUM_RANK)
    return jnp.sum(jnp.where(mask, coords, 0.0), axis=1)


def project_up(coords, factors, mask):
    spread = jnp.where(mask, coords[:, None, :], jnp.zeros((), jnp.bfloat16))
    spread = spread.reshape(coords.shape[0], -1)
    flat = factors.reshape(-1, factors.shape[2])
    return jnp.dot(spread, flat, preferred_element_type=jnp.float32)


def rank_total(coords):
    return lax.psum(coords, "tensor")


def shards(
    tokens,
    token_adapter_ids,
    adapter_pool_slot,
    adapter_rank_blocks,
    query_weight,
    pool_down_factors,
    pool_up_factors,
):
    rows = tokens.shape[0]
    width = tokens.shape[1]
    columns = query_weight.shape[1]
    adapters_dev = pool_down_factors.shape[0]
    base = jnp.dot(
        lax.all_gather(tokens, "tensor", axis=1, tiled=True),
        query_weight,
        preferred_element_type=jnp.float32,
    )
    slot_row = lookup(token_adapter_ids, adapter_pool_slot)
    owners = lax.axis_size(("pool", "inner"))
    mine = lax.axis_index(("pool", "inner"))
    capacity = 2 * rows // owners
    home = slot_row // adapters_dev
    hits = (home[:, None] == jnp.arange(owners, dtype=jnp.int32)[None, :]).astype(jnp.int32)
    place = jnp.sum(hits * (jnp.cumsum(hits, axis=0) - 1), axis=1)
    target = home * capacity + place
    source = (
        jnp.full((owners * capacity,), rows, jnp.int32)
        .at[target]
        .set(jnp.arange(rows, dtype=jnp.int32))
    )
    padded_rows = jnp.concatenate([tokens, jnp.zeros((1, width), jnp.bfloat16)], axis=0)
    padded_ids = jnp.concatenate([token_adapter_ids, jnp.full((1,), -1, jnp.int32)], axis=0)
    send_rows = padded_rows[source].reshape(owners, capacity, width)
    send_ids = padded_ids[source].reshape(owners, capacity)
    arrived_rows = lax.all_to_all(
        send_rows, ("pool", "inner"), split_axis=0, concat_axis=0, tiled=True
    )
    senders = arrived_rows.shape[0]
    items = arrived_rows.shape[1]
    flat_rows = arrived_rows.reshape(senders * items, width)
    flat_ids = lax.all_to_all(
        send_ids, ("pool", "inner"), split_axis=0, concat_axis=0, tiled=True
    ).reshape(senders * items)
    local = lookup(flat_ids, adapter_pool_slot) - mine * adapters_dev
    blocks = lookup(flat_ids, adapter_rank_blocks)
    mask = rank_mask(local, blocks, adapters_dev)
    coords = rank_total(project_down(flat_rows, pool_down_factors, mask)).astype(jnp.bfloat16)
    terms = project_up(coords, pool_up_factors, mask).astype(jnp.bfloat16)
    back = lax.all_to_all(
        terms.reshape(senders, items, columns),
        ("pool", "inner"),
        split_axis=0,
        concat_axis=0,
        tiled=True,
    )
    delta_rows = back.reshape(owners * capacity, columns)[target]
    return (base + delta_rows.astype(jnp.float32)).astype(jnp.bfloat16)


def solution(mesh):
    in_specs = (
        P(("groups", "pool", "inner"), "tensor"),
        P(("groups", "pool", "inner")),
        P("groups"),
        P("groups"),
        P(None, "tensor"),
        P(("groups", "pool", "inner"), None, "tensor"),
        P(("groups", "pool", "inner"), None, "tensor"),
    )
    out_specs = P(("groups", "pool", "inner"), "tensor")
    return jax.shard_map(shards, mesh=mesh, in_specs=in_specs, out_specs=out_specs, check_vma=False)
```

profile of v0, /device:TPU:0, one launch (start us, length us, event | category | flops | bytes accessed | tf_op | source)
XLA Modules:
  0.0 162.1 jit_solution(17974204592836649624)
XLA Ops:
  6.5 0.7 all-gather.2.cloned.1.call-update
  7.3 0.8 select_reduce_fusion.2
  8.1 1.2 reduce-window.6
  9.3 0.2 slice_reduce_fusion
  9.5 0.2 reduce-window.9
  9.8 2.9 %scatter_custom_fusion = s32[768]{0:T(1024)S(1)} fusion(s32[384]{0:T(512)S(1)} %fusion.15, s32[384]{0:T(512)S(1)} %iota.34, s32[]{:T(128)} %constant.16.clone.1), kind=kCustom, calls=%fused_computation.53 | custom fusion | bytes 3076 | tf_op jit(solution)/shard_map/scatter | solution.py:73
  12.8 0.7 pad_add_fusion
  13.5 5.0 %gather_fusion = s32[768]{0:T(1024)S(1)} fusion(s32[385]{0:T(512)S(1)} %pad_add_fusion, s32[1024]{0:T(1024)S(1)} %pad_clamp_fusion.1), kind=kCustom, calls=%fused_computation | custom fusion | bytes 9216 | tf_op jit(solution)/shard_map/gather | solution.py:78
  18.5 0.7 all_to_all.12
  19.1 4.2 %all-to-all-start = ((s32[4,1,192]{2,1,0:T(1,128)}), s32[4,1,192]{2,1,0:T(1,128)S(1)}, u32[]{:S(2)}, u32[]{:S(2)}) async-start(s32[4,1,192]{2,1,0:T(1,128)} %all_to_all.12), calls=%async_computation | async-start | bytes 8192 | tf_op jit(solution)/shard_map/all_to_all | solution.py:85
  23.4 1.5 concatenate.7
  24.9 4.2 %gather_fusion.1 = bf16[768,2048]{1,0:T(8,128)(2,1)} fusion(bf16[385,2048]{1,0:T(8,128)(2,1)S(1)} %concatenate.7, s32[1024]{0:T(1024)S(1)} %pad_clamp_fusion.1), kind=kCustom, calls=%fused_computation.1 | custom fusion | bytes 6294528 | tf_op jit(solution)/shard_map/gather | solution.py:77
  29.1 4.8 %all-to-all-start.1 = ((bf16[4,192,2048]{2,1,0:T(8,128)(2,1)}), bf16[4,192,2048]{2,1,0:T(8,128)(2,1)}, u32[]{:S(2)}, u32[]{:S(2)}) async-start(bf16[4,192,2048]{2,1,0:T(8,128)(2,1)} %bitcast.45), calls=%async_computation.1 | async-start | bytes 6291456 | tf_op jit(solution)/shard_map/all_to_all | solution.py:79
  34.0 0.1 eq.83
  34.1 0.1 select_reduce_fusion.1
  34.2 0.2 iota_compare_fusion
  34.4 36.7 %all-to-all-done.1 = bf16[4,192,2048]{2,1,0:T(8,128)(2,1)} async-done(((bf16[4,192,2048]{2,1,0:T(8,128)(2,1)}), bf16[4,192,2048]{2,1,0:T(8,128)(2,1)}, u32[]{:S(2)}, u32[]{:S(2)}) %all-to-all-start.1) | async-done | bytes 3145760 | tf_op jit(solution)/shard_map/all_to_all | solution.py:79
  71.0 3.0 %fusion = f32[768,128]{1,0:T(8,128)S(1)} fusion(bf16[768,2048,1]{1,0,2:T(8,128)(2,1)} %bitcast.4, bf16[2,128,2048]{2,1,0:T(8,128)(2,1)S(1)} %copy-done, pred[768,128]{1,0:T(8,128)(4,1)S(1)} %iota_compare_fusion, pred[768,2]{0,1:T(4,128)(4,1)S(1)} %iota_compare_fusion.4), kind=kOutput, calls=%fused_computation.7 | convolution fusion | flops 805797888 | bytes 4687360 | tf_op jit(solution)/shard_map/dot_general | solution.py:26
  74.1 40.8 %all-reduce.2 = bf16[768,128]{1,0:T(8,128)(2,1)S(1)} all-reduce(f32[768,128]{1,0:T(8,128)S(1)} %fusion), channel_id=1, replica_groups=mesh['groups'=2,'tensor'=4,'pool'=2,'inner'=2] {'tensor'}, use_global_device_ids=true, to_apply=%region_8.9 | all-reduce | flops 98304 | bytes 589824 | tf_op jit(solution)/shard_map/psum | solution.py:41
  114.9 1.8 %bitcast_convert_fusion = bf16[768,1024]{1,0:T(8,128)(2,1)} fusion(bf16[2,128,1024]{2,1,0:T(8,128)(2,1)S(1)} %copy-done.1, pred[768,128]{1,0:T(8,128)(4,1)S(1)} %iota_compare_fusion, pred[768,2]{0,1:T(4,128)(4,1)S(1)} %iota_compare_fusion.4, bf16[768,128]{1,0:T(8,128)(2,1)S(1)} %all-reduce.2), kind=kOutput, calls=%fused_computation.4 | convolution fusion | flops 403832832 | bytes 2393600 | tf_op jit(solution)/shard_map/dot_general | solution.py:37
  116.7 3.6 %all-to-all-start.2 = ((bf16[4,192,1024]{2,1,0:T(8,128)(2,1)}), bf16[4,192,1024]{2,1,0:T(8,128)(2,1)S(1)}, u32[]{:S(2)}, u32[]{:S(2)}) async-start(bf16[4,192,1024]{2,1,0:T(8,128)(2,1)} %bitcast.46), calls=%async_computation.2 | async-start | bytes 3145728 | tf_op jit(solution)/shard_map/all_to_all | solution.py:93
  120.3 20.0 %all-to-all-done.2 = bf16[4,192,1024]{2,1,0:T(8,128)(2,1)S(1)} async-done(((bf16[4,192,1024]{2,1,0:T(8,128)(2,1)}), bf16[4,192,1024]{2,1,0:T(8,128)(2,1)S(1)}, u32[]{:S(2)}, u32[]{:S(2)}) %all-to-all-start.2) | async-done | bytes 1572896 | tf_op jit(solution)/shard_map/all_to_all | solution.py:93
  140.3 2.1 %gather_fusion.2 = bf16[384,1024]{1,0:T(8,128)(2,1)S(1)} fusion(bf16[768,1024]{1,0:T(8,128)(2,1)S(1)} %bitcast.44, s32[1024]{0:T(1024)S(1)} %pad_clamp_fusion), kind=kCustom, calls=%fused_computation.2 | custom fusion | bytes 1574400 | tf_op jit(solution)/shard_map/gather | solution.py:100
  142.4 12.9 %add_convert_fusion = bf16[384,1024]{1,0:T(8,128)(2,1)} fusion(bf16[384,1024]{1,0:T(8,128)(2,1)S(1)} %gather_fusion.2, bf16[384,8192]{1,0:T(8,128)(2,1)} %all-gather.2.cloned.1.call-done, bf16[8192,1024]{1,0:T(8,128)(2,1)} %param.11), kind=kOutput, calls=%fused_computation.5 | convolution fusion | flops 6443630592 | bytes 24641536 | tf_op jit(solution)/shard_map/dot_general | solution.py:57
  (24 shorter events, 0.3 us)
Async XLA Ops:
  6.5 64.5 %copy-start = (bf16[2,128,2048]{2,1,0:T(8,128)(2,1)S(1)}, bf16[2,128,2048]{2,1,0:T(8,128)(2,1)}, u32[]{:S(2)}) copy-start(bf16[2,128,2048]{2,1,0:T(8,128)(2,1)} %param.12) | copy-start | bytes 3145732
  6.5 135.9 %all-gather.2.cloned.1.call-start = ((), (), s32[]{:S(2)}) async-start(), calls=%async_computation.3 | async-start | bytes 7864320 | tf_op jit(solution)/shard_map/all_gather | solution.py:58
  19.1 10.0 %all-to-all-start = ((s32[4,1,192]{2,1,0:T(1,128)}), s32[4,1,192]{2,1,0:T(1,128)S(1)}, u32[]{:S(2)}, u32[]{:S(2)}) async-start(s32[4,1,192]{2,1,0:T(1,128)} %all_to_all.12), calls=%async_computation | async-start | bytes 8192 | tf_op jit(solution)/shard_map/all_to_all | solution.py:85
  29.1 4.9 %copy-start.2 = (s32[8]{0:T(128)S(1)}, s32[8]{0:T(128)}, u32[]{:S(2)}) copy-start(s32[8]{0:T(128)} %param.9) | copy-start | bytes 100
  29.1 4.9 %copy-start.3 = (s32[8]{0:T(128)S(1)}, s32[8]{0:T(128)}, u32[]{:S(2)}) copy-start(s32[8]{0:T(128)} %param.10) | copy-start | bytes 100
  29.1 41.9 %all-to-all-start.1 = ((bf16[4,192,2048]{2,1,0:T(8,128)(2,1)}), bf16[4,192,2048]{2,1,0:T(8,128)(2,1)}, u32[]{:S(2)}, u32[]{:S(2)}) async-start(bf16[4,192,2048]{2,1,0:T(8,128)(2,1)} %bitcast.45), calls=%async_computation.1 | async-start | bytes 6291456 | tf_op jit(solution)/shard_map/all_to_all | solution.py:79
  71.0 43.9 %copy-start.1 = (bf16[2,128,1024]{2,1,0:T(8,128)(2,1)S(1)}, bf16[2,128,1024]{2,1,0:T(8,128)(2,1)}, u32[]{:S(2)}) copy-start(bf16[2,128,1024]{2,1,0:T(8,128)(2,1)} %param.13) | copy-start | bytes 1572868
  116.7 23.6 %all-to-all-start.2 = ((bf16[4,192,1024]{2,1,0:T(8,128)(2,1)}), bf16[4,192,1024]{2,1,0:T(8,128)(2,1)S(1)}, u32[]{:S(2)}, u32[]{:S(2)}) async-start(bf16[4,192,1024]{2,1,0:T(8,128)(2,1)} %bitcast.46), calls=%async_computation.2 | async-start | bytes 3145728 | tf_op jit(solution)/shard_map/all_to_all | solution.py:93
Sparse Core Ops, SparseCore 0:
  8.9 130.5 all-gather.1
where the time goes:
time: 163 us; the launch traced here: 162 us
  waiting for transfers between devices  57.4 us (35%)
  blocking collectives  40.8 us (25%)
  matrix products  17.7 us (11%)
  local copies, waits for them, and re-layouts  16.7 us (10%)
  between operations  13.5 us (8%)
  starting transfers between devices  12.6 us (8%)
  other arithmetic  3.34 us (2%)
    psum x1, blocking collectives, rank_total(): return lax.psum(coords, 'tensor')  40.8 us
    all_to_all x1, waiting for transfers between devices, shards(): lax.all_to_all(send_rows, ('pool', 'inner'), split_axis=0, concat_axis=0,...  36.7 us
    all_to_all x1, waiting for transfers between devices, shards(): lax.all_to_all(terms.reshape(senders, items, columns), ('pool', 'inner'),...  20 us
    dot_general x1, matrix products, shards(): jnp.dot(lax.all_gather(tokens, 'tensor', axis=1, tiled=True), query_weigh...  12.9 us
    gather x1, local copies, waits for them, and re-layouts, shards(): send_ids = padded_ids[source].reshape(owners, capacity)  5 us
    all_to_all x1, starting transfers between devices, shards(): lax.all_to_all(send_rows, ('pool', 'inner'), split_axis=0, concat_axis=0,...  4.79 us
    gather x1, local copies, waits for them, and re-layouts, shards(): send_rows = padded_rows[source].reshape(owners, capacity, width)  4.24 us
    all_to_all x1, starting transfers between devices, shards(): lax.all_to_all(send_ids, ('pool', 'inner'), split_axis=0, concat_axis=0,...  4.21 us
  transfers between devices with their start and end apart: 4, of which 2 were waited for; matrix products, arithmetic and copies ran while one was open for 15% of the time, Pallas kernels for 0%

commit v1 on v0

v1 whole, which is shorter than its diff:
```python
import functools

import jax
import jax.numpy as jnp
from jax import lax
from jax.experimental import pallas as pl
from jax.experimental.pallas import tpu as pltpu
from jax.sharding import PartitionSpec as P

MAXIMUM_RANK = 128
RBLK = 16
AXES = ("groups", "tensor", "pool", "inner")

PAIRS = [(0, 1), (1, 0), (2, 3), (3, 2)]
MIDDLE = [(1, 2), (2, 1)]
OUTWARD = [(1, 0), (2, 3)]
INWARD = [(0, 1), (3, 2)]
STEPS = 4


def lookup(indices, table):
    count = table.shape[0]
    match = indices[..., None] == jnp.arange(count, dtype=jnp.int32)
    return jnp.sum(jnp.where(match, table, 0), axis=-1)


def swap(x, axis):
    return lax.ppermute(x, axis, [(0, 1), (1, 0)])


def hop(x, pairs):
    return lax.ppermute(x, "tensor", pairs)


def after(x, *others):
    return lax.optimization_barrier((x,) + others)[0]


def owner_mask(owner, slot, rank, adapters):
    local = slot - owner * adapters
    which = local[:, None, None] == jnp.arange(adapters, dtype=jnp.int32)[None, :, None]
    within = jnp.arange(MAXIMUM_RANK, dtype=jnp.int32)[None, None, :] < rank[:, None, None]
    return jnp.logical_and(which, within)


def project_down(tokens, down, mask):
    flat = down.reshape(-1, down.shape[2])
    coords = lax.dot_general(
        tokens, flat, (((1,), (1,)), ((), ())), preferred_element_type=jnp.float32
    )
    return jnp.sum(jnp.where(mask, coords.reshape(mask.shape), 0.0), axis=1)


def project_up(coords, up, mask):
    spread = jnp.where(mask, coords[:, None, :], jnp.zeros((), jnp.bfloat16))
    spread = spread.reshape(coords.shape[0], -1)
    flat = up.reshape(-1, up.shape[2])
    return jnp.dot(spread, flat, preferred_element_type=jnp.float32)


def add_dot(out_ref, a, b):
    out_ref[...] += jnp.dot(a, b, preferred_element_type=jnp.float32)


def cost(rows, depth, columns):
    return pl.CostEstimate(
        flops=2 * rows * depth * columns,
        bytes_accessed=2 * (rows * depth + depth * columns) + 4 * rows * columns,
        transcendentals=0,
    )


def own_block(tokens, weight, index, depth=512):
    rows, width = tokens.shape
    columns = weight.shape[1]
    steps = width // depth

    def body(index_ref, a_ref, w_ref, out_ref):
        @pl.when(pl.program_id(0) == 0)
        def _():
            out_ref[...] = jnp.zeros_like(out_ref)

        add_dot(out_ref, a_ref[...], w_ref[...])

    return pl.pallas_call(
        body,
        out_shape=jax.ShapeDtypeStruct((rows, columns), jnp.float32),
        grid_spec=pltpu.PrefetchScalarGridSpec(
            num_scalar_prefetch=1,
            grid=(steps,),
            in_specs=[
                pl.BlockSpec((rows, depth), lambda k, i: (0, k)),
                pl.BlockSpec((depth, columns), lambda k, i: (i[0] * steps + k, 0)),
            ],
            out_specs=pl.BlockSpec((rows, columns), lambda k, i: (0, 0)),
        ),
        cost_estimate=cost(rows, width, columns),
        compiler_params=pltpu.CompilerParams(vmem_limit_bytes=24 << 20),
    )(index.reshape(1).astype(jnp.int32), tokens, weight)


def near_blocks(total, outer, inner, across, relayed, weight, end, partner, near, depth=512):
    rows, width = outer.shape
    columns = weight.shape[1]
    steps = width // depth
    half = relayed.shape[1] // depth
    count = len(inner)
    size = rows // count

    def body(s_ref, *refs):
        inner_refs = refs[:count]
        outer_ref, across_ref, relayed_ref, w_ref, total_ref, out_ref = refs[count:]
        k = pl.program_id(0)
        at_end = s_ref[0] == 1

        @pl.when(k == 0)
        def _():
            out_ref[...] = total_ref[...]

        @pl.when(jnp.logical_and(k < steps, at_end))
        def _():
            add_dot(out_ref, outer_ref[...], w_ref[...])

        @pl.when(jnp.logical_and(k < steps, jnp.logical_not(at_end)))
        def _():
            a = jnp.concatenate([r[...] for r in inner_refs], axis=0)
            add_dot(out_ref, a, w_ref[...])

        @pl.when(jnp.logical_and(jnp.logical_and(k >= steps, k < steps + half), at_end))
        def _():
            add_dot(out_ref, relayed_ref[...], w_ref[...])

        @pl.when(jnp.logical_and(k >= steps, jnp.logical_not(at_end)))
        def _():
            add_dot(out_ref, across_ref[...], w_ref[...])

    first = lambda k, s: (0, jnp.minimum(k, steps - 1))
    second = lambda k, s: (0, jnp.maximum(k - steps, 0))
    some = lambda k, s: (0, jnp.clip(k - steps, 0, half - 1))
    rows_of = lambda k, s: (
        jnp.where(k < steps, s[1] * steps + k, s[2] * steps + k - steps),
        0,
    )
    whole = lambda k, s: (0, 0)
    scalars = jnp.stack([end.astype(jnp.int32), partner, near]).astype(jnp.int32)
    return pl.pallas_call(
        body,
        out_shape=jax.ShapeDtypeStruct((rows, columns), jnp.float32),
        grid_spec=pltpu.PrefetchScalarGridSpec(
            num_scalar_prefetch=1,
            grid=(2 * steps,),
            in_specs=[pl.BlockSpec((size, depth), first)] * count
            + [
                pl.BlockSpec((rows, depth), first),
                pl.BlockSpec((rows, depth), second),
                pl.BlockSpec((rows, depth), some),
                pl.BlockSpec((depth, columns), rows_of),
                pl.BlockSpec((rows, columns), whole),
            ],
            out_specs=pl.BlockSpec((rows, columns), whole),
        ),
        cost_estimate=cost(rows, 2 * width, columns),
        compiler_params=pltpu.CompilerParams(vmem_limit_bytes=32 << 20),
    )(scalars, *inner, outer, across, relayed, weight, total)


def far_block(total, far, weight, index, place, depth=512):
    size, width = far[0].shape
    rows = size * len(far)
    columns = weight.shape[1]
    steps = width // depth

    def body(index_ref, *refs):
        *far_refs, w_ref, total_ref, out_ref = refs

        @pl.when(pl.program_id(0) == 0)
        def _():
            out_ref[...] = total_ref[...]

        a = jnp.concatenate([r[...] for r in far_refs], axis=0)
        add_dot(out_ref, a, w_ref[...])

    return pl.pallas_call(
        body,
        out_shape=jax.ShapeDtypeStruct((rows, columns), jnp.float32),
        grid_spec=pltpu.PrefetchScalarGridSpec(
            num_scalar_prefetch=1,
            grid=(steps,),
            in_specs=[pl.BlockSpec((size, depth), lambda k, i: (0, k))] * len(far)
            + [
                pl.BlockSpec((depth, columns), lambda k, i: (i[0] * steps + k, 0)),
                pl.BlockSpec((rows, columns), lambda k, i: (place, 0)),
            ],
            out_specs=pl.BlockSpec((rows, columns), lambda k, i: (0, 0)),
        ),
        cost_estimate=cost(rows, width, columns),
        compiler_params=pltpu.CompilerParams(vmem_limit_bytes=24 << 20),
    )(index.reshape(1).astype(jnp.int32), *far, weight, total)


def helped(far, across, place, pieces):
    size, width = far[0].shape
    rows = size * len(far)
    columns = pieces[0][1].shape[1]
    deep = width // len(pieces)
    half = width // 2
    shallow = half // len(pieces)

    def body(place_ref, *refs):
        far_refs = refs[: len(far)]
        across_ref = refs[len(far)]
        piece_refs = refs[len(far) + 1 : -1]
        out_ref = refs[-1]
        total = jnp.zeros(out_ref.shape, jnp.float32)
        for i, piece_ref in enumerate(piece_refs):
            q = place_ref[i]
            columns_far = pl.ds(pl.multiple_of(q * deep, deep), deep)
            columns_near = pl.ds(pl.multiple_of(q * shallow, shallow), shallow)
            a = jnp.concatenate([r[:, columns_far] for r in far_refs], axis=0)
            total += jnp.dot(a, piece_ref[:deep, :], preferred_element_type=jnp.float32)
            total += jnp.dot(
                across_ref[:, columns_near],
                piece_ref[deep:, :],
                preferred_element_type=jnp.float32,
            )
        out_ref[...] = total.astype(out_ref.dtype)

    whole = lambda k, s: (0, 0)
    return pl.pallas_call(
        body,
        out_shape=jax.ShapeDtypeStruct((rows, columns), jnp.bfloat16),
        grid_spec=pltpu.PrefetchScalarGridSpec(
            num_scalar_prefetch=1,
            grid=(1,),
            in_specs=[pl.BlockSpec((size, width), whole)] * len(far)
            + [pl.BlockSpec((rows, half), lambda k, s: (place, 1))]
            + [pl.BlockSpec(pieces[0][1].shape, whole)] * len(pieces),
            out_specs=pl.BlockSpec((rows, columns), whole),
        ),
        cost_estimate=cost(rows, width + half, columns),
        compiler_params=pltpu.CompilerParams(vmem_limit_bytes=40 << 20),
    )(
        jnp.stack([q for q, _ in pieces]).astype(jnp.int32),
        *far,
        across,
        *[piece for _, piece in pieces],
    )


def chained(tokens, slot, rank, weight, down, up):
    rows, width = tokens.shape
    adapters = down.shape[0]
    size = rows // STEPS
    z = lax.axis_index("tensor")
    end = jnp.logical_or(z == 0, z == 3)
    mine = lax.axis_index(("pool", "inner"))
    seat = lax.axis_index(("groups", "pool", "inner"))
    partner, near, far = z ^ 1, jnp.where(end, 3 - (z ^ 1), 3 - z), 3 - (z ^ 1)
    deep, shallow = width // 8, width // 16

    def part(i):
        return tokens[i * size : (i + 1) * size]

    piece = jnp.concatenate(
        [
            lax.dynamic_slice_in_dim(weight, (3 - z) * width + seat * deep, deep, 0),
            lax.dynamic_slice_in_dim(
                weight, near * width + width // 2 + seat * shallow, shallow, 0
            ),
        ],
        axis=0,
    )
    across = hop(tokens, MIDDLE)
    lent = hop(piece, INWARD)
    outer = hop(tokens, OUTWARD)
    down_x = swap(down, "pool")
    inner = [hop(part(0), INWARD), hop(part(1), INWARD), hop(part(2), INWARD)]
    down_c, up_c = swap(down, "inner"), swap(up, "inner")
    total = own_block(tokens, weight, z)
    masks = [owner_mask(mine ^ r, slot, rank, adapters) for r in range(4)]
    coords = project_down(tokens, down, masks[0]) + project_down(tokens, down_c, masks[1])

    lent_y, lent_x = swap(lent, "groups"), swap(lent, "pool")
    lent_c = swap(lent, "inner")
    up_x = swap(after(up, lent), "pool")
    down_xc = swap(down_x, "inner")
    coords = coords + project_down(tokens, down_x, masks[2])
    coords = coords + project_down(tokens, down_xc, masks[3])
    coords = coords.astype(jnp.bfloat16)
    pair = coords.astype(jnp.float32) + hop(coords, PAIRS).astype(jnp.float32)
    pair = pair.astype(jnp.bfloat16)
    inner.append(hop(after(part(3), coords), INWARD))
    relayed = hop(across[:, : width // 2], OUTWARD)
    beyond = [hop(inner[0], MIDDLE), hop(inner[1], MIDDLE)]
    lent_d = swap(lent_x, "groups")
    lent_yc, lent_xc = swap(lent_y, "inner"), swap(lent_x, "inner")
    whole = (pair.astype(jnp.float32) + hop(pair, MIDDLE).astype(jnp.float32)).astype(
        jnp.bfloat16
    )
    beyond.append(hop(after(inner[2], pair), MIDDLE))
    beyond.append(hop(inner[3], MIDDLE))
    low_rank = jnp.where(end, hop(whole, OUTWARD), whole)
    up_xc = swap(up_x, "inner")
    lent_dc = swap(lent_d, "inner")
    pieces = [
        (seat, lent),
        (seat ^ 1, lent_c),
        (seat ^ 2, lent_x),
        (seat ^ 3, lent_xc),
        (seat ^ 4, lent_y),
        (seat ^ 5, lent_yc),
        (seat ^ 6, lent_d),
        (seat ^ 7, lent_dc),
    ]
    total = near_blocks(total, outer, inner, across, relayed, weight, end, partner, near)
    delta = 0.0
    for mask, factors in zip(masks, (up, up_c, up_x, up_xc)):
        delta = delta + project_up(low_rank, factors, mask)
    total = total + delta.astype(jnp.bfloat16).astype(jnp.float32)
    early = hop(helped(beyond[:3], across, 0, pieces), OUTWARD)
    total_early = far_block(total, beyond[:3], weight, far, 0)
    late = hop(helped(beyond[3:], across, 3, pieces), OUTWARD)
    total_late = far_block(total, beyond[3:], weight, far, 3)
    return (
        jnp.concatenate([total_early, total_late], axis=0)
        + jnp.concatenate([early, late], axis=0).astype(jnp.float32)
    ).astype(jnp.bfloat16)


def gathered(tokens, slot, rank, weight, down, up):
    axes = ("pool", "inner")
    adapters = down.shape[0]
    base = jnp.dot(
        lax.all_gather(tokens, "tensor", axis=1, tiled=True),
        weight,
        preferred_element_type=jnp.float32,
    )
    downs = lax.all_gather(down, axes, axis=0, tiled=True)
    ups = lax.all_gather(up, axes, axis=0, tiled=True)
    mask = owner_mask(0, slot, rank, adapters * lax.axis_size(axes))
    coords = lax.psum(project_down(tokens, downs, mask), "tensor").astype(jnp.bfloat16)
    delta = project_up(coords, ups, mask).astype(jnp.bfloat16)
    return (base + delta.astype(jnp.float32)).astype(jnp.bfloat16)


def shards(
    tokens,
    token_adapter_ids,
    adapter_pool_slot,
    adapter_rank_blocks,
    query_weight,
    pool_down_factors,
    pool_up_factors,
):
    slot = lookup(token_adapter_ids, adapter_pool_slot)
    rank = RBLK * lookup(token_adapter_ids, adapter_rank_blocks)
    whole_chain = tuple(lax.axis_size(a) for a in AXES) == (2, 4, 2, 2)
    run = chained if whole_chain else gathered
    return run(tokens, slot, rank, query_weight, pool_down_factors, pool_up_factors)


def solution(mesh):
    in_specs = (
        P(("groups", "pool", "inner"), "tensor"),
        P(("groups", "pool", "inner")),
        P("groups"),
        P("groups"),
        P(None, "tensor"),
        P(("groups", "pool", "inner"), None, "tensor"),
        P(("groups", "pool", "inner"), None, "tensor"),
    )
    out_specs = P(("groups", "pool", "inner"), "tensor")
    return jax.shard_map(shards, mesh=mesh, in_specs=in_specs, out_specs=out_specs, check_vma=False)
```

time: 163 us -> 188 us (1.15)
  blocking collectives: 40.8 us -> 0 us
  waiting for transfers between devices: 57.4 us -> 96.4 us
  starting transfers between devices: 12.6 us -> 37.5 us
  Pallas kernels: 0 us -> 23.6 us
  between operations: 13.5 us -> 0.64 us
  matrix products: 17.7 us -> 8.12 us
    ppermute x0 -> x30, waiting for transfers between devices: none -> 96.4 us  [the longest x17 59.2 us: hop(): return lax.ppermute(x, 'tensor', pairs)]
    all_to_all x3 -> x0, waiting for transfers between devices: 56.7 us -> none  [the longest x1 36.7 us: shards(): lax.all_to_all(send_rows, ('pool', 'inner'), split_axis=0, concat_axis=0,...]
    psum x1 -> x0, blocking collectives: 40.8 us -> none  [rank_total(): return lax.psum(coords, 'tensor')]
    ppermute x0 -> x30, starting transfers between devices: none -> 37.5 us  [the longest x17 29.7 us: hop(): return lax.ppermute(x, 'tensor', pairs)]
    pallas_call x0 -> x6, Pallas kernels: none -> 23.6 us  [the longest x1 8.89 us: near_blocks(): pl.pallas_call(body, out_shape=jax.ShapeDtypeStruct((rows, columns), jnp....]
    all_to_all x3 -> x0, starting transfers between devices: 12.6 us -> none  [the longest x1 4.79 us: shards(): lax.all_to_all(send_rows, ('pool', 'inner'), split_axis=0, concat_axis=0,...]
    unnamed x8 -> x40, local copies, waits for them, and re-layouts: 0.02 us -> 12.4 us
    gather x3 -> x0, local copies, waits for them, and re-layouts: 11.3 us -> none  [the longest x1 5 us: shards(): send_ids = padded_ids[source].reshape(owners, capacity)]
  transfers between devices with their start and end apart: 4 -> 30, of which waited for: 2 -> 8; matrix products, arithmetic and copies ran while one was open for 15% -> 8% of each run, Pallas kernels for 0% -> 13%
where the time goes in v1:
time: 188 us; the launch traced here: 187 us
  waiting for transfers between devices  96.4 us (51%)
  starting transfers between devices  37.5 us (20%)
  Pallas kernels  23.6 us (13%)
  local copies, waits for them, and re-layouts  17.3 us (9%)
  matrix products  8.12 us (4%)
  other arithmetic  3.19 us (2%)
    ppermute x17, waiting for transfers between devices, hop(): return lax.ppermute(x, 'tensor', pairs)  59.2 us
    ppermute x13, waiting for transfers between devices, swap(): return lax.ppermute(x, axis, [(0, 1), (1, 0)])  37.2 us
    ppermute x17, starting transfers between devices, hop(): return lax.ppermute(x, 'tensor', pairs)  29.7 us
    unnamed x40, local copies, waits for them, and re-layouts  12.4 us
    pallas_call x1, Pallas kernels, near_blocks(): pl.pallas_call(body, out_shape=jax.ShapeDtypeStruct((rows, columns), jnp....  8.89 us
    pallas_call x2, Pallas kernels, helped(): pl.pallas_call(body, out_shape=jax.ShapeDtypeStruct((rows, columns), jnp....  8.65 us
    ppermute x13, starting transfers between devices, swap(): return lax.ppermute(x, axis, [(0, 1), (1, 0)])  7.78 us
    dot_general x4, matrix products, project_down(): lax.dot_general(tokens, flat, (((1,), (1,)), ((), ())), preferred_element...  6.39 us
  transfers between devices with their start and end apart: 30, of which 8 were waited for; matrix products, arithmetic and copies ran while one was open for 8% of the time, Pallas kernels for 13%

profile of v1, /device:TPU:0, one launch (start us, length us, event | category | flops | bytes accessed | tf_op | source)
XLA Modules:
  0.0 186.7 jit_solution(17583504264303261226)
XLA Ops:
  0.0 2.9 %collective-permute-start.6 = (bf16[2,128,2048]{2,1,0:T(8,128)(2,1)}, bf16[2,128,2048]{2,1,0:T(8,128)(2,1)}, u32[]{:S(2)}, u32[]{:S(2)}) collective-permute-start(bf16[2,128,2048]{2,1,0:T(8,128)(2,1)} %param.12), channel_id=1, source_target_pairs={{0,2},{2,0},{1,3},{3,1},{4,6},{6,4},{5,7},{7,5},{8,10},{10,8},{9,1... | collective-permute-start | bytes 3145736 | tf_op jit(solution)/shard_map/ppermute | solution.py:28
  2.9 2.5 %fusion.57 = (bf16[96,2048]{1,0:T(8,128)(2,1)}, bf16[96,2048]{1,0:T(8,128)(2,1)}, bf16[96,2048]{1,0:T(8,128)(2,1)}, bf16[96,2048]{1,0:T(8,128)(2,1)}) fusion(bf16[384,2048]{1,0:T(8,128)(2,1)} %a_ref.1), kind=kLoop, calls=%fused_computation.71 | loop fusion | bytes 3145728 | tf_op jit(solution)/shard_map/slice | solution.py:262
  5.5 3.5 %collective-permute-start = (bf16[96,2048]{1,0:T(8,128)(2,1)}, bf16[96,2048]{1,0:T(8,128)(2,1)S(1)}, u32[]{:S(2)}, u32[]{:S(2)}) collective-permute-start(bf16[96,2048]{1,0:T(8,128)(2,1)} %get-tuple-element.16), channel_id=1, source_target_pairs={{0,4},{12,8},{1,5},{13,9},{2,6},{14,10},{3,7},{15,11},{16,20},{28,... | collective-permute-start | bytes 1179656 | tf_op jit(solution)/shard_map/ppermute | solution.py:32
  9.0 2.1 %collective-permute-start.2 = (bf16[96,2048]{1,0:T(8,128)(2,1)}, bf16[96,2048]{1,0:T(8,128)(2,1)}, u32[]{:S(2)}, u32[]{:S(2)}) collective-permute-start(bf16[96,2048]{1,0:T(8,128)(2,1)} %get-tuple-element.15), channel_id=1, source_target_pairs={{0,4},{12,8},{1,5},{13,9},{2,6},{14,10},{3,7},{15,11},{16,20},{28,... | collective-permute-start | bytes 1179656 | tf_op jit(solution)/shard_map/ppermute | solution.py:32
  13.3 2.2 %collective-permute-start.17 = (bf16[384,1024]{1,0:T(8,128)(2,1)S(1)}, bf16[384,1024]{1,0:T(8,128)(2,1)}, u32[]{:S(2)}, u32[]{:S(2)}) collective-permute-start(bf16[384,1024]{1,0:T(8,128)(2,1)S(1)} %pad_maximum_fusion), channel_id=1, source_target_pairs={{0,4},{12,8},{1,5},{13,9},{2,6},{14,10},{3,7},{15,11},{16,20},{28,... | collective-permute-start | bytes 2359304 | tf_op jit(solution)/shard_map/ppermute | solution.py:32
  15.8 10.6 %collective-permute-done.6 = bf16[2,128,2048]{2,1,0:T(8,128)(2,1)} collective-permute-done((bf16[2,128,2048]{2,1,0:T(8,128)(2,1)}, bf16[2,128,2048]{2,1,0:T(8,128)(2,1)}, u32[]{:S(2)}, u32[]{:S(2)}) %collective-permute-start.6) | collective-permute-done | bytes 1048608 | tf_op jit(solution)/shard_map/ppermute | solution.py:28
  28.4 15.1 %collective-permute-done.17.refs_4_.refs_2_ = bf16[384,1024]{1,0:T(8,128)(2,1)} collective-permute-done((bf16[384,1024]{1,0:T(8,128)(2,1)S(1)}, bf16[384,1024]{1,0:T(8,128)(2,1)}, u32[]{:S(2)}, u32[]{:S(2)}) %collective-permute-start.17) | collective-permute-done | bytes 786464 | tf_op jit(solution)/shard_map/ppermute | solution.py:32
  44.2 7.2 %collective-permute-start.4 = (bf16[96,2048]{1,0:T(8,128)(2,1)S(1)}, bf16[96,2048]{1,0:T(8,128)(2,1)S(1)}, u32[]{:S(2)}, u32[]{:S(2)}) collective-permute-start(bf16[96,2048]{1,0:T(8,128)(2,1)S(1)} %copy-done.14), channel_id=1, source_target_pairs={{0,4},{12,8},{1,5},{13,9},{2,6},{14,10},{3,7},{15,11},{16,20},{28,... | collective-permute-start | bytes 1179656 | tf_op jit(solution)/shard_map/ppermute | solution.py:32
  51.5 2.0 %fusion.25 = f32[384,128]{1,0:T(8,128)S(1)} fusion(bf16[2,128,2048]{2,1,0:T(8,128)(2,1)} %collective-permute-done.6, bf16[384,2048]{1,0:T(8,128)(2,1)S(1)} %copy-done.2, pred[384,2]{0,1:T(4,128)(4,1)S(1)} %get-tuple-element.21, pred[384,128]{1,0:T(8,128)(4,1)S(1)} %iota_compare_fusion), kind=kOutput, calls=%fused_computation.20 | convolution fusion | flops 402898944 | bytes 2867968 | tf_op jit(solution)/shard_map/dot_general | solution.py:48
  54.9 1.9 %fusion.28 = f32[384,128]{1,0:T(8,128)S(1)} fusion(bf16[2,128,2048]{2,1,0:T(8,128)(2,1)} %collective-permute-done.5, bf16[384,2048]{1,0:T(8,128)(2,1)S(1)} %copy-done.2, pred[384,2]{0,1:T(4,128)(4,1)S(1)} %get-tuple-element.22, pred[384,128]{1,0:T(8,128)(4,1)S(1)} %iota_compare_fusion), kind=kOutput, calls=%fused_computation.21 | convolution fusion | flops 402898944 | bytes 2867968 | tf_op jit(solution)/shard_map/dot_general | solution.py:48
  56.8 2.6 %collective-permute-done.4.refs_2_ = bf16[96,2048]{1,0:T(8,128)(2,1)S(1)} collective-permute-done((bf16[96,2048]{1,0:T(8,128)(2,1)S(1)}, bf16[96,2048]{1,0:T(8,128)(2,1)S(1)}, u32[]{:S(2)}, u32[]{:S(2)}) %collective-permute-start.4) | collective-permute-done | bytes 393248 | tf_op jit(solution)/shard_map/ppermute | solution.py:32
  62.8 2.5 %collective-permute-start.8 = (bf16[384,128]{1,0:T(8,128)(2,1)}, bf16[384,128]{1,0:T(8,128)(2,1)}, u32[]{:S(2)}, u32[]{:S(2)}) collective-permute-start(bf16[384,128]{1,0:T(8,128)(2,1)} %add_convert_fusion.2), channel_id=1, source_target_pairs={{0,4},{4,0},{8,12},{12,8},{1,5},{5,1},{9,13},{13,9},{2,6},{6,2},{1... | collective-permute-start | bytes 294920 | tf_op jit(solution)/shard_map/ppermute | solution.py:32
  65.3 9.0 %collective-permute-done.18 = bf16[2,128,1024]{2,1,0:T(8,128)(2,1)S(1)} collective-permute-done((bf16[2,128,1024]{2,1,0:T(8,128)(2,1)S(1)}, bf16[2,128,1024]{2,1,0:T(8,128)(2,1)S(1)}, u32[]{:S(2)}, u32[]{:S(2)}) %collective-permute-start.18) | collective-permute-done | bytes 524320 | tf_op jit(solution)/shard_map/ppermute | solution.py:28
  75.1 18.0 %collective-permute-done.8 = bf16[384,128]{1,0:T(8,128)(2,1)} collective-permute-done((bf16[384,128]{1,0:T(8,128)(2,1)}, bf16[384,128]{1,0:T(8,128)(2,1)}, u32[]{:S(2)}, u32[]{:S(2)}) %collective-permute-start.8) | collective-permute-done | bytes 98336 | tf_op jit(solution)/shard_map/ppermute | solution.py:32
  96.3 5.8 %copy-done = bf16[8192,1024]{1,0:T(8,128)(2,1)S(1)} copy-done((bf16[8192,1024]{1,0:T(8,128)(2,1)S(1)}, bf16[8192,1024]{1,0:T(8,128)(2,1)}, u32[]{:S(2)}) %copy-start) | copy-done | bytes 16777240
  102.1 2.6 %shard_map.73.refs_8_ = f32[384,1024]{1,0:T(8,128)S(1)} custom-call(s32[1]{0:T(128)} %bitcast.5.index_ref, bf16[384,2048]{1,0:T(8,128)(2,1)S(1)} %copy-done.2, bf16[8192,1024]{1,0:T(8,128)(2,1)S(1)} %copy-done), custom_call_target="tpu_custom_call" | custom-call | flops 1610612736 | bytes 7340032 | tf_op jit(solution)/shard_map/pallas_call | solution.py:85
  108.4 5.5 %collective-permute-done.24.refs_8_.refs_6_ = bf16[384,1024]{1,0:T(8,128)(2,1)} collective-permute-done((bf16[384,1024]{1,0:T(8,128)(2,1)}, bf16[384,1024]{1,0:T(8,128)(2,1)}, u32[]{:S(2)}, u32[]{:S(2)}) %collective-permute-start.24) | collective-permute-done | bytes 786464 | tf_op jit(solution)/shard_map/ppermute | solution.py:28
  115.8 12.0 %collective-permute-done.26.refs_10_.refs_8_ = bf16[384,1024]{1,0:T(8,128)(2,1)S(1)} collective-permute-done((bf16[384,1024]{1,0:T(8,128)(2,1)}, bf16[384,1024]{1,0:T(8,128)(2,1)S(1)}, u32[]{:S(2)}, u32[]{:S(2)}) %collective-permute-start.26) | collective-permute-done | bytes 786464 | tf_op jit(solution)/shard_map/ppermute | solution.py:28
  132.1 8.9 %shard_map.74 = f32[384,1024]{1,0:T(8,128)S(1)} custom-call(s32[3]{0:T(128)S(1)} %pad_add_fusion.s_ref, bf16[96,2048]{1,0:T(8,128)(2,1)S(1)} %collective-permute-done.refs_0_, bf16[96,2048]{1,0:T(8,128)(2,1)} %collective-permute-done.2.refs_1_, bf16[96,2048]{1,0:T(8,128)(2,1)S(1)} %copy-done.4, bf16[96,2048]{1,0:T(8,128)(2,1)S(1)} %collective-permute-done.10.refs_3_, ...), custom_call_target="tpu_custom_call" | custom-call | flops 3221225472 | bytes 13107200 | tf_op jit(solution)/shard_map/pallas_call | solution.py:146
  141.0 3.7 %shard_map.78 = bf16[96,1024]{1,0:T(8,128)(2,1)S(1)} custom-call(s32[8]{0:T(128)S(1)} %stack.64.place_ref, bf16[96,2048]{1,0:T(8,128)(2,1)S(1)} %collective-permute-done.20.refs_0_, bf16[384,2048]{1,0:T(8,128)(2,1)S(1)} %collective-permute-done.12.refs_5_.refs_3_.refs_1_, bf16[384,1024]{1,0:T(8,128)(2,1)} %collective-permute-done.17.refs_4_.refs_2_, ...), custom_call_target="tpu_custom_call" | custom-call | flops 603979776 | bytes 7274496 | tf_op jit(solution)/shard_map/pallas_call | solution.py:229
  146.0 5.0 %shard_map.77 = bf16[288,1024]{1,0:T(8,128)(2,1)S(1)} custom-call(s32[8]{0:T(128)S(1)} %stack.64.place_ref, bf16[96,2048]{1,0:T(8,128)(2,1)S(1)} %collective-permute-done.1.refs_0_, bf16[96,2048]{1,0:T(8,128)(2,1)S(1)} %collective-permute-done.3.refs_1_, bf16[96,2048]{1,0:T(8,128)(2,1)S(1)} %collective-permute-done.9.refs_2_, ...), custom_call_target="tpu_custom_call" | custom-call | flops 1811939328 | bytes 9240576 | tf_op jit(solution)/shard_map/pallas_call | solution.py:229
  152.8 5.8 %copy-done.1 = bf16[8192,1024]{1,0:T(8,128)(2,1)S(1)} copy-done((bf16[8192,1024]{1,0:T(8,128)(2,1)S(1)}, bf16[8192,1024]{1,0:T(8,128)(2,1)}, u32[]{:S(2)}) %copy-start.1) | copy-done | bytes 16777240
  158.5 2.1 %shard_map.75 = f32[288,1024]{1,0:T(8,128)S(1)} custom-call(s32[1]{0:T(128)} %bitcast.index_ref, bf16[96,2048]{1,0:T(8,128)(2,1)S(1)} %collective-permute-done.1.refs_0_, bf16[96,2048]{1,0:T(8,128)(2,1)S(1)} %collective-permute-done.3.refs_1_, bf16[96,2048]{1,0:T(8,128)(2,1)S(1)} %collective-permute-done.9.refs_2_, bf16[8192,1024]{1,0:T(8,128)(2,1)S(1)} %copy-done.1, ...), custom_call_target="tpu_custom_call" | custom-call | flops 1207959552 | bytes 6553600 | tf_op jit(solution)/shard_map/pallas_call | solution.py:183
  162.1 23.5 %collective-permute-done.28 = bf16[288,1024]{1,0:T(8,128)(2,1)S(1)} collective-permute-done((bf16[288,1024]{1,0:T(8,128)(2,1)S(1)}, bf16[288,1024]{1,0:T(8,128)(2,1)S(1)}, u32[]{:S(2)}, u32[]{:S(2)}) %collective-permute-start.28) | collective-permute-done | bytes 589856 | tf_op jit(solution)/shard_map/ppermute | solution.py:32
  (109 shorter events, 29.1 us)
Async XLA Ops:
  0.0 26.4 %collective-permute-start.6 = (bf16[2,128,2048]{2,1,0:T(8,128)(2,1)}, bf16[2,128,2048]{2,1,0:T(8,128)(2,1)}, u32[]{:S(2)}, u32[]{:S(2)}) collective-permute-start(bf16[2,128,2048]{2,1,0:T(8,128)(2,1)} %param.12), channel_id=1, source_target_pairs={{0,2},{2,0},{1,3},{3,1},{4,6},{6,4},{5,7},{7,5},{8,10},{10,8},{9,1... | collective-permute-start | bytes 3145736 | tf_op jit(solution)/shard_map/ppermute | solution.py:28
  2.9 51.8 %collective-permute-start.5 = (bf16[2,128,2048]{2,1,0:T(8,128)(2,1)}, bf16[2,128,2048]{2,1,0:T(8,128)(2,1)}, u32[]{:S(2)}, u32[]{:S(2)}) collective-permute-start(bf16[2,128,2048]{2,1,0:T(8,128)(2,1)} %param.12), channel_id=1, source_target_pairs={{0,1},{1,0},{2,3},{3,2},{4,5},{5,4},{6,7},{7,6},{8,9},{9,8},{10,11... | collective-permute-start | bytes 3145736 | tf_op jit(solution)/shard_map/ppermute | solution.py:28
  5.5 38.8 %collective-permute-start = (bf16[96,2048]{1,0:T(8,128)(2,1)}, bf16[96,2048]{1,0:T(8,128)(2,1)S(1)}, u32[]{:S(2)}, u32[]{:S(2)}) collective-permute-start(bf16[96,2048]{1,0:T(8,128)(2,1)} %get-tuple-element.16), channel_id=1, source_target_pairs={{0,4},{12,8},{1,5},{13,9},{2,6},{14,10},{3,7},{15,11},{16,20},{28,... | collective-permute-start | bytes 1179656 | tf_op jit(solution)/shard_map/ppermute | solution.py:32
  9.0 44.5 %collective-permute-start.2 = (bf16[96,2048]{1,0:T(8,128)(2,1)}, bf16[96,2048]{1,0:T(8,128)(2,1)}, u32[]{:S(2)}, u32[]{:S(2)}) collective-permute-start(bf16[96,2048]{1,0:T(8,128)(2,1)} %get-tuple-element.15), channel_id=1, source_target_pairs={{0,4},{12,8},{1,5},{13,9},{2,6},{14,10},{3,7},{15,11},{16,20},{28,... | collective-permute-start | bytes 1179656 | tf_op jit(solution)/shard_map/ppermute | solution.py:32
  13.3 30.2 %collective-permute-start.17 = (bf16[384,1024]{1,0:T(8,128)(2,1)S(1)}, bf16[384,1024]{1,0:T(8,128)(2,1)}, u32[]{:S(2)}, u32[]{:S(2)}) collective-permute-start(bf16[384,1024]{1,0:T(8,128)(2,1)S(1)} %pad_maximum_fusion), channel_id=1, source_target_pairs={{0,4},{12,8},{1,5},{13,9},{2,6},{14,10},{3,7},{15,11},{16,20},{28,... | collective-permute-start | bytes 2359304 | tf_op jit(solution)/shard_map/ppermute | solution.py:32
  26.4 33.6 %collective-permute-start.7 = (bf16[2,128,2048]{2,1,0:T(8,128)(2,1)}, bf16[2,128,2048]{2,1,0:T(8,128)(2,1)S(1)}, u32[]{:S(2)}, u32[]{:S(2)}) collective-permute-start(bf16[2,128,2048]{2,1,0:T(8,128)(2,1)} %collective-permute-done.6), channel_id=1, source_target_pairs={{0,1},{1,0},{2,3},{3,2},{4,5},{5,4},{6,7},{7,6},{8,9},{9,8},{10,11... | collective-permute-start | bytes 3145736 | tf_op jit(solution)/shard_map/ppermute | solution.py:28
  43.5 61.9 %collective-permute-start.12 = (bf16[384,2048]{1,0:T(8,128)(2,1)S(1)}, bf16[384,2048]{1,0:T(8,128)(2,1)S(1)}, u32[]{:S(2)}, u32[]{:S(2)}) collective-permute-start(bf16[384,2048]{1,0:T(8,128)(2,1)S(1)} %copy-done.2), channel_id=1, source_target_pairs={{4,8},{8,4},{5,9},{9,5},{6,10},{10,6},{7,11},{11,7},{20,24},{24,20... | collective-permute-start | bytes 4718600 | tf_op jit(solution)/shard_map/ppermute | solution.py:32
  44.2 15.2 %collective-permute-start.4 = (bf16[96,2048]{1,0:T(8,128)(2,1)S(1)}, bf16[96,2048]{1,0:T(8,128)(2,1)S(1)}, u32[]{:S(2)}, u32[]{:S(2)}) collective-permute-start(bf16[96,2048]{1,0:T(8,128)(2,1)S(1)} %copy-done.14), channel_id=1, source_target_pairs={{0,4},{12,8},{1,5},{13,9},{2,6},{14,10},{3,7},{15,11},{16,20},{28,... | collective-permute-start | bytes 1179656 | tf_op jit(solution)/shard_map/ppermute | solution.py:32
  53.5 53.3 %collective-permute-start.11 = (bf16[384,2048]{1,0:T(8,128)(2,1)S(1)}, bf16[384,2048]{1,0:T(8,128)(2,1)}, u32[]{:S(2)}, u32[]{:S(2)}) collective-permute-start(bf16[384,2048]{1,0:T(8,128)(2,1)S(1)} %copy-done.2), channel_id=1, source_target_pairs={{4,0},{8,12},{5,1},{9,13},{6,2},{10,14},{7,3},{11,15},{20,16},{24,... | collective-permute-start | bytes 4718600 | tf_op jit(solution)/shard_map/ppermute | solution.py:32
  59.4 14.9 %collective-permute-start.18 = (bf16[2,128,1024]{2,1,0:T(8,128)(2,1)S(1)}, bf16[2,128,1024]{2,1,0:T(8,128)(2,1)S(1)}, u32[]{:S(2)}, u32[]{:S(2)}) collective-permute-start(bf16[2,128,1024]{2,1,0:T(8,128)(2,1)S(1)} %copy-done.7), channel_id=1, source_target_pairs={{0,2},{2,0},{1,3},{3,1},{4,6},{6,4},{5,7},{7,5},{8,10},{10,8},{9,1... | collective-permute-start | bytes 1572872 | tf_op jit(solution)/shard_map/ppermute | solution.py:28
  60.0 35.7 %collective-permute-start.22 = (bf16[384,1024]{1,0:T(8,128)(2,1)}, bf16[384,1024]{1,0:T(8,128)(2,1)}, u32[]{:S(2)}, u32[]{:S(2)}) collective-permute-start(bf16[384,1024]{1,0:T(8,128)(2,1)} %collective-permute-done.17.refs_4_.refs_2_), channel_id=1, source_target_pairs={{0,2},{2,0},{1,3},{3,1},{4,6},{6,4},{5,7},{7,5},{8,10},{10,8},{9,1... | collective-permute-start | bytes 2359304 | tf_op jit(solution)/shard_map/ppermute | solution.py:28
  62.8 30.3 %collective-permute-start.8 = (bf16[384,128]{1,0:T(8,128)(2,1)}, bf16[384,128]{1,0:T(8,128)(2,1)}, u32[]{:S(2)}, u32[]{:S(2)}) collective-permute-start(bf16[384,128]{1,0:T(8,128)(2,1)} %add_convert_fusion.2), channel_id=1, source_target_pairs={{0,4},{4,0},{8,12},{12,8},{1,5},{5,1},{9,13},{13,9},{2,6},{6,2},{1... | collective-permute-start | bytes 294920 | tf_op jit(solution)/shard_map/ppermute | solution.py:32
  75.1 33.2 %collective-permute-start.21 = (bf16[384,1024]{1,0:T(8,128)(2,1)}, bf16[384,1024]{1,0:T(8,128)(2,1)}, u32[]{:S(2)}, u32[]{:S(2)}) collective-permute-start(bf16[384,1024]{1,0:T(8,128)(2,1)} %collective-permute-done.17.refs_4_.refs_2_), channel_id=1, source_target_pairs={{0,1},{1,0},{2,3},{3,2},{4,5},{5,4},{6,7},{7,6},{8,9},{9,8},{10,11... | collective-permute-start | bytes 2359304 | tf_op jit(solution)/shard_map/ppermute | solution.py:28
  93.1 20.8 %collective-permute-start.24 = (bf16[384,1024]{1,0:T(8,128)(2,1)}, bf16[384,1024]{1,0:T(8,128)(2,1)}, u32[]{:S(2)}, u32[]{:S(2)}) collective-permute-start(bf16[384,1024]{1,0:T(8,128)(2,1)} %collective-permute-done.17.refs_4_.refs_2_), channel_id=1, source_target_pairs={{0,16},{16,0},{1,17},{17,1},{2,18},{18,2},{3,19},{19,3},{4,20},{20... | collective-permute-start | bytes 2359304 | tf_op jit(solution)/shard_map/ppermute | solution.py:28
  104.7 23.1 %collective-permute-start.26 = (bf16[384,1024]{1,0:T(8,128)(2,1)}, bf16[384,1024]{1,0:T(8,128)(2,1)S(1)}, u32[]{:S(2)}, u32[]{:S(2)}) collective-permute-start(bf16[384,1024]{1,0:T(8,128)(2,1)} %collective-permute-done.22.refs_6_.refs_4_), channel_id=1, source_target_pairs={{0,16},{16,0},{1,17},{17,1},{2,18},{18,2},{3,19},{19,3},{4,20},{20... | collective-permute-start | bytes 2359304 | tf_op jit(solution)/shard_map/ppermute | solution.py:28
  106.8 22.1 %collective-permute-start.13 = (bf16[384,1024]{1,0:T(8,128)(2,1)S(1)}, bf16[384,1024]{1,0:T(8,128)(2,1)S(1)}, u32[]{:S(2)}, u32[]{:S(2)}) collective-permute-start(bf16[384,1024]{1,0:T(8,128)(2,1)S(1)} %slice.20), channel_id=1, source_target_pairs={{4,0},{8,12},{5,1},{9,13},{6,2},{10,14},{7,3},{11,15},{20,16},{24,... | collective-permute-start | bytes 2359304 | tf_op jit(solution)/shard_map/ppermute | solution.py:32
  108.3 21.4 %collective-permute-start.23 = (bf16[384,1024]{1,0:T(8,128)(2,1)}, bf16[384,1024]{1,0:T(8,128)(2,1)S(1)}, u32[]{:S(2)}, u32[]{:S(2)}) collective-permute-start(bf16[384,1024]{1,0:T(8,128)(2,1)} %collective-permute-done.22.refs_6_.refs_4_), channel_id=1, source_target_pairs={{0,1},{1,0},{2,3},{3,2},{4,5},{5,4},{6,7},{7,6},{8,9},{9,8},{10,11... | collective-permute-start | bytes 2359304 | tf_op jit(solution)/shard_map/ppermute | solution.py:28
  113.9 16.5 %collective-permute-start.25 = (bf16[384,1024]{1,0:T(8,128)(2,1)}, bf16[384,1024]{1,0:T(8,128)(2,1)S(1)}, u32[]{:S(2)}, u32[]{:S(2)}) collective-permute-start(bf16[384,1024]{1,0:T(8,128)(2,1)} %collective-permute-done.24.refs_8_.refs_6_), channel_id=1, source_target_pairs={{0,1},{1,0},{2,3},{3,2},{4,5},{5,4},{6,7},{7,6},{8,9},{9,8},{10,11... | collective-permute-start | bytes 2359304 | tf_op jit(solution)/shard_map/ppermute | solution.py:28
  128.9 17.0 %collective-permute-start.1 = (bf16[96,2048]{1,0:T(8,128)(2,1)S(1)}, bf16[96,2048]{1,0:T(8,128)(2,1)S(1)}, u32[]{:S(2)}, u32[]{:S(2)}) collective-permute-start(bf16[96,2048]{1,0:T(8,128)(2,1)S(1)} %collective-permute-done.refs_0_), channel_id=1, source_target_pairs={{4,8},{8,4},{5,9},{9,5},{6,10},{10,6},{7,11},{11,7},{20,24},{24,20... | collective-permute-start | bytes 1179656 | tf_op jit(solution)/shard_map/ppermute | solution.py:32
  129.7 16.3 %collective-permute-start.3 = (bf16[96,2048]{1,0:T(8,128)(2,1)}, bf16[96,2048]{1,0:T(8,128)(2,1)S(1)}, u32[]{:S(2)}, u32[]{:S(2)}) collective-permute-start(bf16[96,2048]{1,0:T(8,128)(2,1)} %collective-permute-done.2.refs_1_), channel_id=1, source_target_pairs={{4,8},{8,4},{5,9},{9,5},{6,10},{10,6},{7,11},{11,7},{20,24},{24,20... | collective-permute-start | bytes 1179656 | tf_op jit(solution)/shard_map/ppermute | solution.py:32
  130.4 15.6 %collective-permute-start.9 = (bf16[96,2048]{1,0:T(8,128)(2,1)S(1)}, bf16[96,2048]{1,0:T(8,128)(2,1)S(1)}, u32[]{:S(2)}, u32[]{:S(2)}) collective-permute-start(bf16[96,2048]{1,0:T(8,128)(2,1)S(1)} %copy-done.4), channel_id=1, source_target_pairs={{4,8},{8,4},{5,9},{9,5},{6,10},{10,6},{7,11},{11,7},{20,24},{24,20... | collective-permute-start | bytes 1179656 | tf_op jit(solution)/shard_map/ppermute | solution.py:32
  131.5 20.8 %collective-permute-start.19 = (bf16[2,128,1024]{2,1,0:T(8,128)(2,1)S(1)}, bf16[2,128,1024]{2,1,0:T(8,128)(2,1)S(1)}, u32[]{:S(2)}, u32[]{:S(2)}) collective-permute-start(bf16[2,128,1024]{2,1,0:T(8,128)(2,1)S(1)} %copy-done.10), channel_id=1, source_target_pairs={{0,1},{1,0},{2,3},{3,2},{4,5},{5,4},{6,7},{7,6},{8,9},{9,8},{10,11... | collective-permute-start | bytes 1572872 | tf_op jit(solution)/shard_map/ppermute | solution.py:28
  144.6 17.4 %collective-permute-start.29 = (bf16[96,1024]{1,0:T(8,128)(2,1)S(1)}, bf16[96,1024]{1,0:T(8,128)(2,1)S(1)}, u32[]{:S(2)}, u32[]{:S(2)}) collective-permute-start(bf16[96,1024]{1,0:T(8,128)(2,1)S(1)} %shard_map.78), channel_id=1, source_target_pairs={{4,0},{8,12},{5,1},{9,13},{6,2},{10,14},{7,3},{11,15},{20,16},{24,... | collective-permute-start | bytes 589832 | tf_op jit(solution)/shard_map/ppermute | solution.py:32
  151.0 34.6 %collective-permute-start.28 = (bf16[288,1024]{1,0:T(8,128)(2,1)S(1)}, bf16[288,1024]{1,0:T(8,128)(2,1)S(1)}, u32[]{:S(2)}, u32[]{:S(2)}) collective-permute-start(bf16[288,1024]{1,0:T(8,128)(2,1)S(1)} %shard_map.77), channel_id=1, source_target_pairs={{4,0},{8,12},{5,1},{9,13},{6,2},{10,14},{7,3},{11,15},{20,16},{24,... | collective-permute-start | bytes 1769480 | tf_op jit(solution)/shard_map/ppermute | solution.py:32
  (26 other events, 295.1 us)

commit v2 on v0

v2 whole, which is shorter than its diff:
```python
import jax
import jax.numpy as jnp
from jax import lax
from jax.experimental import pallas as pl
from jax.experimental.pallas import tpu as pltpu
from jax.sharding import PartitionSpec as P

MAXIMUM_RANK = 128
RBLK = 16
AXES = ("groups", "tensor", "pool", "inner")

PAIRS = [(0, 1), (1, 0), (2, 3), (3, 2)]
MIDDLE = [(1, 2), (2, 1)]
OUTWARD = [(1, 0), (2, 3)]
INWARD = [(0, 1), (3, 2)]


def lookup(indices, table):
    count = table.shape[0]
    match = indices[..., None] == jnp.arange(count, dtype=jnp.int32)
    return jnp.sum(jnp.where(match, table, 0), axis=-1)


def slot_and_rank(ids, slots, blocks):
    return lookup(ids, slots), RBLK * lookup(ids, blocks)


def swap(x, axis):
    return lax.ppermute(x, axis, [(0, 1), (1, 0)])


def hop(x, pairs):
    return lax.ppermute(x, "tensor", pairs)


VMEM = pl.BlockSpec(memory_space=pltpu.VMEM)
ANY = pl.BlockSpec(memory_space=pl.ANY)
HBM = pl.BlockSpec(memory_space=pltpu.HBM)


def call(held, body, out_shapes, operands, in_specs, out_specs=None, scratch=(), room=16):
    single = not isinstance(out_shapes, list)
    shapes = [out_shapes] if single else out_shapes
    out_specs = out_specs or [VMEM] * len(shapes)
    ins, outs = len(operands), len(shapes)
    tick = held["tick"]

    def counted(*refs):
        into = refs[ins + 1 + outs]
        into[...] = refs[ins][...] + 1.0
        body(*refs[:ins], *refs[ins + 1 : ins + 1 + outs], *refs[ins + 2 + outs :])

    *results, held["tick"] = pl.pallas_call(
        counted,
        out_shape=[*shapes, jax.ShapeDtypeStruct(tick.shape, tick.dtype)],
        in_specs=[*in_specs, VMEM],
        out_specs=[*out_specs, VMEM],
        scratch_shapes=list(scratch),
        cost_estimate=pl.CostEstimate(flops=10**12, bytes_accessed=0, transcendentals=0),
        compiler_params=pltpu.CompilerParams(vmem_limit_bytes=room << 20),
    )(*operands, tick)
    return results[0] if single else results


def fence(held):
    call(held, lambda: None, [], [], [])
    names = sorted(held)
    held.update(zip(names, lax.optimization_barrier(tuple(held[n] for n in names))))


def array(*shape, dtype=jnp.bfloat16):
    return jax.ShapeDtypeStruct(shape, dtype)


def dot(a, b):
    return jnp.dot(a, b, preferred_element_type=jnp.float32)


class Place:
    def __init__(self):
        z = lax.axis_index("tensor")
        self.own, self.partner = z, z ^ 1
        self.end = jnp.logical_or(z == 0, z == 3)
        self.near = jnp.where(self.end, 3 - self.partner, 3 - z)
        self.far = jnp.where(self.end, 3 - z, 3 - self.partner)
        self.seat = lax.axis_index(("groups", "pool", "inner"))
        self.mine = lax.axis_index(("pool", "inner"))


class Layout:
    def __init__(self, tokens, weight):
        self.tall, self.width = tokens.shape
        self.columns = weight.shape[1]
        self.deep, self.shallow = self.width // 8, self.width // 32
        self.lent = 8 * self.shallow
        self.rows = (self.deep + self.shallow) // 2
        self.spans = [
            (0, 0, 0, self.rows),
            (self.rows, 0, 1, self.deep - self.rows),
            (0, self.deep - self.rows, 1, self.shallow),
        ]
        self.cut = self.tall * 7 // 12
        self.sizes = [self.cut, self.tall - self.cut]

    def parts(self, ref):
        for first, at, side, size in self.spans:
            columns = pl.ds(side * self.columns, self.columns)
            yield first, size, ref.at[pl.ds(at, size), columns]


def run_copies(copies):
    for copy in copies:
        copy.start()
    for copy in copies:
        copy.wait()


def first_rows(held, tokens, weight, layout):
    width, rows = layout.width, layout.rows

    def body(t_ref, w_ref, out_ref, sem):
        place = Place()

        @pl.when(place.end)
        def _():
            far = place.far * width + place.seat * layout.deep
            near = (place.near + 1) * width - (8 - place.seat) * layout.shallow
            lend = []
            for i, (first, size, into) in enumerate(layout.parts(out_ref)):
                at = pl.multiple_of((far if i < 2 else near) + first, 32)
                lend.append(
                    pltpu.make_async_copy(w_ref.at[pl.ds(at, size)], into, sem.at[i])
                )
            run_copies(lend)

        @pl.when(jnp.logical_not(place.end))
        def _():
            run_copies(
                [pltpu.make_async_copy(t_ref.at[pl.ds(0, rows)], out_ref, sem.at[0])]
            )

    return call(
        held,
        body,
        array(rows, width),
        [tokens, weight],
        [HBM, HBM],
        scratch=[pltpu.SemaphoreType.DMA((3,))],
    )


def cut_up(held, tokens, layout):
    tall, width, rows, cut = layout.tall, layout.width, layout.rows, layout.cut
    cuts = [(rows, tall - rows), (0, cut), (cut, tall - cut)]

    def body(t_ref, *refs):
        *into_refs, all_ref, sem = refs
        run_copies([pltpu.make_async_copy(t_ref, all_ref, sem.at[0])])
        run_copies(
            [
                pltpu.make_async_copy(all_ref.at[pl.ds(at, size)], into, sem.at[i])
                for i, ((at, size), into) in enumerate(zip(cuts, into_refs))
            ]
        )

    return call(
        held,
        body,
        [array(size, width) for _, size in cuts],
        [tokens],
        [ANY],
        [ANY] * len(cuts),
        [pltpu.VMEM((tall, width), tokens.dtype), pltpu.SemaphoreType.DMA((3,))],
    )


def left_columns(held, x, layout):
    keep = layout.width - layout.lent

    def body(x_ref, out_ref, sem):
        run_copies([pltpu.make_async_copy(x_ref.at[:, pl.ds(0, keep)], out_ref, sem)])

    shape = array(x.shape[0], keep)
    return call(held, body, shape, [x], [ANY], [VMEM], [pltpu.SemaphoreType.DMA])


class Rows:
    def __init__(self, x_ref, start, depth):
        self.x_ref, self.start, self.depth = x_ref, start, depth

    def dot(self, a_ref, limit=None):
        some = pl.ds(pl.multiple_of(self.start, 128), limit or self.depth)
        return dot(a_ref[...] if limit is None else a_ref[:, :limit], self.x_ref[some, :])


def started(*copies):
    for copy in copies:
        copy.start()
    return copies


def waited(copies):
    for copy in copies:
        copy.wait()


def sums(layout):
    return array(layout.tall, layout.columns, dtype=jnp.float32)


def sums_room(layout):
    return [
        pltpu.VMEM((layout.tall, layout.columns), jnp.float32),
        pltpu.SemaphoreType.DMA((8,)),
    ]


def own_block(held, tokens, weight, layout):
    def body(a_ref, w_ref, out_ref, a_held, sum_ref, sem):
        load = started(pltpu.make_async_copy(a_ref, a_held, sem.at[0]))
        w = Rows(w_ref, Place().own * layout.width, layout.width)
        waited(load)
        sum_ref[...] = w.dot(a_held)
        run_copies([pltpu.make_async_copy(sum_ref, out_ref, sem.at[1])])

    return call(
        held,
        body,
        sums(layout),
        [tokens, weight],
        [ANY, VMEM],
        [HBM],
        [pltpu.VMEM((layout.tall, layout.width), jnp.bfloat16)] + sums_room(layout),
    )


def add_partner(held, total, first, rest, inner, beyond, weight, layout):
    width, tall, cut, rows = layout.width, layout.tall, layout.cut, layout.rows

    def body(total_ref, first_ref, rest_ref, in0_ref, in1_ref, beyond_ref, w_ref, *refs):
        out_ref, p_held, f_held, sum_ref, sem = refs
        place = Place()

        def into(x_ref, at, size, i):
            return pltpu.make_async_copy(x_ref, p_held.at[pl.ds(at, size)], sem.at[i])

        at_end = [into(first_ref, 0, rows, 0), into(rest_ref, rows, tall - rows, 1)]
        inside = [
            into(in0_ref, 0, cut, 0),
            into(in1_ref, cut, tall - cut, 1),
            pltpu.make_async_copy(beyond_ref, f_held, sem.at[2]),
        ]

        @pl.when(place.end)
        def _():
            started(*at_end)

        @pl.when(jnp.logical_not(place.end))
        def _():
            started(*inside)

        more = started(pltpu.make_async_copy(total_ref, sum_ref, sem.at[3]))
        p = Rows(w_ref, place.partner * width, width)
        f = Rows(w_ref, place.far * width, width)

        @pl.when(place.end)
        def _():
            waited(at_end)
            waited(more)
            sum_ref[...] += p.dot(p_held)

        @pl.when(jnp.logical_not(place.end))
        def _():
            waited(inside)
            waited(more)
            sum_ref[...] += p.dot(p_held)
            sum_ref[:cut, :] += f.dot(f_held)

        run_copies([pltpu.make_async_copy(sum_ref, out_ref, sem.at[4])])

    return call(
        held,
        body,
        sums(layout),
        [total, first, rest, *inner, beyond, weight],
        [ANY] * 6 + [VMEM],
        [HBM],
        [pltpu.VMEM((size, width), jnp.bfloat16) for size in (tall, cut)]
        + sums_room(layout),
    )


def add_last(held, total, low, use, ups, relayed, across, beyond, term, weight, layout):
    adapters, rank, columns = ups[0].shape
    count = len(ups)
    cut, last = layout.sizes
    tall, width = layout.tall, layout.width
    keep = width - layout.lent

    def body(hop_ref, low_ref, use_ref, *refs):
        up_refs = refs[:count]
        total_ref, relayed_ref, across_ref, b_ref, term_ref, w_ref = refs[count : count + 6]
        out_ref, late_ref, n_held, b_held, t_held, first_ref, sum_ref, sem = refs[count + 6 :]
        place = Place()
        at_end = [pltpu.make_async_copy(relayed_ref, n_held.at[:, pl.ds(0, keep)], sem.at[0])]
        inside = [
            pltpu.make_async_copy(across_ref, n_held, sem.at[0]),
            pltpu.make_async_copy(b_ref, b_held, sem.at[1]),
        ]

        @pl.when(place.end)
        def _():
            started(*at_end)

        @pl.when(jnp.logical_not(place.end))
        def _():
            started(*inside)

        more = started(
            pltpu.make_async_copy(total_ref, sum_ref, sem.at[2]),
            pltpu.make_async_copy(term_ref, t_held, sem.at[3]),
        )
        n = Rows(w_ref, place.near * width, width)
        f = Rows(w_ref, place.far * width, width)
        low = jnp.where(place.end, hop_ref[...], low_ref[...])
        terms = 0.0
        for turn, up_ref in enumerate(up_refs):
            owner = place.mine ^ turn
            some = [
                jnp.where(use_ref[...] == owner * adapters + j, low, 0)
                for j in range(adapters)
            ]
            terms += dot(jnp.concatenate(some, axis=1), up_ref[...])
        waited(more)
        sum_ref[...] += terms.astype(jnp.bfloat16).astype(jnp.float32)
        sum_ref[:cut, :] += t_held[...].astype(jnp.float32)

        @pl.when(place.end)
        def _():
            waited(at_end)
            sum_ref[...] += n.dot(n_held, keep)

        @pl.when(jnp.logical_not(place.end))
        def _():
            waited(inside)
            sum_ref[...] += n.dot(n_held)
            sum_ref[cut:, :] += f.dot(b_held)

        first_ref[...] = sum_ref[:cut, :].astype(first_ref.dtype)
        run_copies(
            [
                pltpu.make_async_copy(first_ref, out_ref.at[pl.ds(0, cut)], sem.at[4]),
                pltpu.make_async_copy(sum_ref.at[pl.ds(cut, last)], late_ref, sem.at[5]),
            ]
        )

    return call(
        held,
        body,
        [array(tall, columns), array(last, columns, dtype=jnp.float32)],
        [*low, use, *[u.reshape(-1, columns) for u in ups]]
        + [total, relayed, across, beyond, term, weight],
        [VMEM] * (3 + count) + [ANY] * 5 + [VMEM],
        [ANY, ANY],
        [
            pltpu.VMEM((tall, width), jnp.bfloat16),
            pltpu.VMEM((last, width), jnp.bfloat16),
            pltpu.VMEM((cut, columns), jnp.bfloat16),
            pltpu.VMEM((cut, columns), jnp.bfloat16),
        ]
        + sums_room(layout),
    )


def helped(held, beyond, across, pieces, layout, i):
    half, width, columns = layout.sizes[i], layout.width, layout.columns
    start = i * layout.cut
    count = len(pieces)
    deep, shallow, lent = layout.deep, layout.shallow, layout.lent

    def body(beyond_ref, across_ref, *refs):
        piece_refs = refs[:count]
        out_ref, b_held, a_held, deep_ref, near_ref, sem = refs[count:]
        seat = Place().seat
        copies = started(
            pltpu.make_async_copy(beyond_ref, b_held, sem.at[0]),
            pltpu.make_async_copy(
                across_ref.at[pl.ds(start, half), pl.ds(width - lent, lent)],
                a_held,
                sem.at[1],
            ),
        )
        lends = []
        for k, piece_ref in enumerate(piece_refs):
            for j, (first, size, part) in enumerate(layout.parts(piece_ref)):
                if j < 2:
                    into = deep_ref.at[pl.ds(k * deep + first, size)]
                else:
                    at = pl.multiple_of((seat ^ k) * shallow, shallow)
                    into = near_ref.at[pl.ds(at, size)]
                lends.append(pltpu.make_async_copy(part, into, sem.at[2 + 3 * k + j]))
        started(*lends)
        waited(copies)
        total = 0.0
        step = count // 2
        for first in (0, step):
            turns = range(first, first + step)
            blocks = [
                b_held[:, pl.ds(pl.multiple_of((seat ^ k) * deep, deep), deep)] for k in turns
            ]
            waited(lends[3 * first : 3 * (first + step)])
            some = deep_ref[first * deep : (first + step) * deep, :]
            total += dot(jnp.concatenate(blocks, axis=1), some)
        total += dot(a_held[...], near_ref[...])
        out_ref[...] = total.astype(out_ref.dtype)

    return call(
        held,
        body,
        array(half, columns),
        [beyond, across, *pieces],
        [ANY] * (2 + count),
        scratch=[
            pltpu.VMEM((half, width), jnp.bfloat16),
            pltpu.VMEM((half, lent), jnp.bfloat16),
            pltpu.VMEM((deep * count, columns), jnp.bfloat16),
            pltpu.VMEM((lent, columns), jnp.bfloat16),
            pltpu.SemaphoreType.DMA((2 + 3 * count,)),
        ],
    )


def finished(held, out, late, term, layout):
    kept = [held[n] for n in sorted(held) if n != "tick"]
    cut, last = layout.sizes

    def body(out_ref, late_ref, term_ref, *refs):
        into_ref, sum_ref, sem = refs[len(kept) :]
        sum_ref[...] = (late_ref[...] + term_ref[...].astype(jnp.float32)).astype(
            sum_ref.dtype
        )
        run_copies([pltpu.make_async_copy(sum_ref, into_ref.at[pl.ds(cut, last)], sem)])

    return pl.pallas_call(
        body,
        out_shape=array(*out.shape),
        in_specs=[ANY, VMEM, VMEM] + [ANY] * len(kept),
        out_specs=ANY,
        scratch_shapes=[
            pltpu.VMEM((last, layout.columns), out.dtype),
            pltpu.SemaphoreType.DMA,
        ],
        input_output_aliases={0: 0},
        compiler_params=pltpu.CompilerParams(vmem_limit_bytes=16 << 20),
    )(out, late, term, *kept)


def coords_of(held, tokens, use, downs, turns, before=None):
    adapters, rank = downs[0].shape[0], downs[0].shape[1]
    count = len(downs)

    def body(use_ref, tokens_ref, *refs):
        out_ref, sent_ref = refs[-2:]
        mine = Place().mine
        total = refs[count][...] if before is not None else 0.0
        for turn, down_ref in zip(turns, refs[:count]):
            coords = lax.dot_general(
                tokens_ref[...],
                down_ref[...],
                (((1,), (1,)), ((), ())),
                preferred_element_type=jnp.float32,
            )
            for j in range(adapters):
                some = coords[:, j * rank : (j + 1) * rank]
                mask = use_ref[...] == (mine ^ turn) * adapters + j
                total = total + jnp.where(mask, some, 0.0)
        out_ref[...] = total
        sent_ref[...] = total.astype(sent_ref.dtype)

    flat = [d.reshape(-1, d.shape[2]) for d in downs]
    more = [] if before is None else [before]
    shape = (tokens.shape[0], rank)
    return call(
        held,
        body,
        [array(*shape, dtype=jnp.float32), array(*shape)],
        [use, tokens, *flat, *more],
        [VMEM] * (2 + count + len(more)),
    )


def added(held, a, b):
    def body(a_ref, b_ref, out_ref):
        sums = a_ref[...].astype(jnp.float32) + b_ref[...].astype(jnp.float32)
        out_ref[...] = sums.astype(out_ref.dtype)

    return call(held, body, array(*a.shape), [a, b], [VMEM] * 2)


def chained(tokens, tables, weight, down, up):
    layout = Layout(tokens, weight)
    across = hop(tokens, MIDDLE)
    h = dict(tick=jnp.zeros((8, 128), jnp.float32), down=down, up=up, tokens=tokens)
    h["ids"], h["slots"], h["blocks"] = tables
    fence(h)
    down_x, down_c = swap(h["down"], "pool"), swap(h["down"], "inner")
    h["first"] = first_rows(h, h["tokens"], weight, layout)
    fence(h)
    first_p = hop(h["first"], PAIRS)
    h["rest"], h["part0"], h["part1"] = cut_up(h, h["tokens"], layout)
    slot, rank = slot_and_rank(h.pop("ids"), h.pop("slots"), h.pop("blocks"))
    row = jnp.arange(MAXIMUM_RANK, dtype=jnp.int32)[None, :]
    h["use"] = jnp.where(row < rank[:, None], slot[:, None], -1)
    h["down_c"] = down_c
    fence(h)
    inner0 = hop(h["part0"], INWARD)
    fence(h)
    rest_o = hop(h["rest"], OUTWARD)
    total = own_block(h, h["tokens"], weight, layout)
    h["lent"] = first_p
    fence(h)
    lent_y = swap(h["lent"], "groups")
    h["down_x"] = down_x
    fence(h)
    lent_x = swap(h["lent"], "pool")
    downs = [h["down"], h["down_c"], h["down_x"]]
    coords, _ = coords_of(h, h["tokens"], h["use"], downs, [0, 1, 2])
    h["across"] = across
    fence(h)
    inner1 = hop(h["part1"], INWARD)
    h["left"] = left_columns(h, h["across"], layout)
    h["lent_y"], h["inner0"] = lent_y, inner0
    fence(h)
    beyond0 = hop(h["inner0"], MIDDLE)
    h["rest_o"], h["lent_x"] = rest_o, lent_x
    fence(h)
    lent_d = swap(h["lent_x"], "groups")
    fence(h)
    relayed = hop(h["left"], OUTWARD)
    fence(h)
    down_xc = swap(h["down_x"], "inner")
    h["down_xc"] = down_xc
    fence(h)
    lent_c = swap(h["lent"], "inner")
    coords, h["coords"] = coords_of(h, h["tokens"], h["use"], [h["down_xc"]], [3], coords)
    h["lent_c"] = lent_c
    fence(h)
    coords_p = hop(h["coords"], INWARD)
    h["inner1"] = inner1
    fence(h)
    lent_yc = swap(h["lent_y"], "inner")
    h["coords_p"], h["lent_yc"] = coords_p, lent_yc
    fence(h)
    h["pair"] = added(h, coords, h["coords_p"])
    fence(h)
    pair_m = hop(h["pair"], MIDDLE)
    h["beyond0"] = beyond0
    fence(h)
    beyond1 = hop(h["inner1"], MIDDLE)
    h["pair_m"], h["lent_d"] = pair_m, lent_d
    fence(h)
    lent_xc, lent_dc = swap(h["lent_x"], "inner"), swap(h["lent_d"], "inner")
    h["whole"] = added(h, h["pair"], h["pair_m"])
    h["lent_xc"], h["lent_dc"] = lent_xc, lent_dc
    fence(h)
    low_o = hop(h["whole"], OUTWARD)
    up_x = swap(h["up"], "pool")
    fence(h)
    names = ("lent", "lent_c", "lent_x", "lent_xc", "lent_y", "lent_yc", "lent_d", "lent_dc")
    pieces = [h[n] for n in names]
    h["help0"] = helped(h, h["beyond0"], h["across"], pieces, layout, 0)
    fence(h)
    help_o0 = hop(h["help0"], OUTWARD)
    fence(h)
    total = add_partner(
        h,
        total,
        h["lent"],
        h["rest_o"],
        [h["inner0"], h["inner1"]],
        h["beyond0"],
        weight,
        layout,
    )
    h["beyond1"] = beyond1
    h["relayed"], h["up_x"], h["low_o"] = relayed, up_x, low_o
    fence(h)
    up_xc, up_c = swap(h["up_x"], "inner"), swap(h["up"], "inner")
    pieces = [h[n] for n in names]
    h["help1"] = helped(h, h["beyond1"], h["across"], pieces, layout, 1)
    h["up_xc"], h["up_c"] = up_xc, up_c
    fence(h)
    help_o1 = hop(h["help1"], OUTWARD)
    h["help_o0"] = help_o0
    fence(h)
    out, late = add_last(
        h,
        total,
        [h["low_o"], h["whole"]],
        h["use"],
        [h["up"], h["up_c"], h["up_x"], h["up_xc"]],
        h["relayed"],
        h["across"],
        h["beyond1"],
        h["help_o0"],
        weight,
        layout,
    )
    h["help_o1"] = help_o1
    fence(h)
    return finished(h, out, late, h.pop("help_o1"), layout)


def owner_mask(slot, rank, adapters):
    which = slot[:, None, None] == jnp.arange(adapters, dtype=jnp.int32)[None, :, None]
    within = jnp.arange(MAXIMUM_RANK, dtype=jnp.int32)[None, None, :] < rank[:, None, None]
    return jnp.logical_and(which, within)


def gathered(tokens, tables, weight, down, up):
    slot, rank = slot_and_rank(*tables)
    axes = ("pool", "inner")
    base = jnp.dot(
        lax.all_gather(tokens, "tensor", axis=1, tiled=True),
        weight,
        preferred_element_type=jnp.float32,
    )
    downs = lax.all_gather(down, axes, axis=0, tiled=True)
    ups = lax.all_gather(up, axes, axis=0, tiled=True)
    mask = owner_mask(slot, rank, downs.shape[0])
    coords = lax.dot_general(
        tokens,
        downs.reshape(-1, downs.shape[2]),
        (((1,), (1,)), ((), ())),
        preferred_element_type=jnp.float32,
    ).reshape(mask.shape)
    coords = jnp.sum(jnp.where(mask, coords, 0.0), axis=1)
    low_rank = lax.psum(coords, "tensor").astype(jnp.bfloat16)
    spread = jnp.where(mask, low_rank[:, None, :], jnp.zeros((), jnp.bfloat16))
    delta = jnp.dot(
        spread.reshape(spread.shape[0], -1),
        ups.reshape(-1, ups.shape[2]),
        preferred_element_type=jnp.float32,
    ).astype(jnp.bfloat16)
    return (base + delta.astype(jnp.float32)).astype(jnp.bfloat16)


def shards(
    tokens,
    token_adapter_ids,
    adapter_pool_slot,
    adapter_rank_blocks,
    query_weight,
    pool_down_factors,
    pool_up_factors,
):
    tables = (token_adapter_ids, adapter_pool_slot, adapter_rank_blocks)
    whole_chain = tuple(lax.axis_size(a) for a in AXES) == (2, 4, 2, 2)
    run = chained if whole_chain else gathered
    return run(tokens, tables, query_weight, pool_down_factors, pool_up_factors)


def solution(mesh):
    in_specs = (
        P(("groups", "pool", "inner"), "tensor"),
        P(("groups", "pool", "inner")),
        P("groups"),
        P("groups"),
        P(None, "tensor"),
        P(("groups", "pool", "inner"), None, "tensor"),
        P(("groups", "pool", "inner"), None, "tensor"),
    )
    out_specs = P(("groups", "pool", "inner"), "tensor")
    return jax.shard_map(shards, mesh=mesh, in_specs=in_specs, out_specs=out_specs, check_vma=False)
```

time: 163 us -> 120 us (0.74)
  the two profiles are of different devices: /device:TPU:0 before, /device:TPU:17 now
where the time goes in v2:
time: 120 us; the launch traced here: 119 us
  Pallas kernels  45.2 us (38%)
  starting transfers between devices  45.1 us (38%)
  waiting for transfers between devices  19.3 us (16%)
  local copies, waits for them, and re-layouts  8.94 us (7%)
    pallas_call x37, Pallas kernels, call(): pl.pallas_call(counted, out_shape=[*shapes, jax.ShapeDtypeStruct(tick.sha...  43.4 us
    ppermute x13, starting transfers between devices, hop(): return lax.ppermute(x, 'tensor', pairs)  33 us
    ppermute x13, waiting for transfers between devices, hop(): return lax.ppermute(x, 'tensor', pairs)  15.2 us
    ppermute x13, starting transfers between devices, swap(): return lax.ppermute(x, axis, [(0, 1), (1, 0)])  12.1 us
    unnamed x18, local copies, waits for them, and re-layouts  8.94 us
    ppermute x13, waiting for transfers between devices, swap(): return lax.ppermute(x, axis, [(0, 1), (1, 0)])  4.05 us
  transfers between devices with their start and end apart: 26, of which 6 were waited for; matrix products, arithmetic and copies ran while one was open for 0% of the time, Pallas kernels for 36%

profile of v2, /device:TPU:17, one launch (start us, length us, event | category | flops | bytes accessed | tf_op | source)
XLA Modules:
  0.0 119.4 jit_solution(12936877829085757519)
XLA Ops:
  2.2 2.5 %collective-permute-start = (bf16[384,2048]{1,0:T(8,128)(2,1)}, bf16[384,2048]{1,0:T(8,128)(2,1)}, u32[]{:S(2)}, u32[]{:S(2)}) collective-permute-start(bf16[384,2048]{1,0:T(8,128)(2,1)} %refs_32_), channel_id=1, source_target_pairs={{4,8},{8,4},{5,9},{9,5},{6,10},{10,6},{7,11},{11,7},{20,24},{24,20... | collective-permute-start | bytes 4718600 | tf_op jit(solution)/shard_map/ppermute | solution.py:33
  5.8 2.0 %shard_map.74 = (bf16[160,2048]{1,0:T(8,128)(2,1)}, f32[8,128]{1,0:T(8,128)S(1)}) custom-call(bf16[384,2048]{1,0:T(8,128)(2,1)} %refs_32_, bf16[8192,1024]{1,0:T(8,128)(2,1)S(1)} %copy-done.2, f32[8,128]{1,0:T(8,128)S(1)} %shard_map.73.refs_2_), custom_call_target="tpu_custom_call" | custom-call | flops 999999995904 | tf_op jit(solution)/shard_map/pallas_call | solution.py:53
  8.7 2.9 %shard_map.76 = (bf16[224,2048]{1,0:T(8,128)(2,1)}, bf16[224,2048]{1,0:T(8,128)(2,1)}, bf16[160,2048]{1,0:T(8,128)(2,1)}, f32[8,128]{1,0:T(8,128)S(1)}) custom-call(bf16[384,2048]{1,0:T(8,128)(2,1)} %refs_32_, f32[8,128]{1,0:T(8,128)S(1)} %shard_map.75.refs_1_), custom_call_target="tpu_custom_call" | custom-call | flops 999999995904 | tf_op jit(solution)/shard_map/pallas_call | solution.py:53
  14.1 6.2 %collective-permute-start.7 = (bf16[224,2048]{1,0:T(8,128)(2,1)}, bf16[224,2048]{1,0:T(8,128)(2,1)}, u32[]{:S(2)}, u32[]{:S(2)}) collective-permute-start(bf16[224,2048]{1,0:T(8,128)(2,1)} %get-tuple-element.1224.refs_30_), channel_id=1, source_target_pairs={{4,0},{8,12},{5,1},{9,13},{6,2},{10,14},{7,3},{11,15},{20,16},{24,... | collective-permute-start | bytes 2752520 | tf_op jit(solution)/shard_map/ppermute | solution.py:33
  20.4 3.4 %shard_map.79 = (f32[384,1024]{1,0:T(8,128)S(1)}, f32[8,128]{1,0:T(8,128)S(1)}) custom-call(bf16[384,2048]{1,0:T(8,128)(2,1)} %refs_32_, bf16[8192,1024]{1,0:T(8,128)(2,1)S(1)} %copy-done.3, f32[8,128]{1,0:T(8,128)S(1)} %shard_map.78.refs_2_), custom_call_target="tpu_custom_call" | custom-call | flops 999999995904 | tf_op jit(solution)/shard_map/pallas_call | solution.py:53
  25.1 4.4 %shard_map.82 = (f32[384,128]{1,0:T(8,128)S(1)}, bf16[384,128]{1,0:T(8,128)(2,1)}, f32[8,128]{1,0:T(8,128)S(1)}) custom-call(s32[384,128]{1,0:T(8,128)S(1)} %fusion.refs_0_.refs_2_.refs_37_, bf16[384,2048]{1,0:T(8,128)(2,1)} %refs_32_, bf16[256,2048]{1,0:T(8,128)(2,1)} %bitcast.refs_2_, bf16[256,2048]{1,0:T(8,128)(2,1)} %bitcast.1.refs_3_, ...), custom_call_target="tpu_custom_call" | custom-call | flops 999999995904 | tf_op jit(solution)/shard_map/pallas_call | solution.py:53
  30.7 9.9 %collective-permute-done.refs_0_.refs_1_.refs_9_ = bf16[384,2048]{1,0:T(8,128)(2,1)} collective-permute-done((bf16[384,2048]{1,0:T(8,128)(2,1)}, bf16[384,2048]{1,0:T(8,128)(2,1)}, u32[]{:S(2)}, u32[]{:S(2)}) %collective-permute-start) | collective-permute-done | bytes 1572896 | tf_op jit(solution)/shard_map/ppermute | solution.py:33
  41.9 2.3 %shard_map.84 = (bf16[384,1536]{1,0:T(8,128)(2,1)}, f32[8,128]{1,0:T(8,128)S(1)}) custom-call(bf16[384,2048]{1,0:T(8,128)(2,1)} %collective-permute-done.refs_0_.refs_1_.refs_9_, f32[8,128]{1,0:T(8,128)S(1)} %shard_map.83.refs_1_), custom_call_target="tpu_custom_call" | custom-call | flops 999999995904 | tf_op jit(solution)/shard_map/pallas_call | solution.py:53
  44.2 2.4 %collective-permute-start.13 = (bf16[224,2048]{1,0:T(8,128)(2,1)}, bf16[224,2048]{1,0:T(8,128)(2,1)}, u32[]{:S(2)}, u32[]{:S(2)}) collective-permute-start(bf16[224,2048]{1,0:T(8,128)(2,1)} %collective-permute-done.4.refs_3_.refs_13_), channel_id=1, source_target_pairs={{4,8},{8,4},{5,9},{9,5},{6,10},{10,6},{7,11},{11,7},{20,24},{24,20... | collective-permute-start | bytes 2752520 | tf_op jit(solution)/shard_map/ppermute | solution.py:33
  47.9 5.0 %collective-permute-start.20 = (bf16[384,1536]{1,0:T(8,128)(2,1)}, bf16[384,1536]{1,0:T(8,128)(2,1)}, u32[]{:S(2)}, u32[]{:S(2)}) collective-permute-start(bf16[384,1536]{1,0:T(8,128)(2,1)} %get-tuple-element.1209.refs_15_), channel_id=1, source_target_pairs={{4,0},{8,12},{5,1},{9,13},{6,2},{10,14},{7,3},{11,15},{20,16},{24,... | collective-permute-start | bytes 3538952 | tf_op jit(solution)/shard_map/ppermute | solution.py:33
  54.7 2.6 %collective-permute-done.8.refs_8_ = bf16[2,128,2048]{2,1,0:T(8,128)(2,1)} collective-permute-done((bf16[2,128,2048]{2,1,0:T(8,128)(2,1)}, bf16[2,128,2048]{2,1,0:T(8,128)(2,1)}, u32[]{:S(2)}, u32[]{:S(2)}) %collective-permute-start.8) | collective-permute-done | bytes 1048608 | tf_op jit(solution)/shard_map/ppermute | solution.py:29
  57.7 2.9 %shard_map.90 = (f32[384,128]{1,0:T(8,128)S(1)}, bf16[384,128]{1,0:T(8,128)(2,1)}, f32[8,128]{1,0:T(8,128)S(1)}) custom-call(s32[384,128]{1,0:T(8,128)S(1)} %fusion.refs_0_.refs_2_.refs_37_, bf16[384,2048]{1,0:T(8,128)(2,1)} %refs_32_, bf16[256,2048]{1,0:T(8,128)(2,1)} %bitcast.3.refs_2_, f32[384,128]{1,0:T(8,128)S(1)} %get-tuple-element.774.refs_3_, ...), custom_call_target="tpu_custom_call" | custom-call | flops 999999995904 | tf_op jit(solution)/shard_map/pallas_call | solution.py:53
  62.2 5.0 %collective-permute-done.11.refs_1_.refs_4_ = bf16[384,128]{1,0:T(8,128)(2,1)} collective-permute-done((bf16[384,128]{1,0:T(8,128)(2,1)}, bf16[384,128]{1,0:T(8,128)(2,1)}, u32[]{:S(2)}, u32[]{:S(2)}) %collective-permute-start.11) | collective-permute-done | bytes 98336 | tf_op jit(solution)/shard_map/ppermute | solution.py:33
  68.7 2.2 %collective-permute-start.15 = (bf16[384,128]{1,0:T(8,128)(2,1)}, bf16[384,128]{1,0:T(8,128)(2,1)}, u32[]{:S(2)}, u32[]{:S(2)}) collective-permute-start(bf16[384,128]{1,0:T(8,128)(2,1)} %get-tuple-element.1219.refs_0_.refs_25_), channel_id=1, source_target_pairs={{4,8},{8,4},{5,9},{9,5},{6,10},{10,6},{7,11},{11,7},{20,24},{24,20... | collective-permute-start | bytes 294920 | tf_op jit(solution)/shard_map/ppermute | solution.py:33
  71.0 3.1 %collective-permute-start.18 = (bf16[160,2048]{1,0:T(8,128)(2,1)}, bf16[160,2048]{1,0:T(8,128)(2,1)}, u32[]{:S(2)}, u32[]{:S(2)}) collective-permute-start(bf16[160,2048]{1,0:T(8,128)(2,1)} %collective-permute-done.10.refs_4_.refs_14_), channel_id=1, source_target_pairs={{4,8},{8,4},{5,9},{9,5},{6,10},{10,6},{7,11},{11,7},{20,24},{24,20... | collective-permute-start | bytes 1966088 | tf_op jit(solution)/shard_map/ppermute | solution.py:33
  74.4 2.4 %collective-permute-start.16 = (bf16[160,2048]{1,0:T(8,128)(2,1)}, bf16[160,2048]{1,0:T(8,128)(2,1)}, u32[]{:S(2)}, u32[]{:S(2)}) collective-permute-start(bf16[160,2048]{1,0:T(8,128)(2,1)} %collective-permute-done.14.refs_8_.refs_18_), channel_id=1, source_target_pairs={{0,1},{1,0},{2,3},{3,2},{4,5},{5,4},{6,7},{7,6},{8,9},{9,8},{10,11... | collective-permute-start | bytes 1966088 | tf_op jit(solution)/shard_map/ppermute | solution.py:29
  82.2 5.1 %shard_map.101 = (bf16[224,1024]{1,0:T(8,128)(2,1)}, f32[8,128]{1,0:T(8,128)S(1)}) custom-call(bf16[224,2048]{1,0:T(8,128)(2,1)} %collective-permute-done.13.refs_0_.refs_5_.refs_1_, bf16[384,2048]{1,0:T(8,128)(2,1)} %collective-permute-done.refs_0_.refs_1_.refs_9_, bf16[160,2048]{1,0:T(8,128)(2,1)} %collective-permute-done.2.refs_2_.refs_1_.refs_16_, ...), custom_call_target="tpu_custom_call" | custom-call | flops 999999995904 | tf_op jit(solution)/shard_map/pallas_call | solution.py:53
  87.4 2.4 %collective-permute-start.24 = (bf16[224,1024]{1,0:T(8,128)(2,1)}, bf16[224,1024]{1,0:T(8,128)(2,1)}, u32[]{:S(2)}, u32[]{:S(2)}) collective-permute-start(bf16[224,1024]{1,0:T(8,128)(2,1)} %get-tuple-element.1204.refs_10_), channel_id=1, source_target_pairs={{4,0},{8,12},{5,1},{9,13},{6,2},{10,14},{7,3},{11,15},{20,16},{24,... | collective-permute-start | bytes 1376264 | tf_op jit(solution)/shard_map/ppermute | solution.py:33
  89.8 3.5 %copy-done.4 = bf16[8192,1024]{1,0:T(8,128)(2,1)S(1)} copy-done((bf16[8192,1024]{1,0:T(8,128)(2,1)S(1)}, bf16[8192,1024]{1,0:T(8,128)(2,1)}, u32[]{:S(2)}) %copy-start.4) | copy-done | bytes 16777240
  93.3 4.6 %shard_map.104 = (f32[384,1024]{1,0:T(8,128)S(1)}, f32[8,128]{1,0:T(8,128)S(1)}) custom-call(f32[384,1024]{1,0:T(8,128)S(1)} %get-tuple-element.1066.refs_0_, bf16[160,2048]{1,0:T(8,128)(2,1)} %collective-permute-done.2.refs_2_.refs_1_.refs_16_, bf16[224,2048]{1,0:T(8,128)(2,1)} %collective-permute-done.7.refs_2_.refs_31_, ...), custom_call_target="tpu_custom_call" | custom-call | flops 999999995904 | tf_op jit(solution)/shard_map/pallas_call | solution.py:53
  98.8 4.6 %shard_map.106 = (bf16[160,1024]{1,0:T(8,128)(2,1)}, f32[8,128]{1,0:T(8,128)S(1)}) custom-call(bf16[160,2048]{1,0:T(8,128)(2,1)} %collective-permute-done.18.refs_0_.refs_10_.refs_2_, bf16[384,2048]{1,0:T(8,128)(2,1)} %collective-permute-done.refs_0_.refs_1_.refs_9_, bf16[160,2048]{1,0:T(8,128)(2,1)} %collective-permute-done.2.refs_2_.refs_1_.refs_16_, ...), custom_call_target="tpu_custom_call" | custom-call | flops 999999995904 | tf_op jit(solution)/shard_map/pallas_call | solution.py:53
  103.5 2.3 %collective-permute-start.25 = (bf16[160,1024]{1,0:T(8,128)(2,1)}, bf16[160,1024]{1,0:T(8,128)(2,1)}, u32[]{:S(2)}, u32[]{:S(2)}) collective-permute-start(bf16[160,1024]{1,0:T(8,128)(2,1)} %get-tuple-element.1205.refs_11_), channel_id=1, source_target_pairs={{4,0},{8,12},{5,1},{9,13},{6,2},{10,14},{7,3},{11,15},{20,16},{24,... | collective-permute-start | bytes 983048 | tf_op jit(solution)/shard_map/ppermute | solution.py:33
  105.8 3.7 %copy-done.5 = bf16[8192,1024]{1,0:T(8,128)(2,1)S(1)} copy-done((bf16[8192,1024]{1,0:T(8,128)(2,1)S(1)}, bf16[8192,1024]{1,0:T(8,128)(2,1)}, u32[]{:S(2)}) %copy-start.5) | copy-done | bytes 16777240
  109.5 7.9 %shard_map.109 = (bf16[384,1024]{1,0:T(8,128)(2,1)}, f32[160,1024]{1,0:T(8,128)S(1)}, f32[8,128]{1,0:T(8,128)}) custom-call(bf16[384,128]{1,0:T(8,128)(2,1)} %collective-permute-done.19.refs_0_.refs_24_, bf16[384,128]{1,0:T(8,128)(2,1)} %get-tuple-element.1232.refs_1_.refs_38_, s32[384,128]{1,0:T(8,128)S(1)} %copy-done.1, bf16[256,1024]{1,0:T(8,128)(2,1)} %bitcast.4.refs_3_, ...), custom_call_target="tpu_custom_call" | custom-call | flops 999999995904 | tf_op jit(solution)/shard_map/pallas_call | solution.py:53
  (88 shorter events, 25.5 us)
Async XLA Ops:
  0.0 25.1 %collective-permute-start.3 = (bf16[2,128,2048]{2,1,0:T(8,128)(2,1)}, bf16[2,128,2048]{2,1,0:T(8,128)(2,1)}, u32[]{:S(2)}, u32[]{:S(2)}) collective-permute-start(bf16[2,128,2048]{2,1,0:T(8,128)(2,1)} %refs_5_), channel_id=1, source_target_pairs={{0,2},{2,0},{1,3},{3,1},{4,6},{6,4},{5,7},{7,5},{8,10},{10,8},{9,1... | collective-permute-start | bytes 3145736 | tf_op jit(solution)/shard_map/ppermute | solution.py:29
  1.3 11.2 %collective-permute-start.1 = (bf16[2,128,2048]{2,1,0:T(8,128)(2,1)}, bf16[2,128,2048]{2,1,0:T(8,128)(2,1)}, u32[]{:S(2)}, u32[]{:S(2)}) collective-permute-start(bf16[2,128,2048]{2,1,0:T(8,128)(2,1)} %refs_5_), channel_id=1, source_target_pairs={{0,1},{1,0},{2,3},{3,2},{4,5},{5,4},{6,7},{7,6},{8,9},{9,8},{10,11... | collective-permute-start | bytes 3145736 | tf_op jit(solution)/shard_map/ppermute | solution.py:29
  2.2 38.3 %collective-permute-start = (bf16[384,2048]{1,0:T(8,128)(2,1)}, bf16[384,2048]{1,0:T(8,128)(2,1)}, u32[]{:S(2)}, u32[]{:S(2)}) collective-permute-start(bf16[384,2048]{1,0:T(8,128)(2,1)} %refs_32_), channel_id=1, source_target_pairs={{4,8},{8,4},{5,9},{9,5},{6,10},{10,6},{7,11},{11,7},{20,24},{24,20... | collective-permute-start | bytes 4718600 | tf_op jit(solution)/shard_map/ppermute | solution.py:33
  7.8 16.0 %collective-permute-start.2 = (bf16[160,2048]{1,0:T(8,128)(2,1)}, bf16[160,2048]{1,0:T(8,128)(2,1)}, u32[]{:S(2)}, u32[]{:S(2)}) collective-permute-start(bf16[160,2048]{1,0:T(8,128)(2,1)} %get-tuple-element.1203.refs_9_), channel_id=1, source_target_pairs={{0,4},{4,0},{8,12},{12,8},{1,5},{5,1},{9,13},{13,9},{2,6},{6,2},{1... | collective-permute-start | bytes 1966088 | tf_op jit(solution)/shard_map/ppermute | solution.py:33
  12.6 31.6 %collective-permute-start.4 = (bf16[224,2048]{1,0:T(8,128)(2,1)}, bf16[224,2048]{1,0:T(8,128)(2,1)}, u32[]{:S(2)}, u32[]{:S(2)}) collective-permute-start(bf16[224,2048]{1,0:T(8,128)(2,1)} %get-tuple-element.1221.refs_27_), channel_id=1, source_target_pairs={{0,4},{12,8},{1,5},{13,9},{2,6},{14,10},{3,7},{15,11},{16,20},{28,... | collective-permute-start | bytes 2752520 | tf_op jit(solution)/shard_map/ppermute | solution.py:33
  14.1 32.5 %collective-permute-start.7 = (bf16[224,2048]{1,0:T(8,128)(2,1)}, bf16[224,2048]{1,0:T(8,128)(2,1)}, u32[]{:S(2)}, u32[]{:S(2)}) collective-permute-start(bf16[224,2048]{1,0:T(8,128)(2,1)} %get-tuple-element.1224.refs_30_), channel_id=1, source_target_pairs={{4,0},{8,12},{5,1},{9,13},{6,2},{10,14},{7,3},{11,15},{20,16},{24,... | collective-permute-start | bytes 2752520 | tf_op jit(solution)/shard_map/ppermute | solution.py:33
  23.8 20.4 %collective-permute-start.5 = (bf16[160,2048]{1,0:T(8,128)(2,1)}, bf16[160,2048]{1,0:T(8,128)(2,1)}, u32[]{:S(2)}, u32[]{:S(2)}) collective-permute-start(bf16[160,2048]{1,0:T(8,128)(2,1)} %collective-permute-done.2.refs_2_.refs_1_.refs_16_), channel_id=1, source_target_pairs={{0,16},{16,0},{1,17},{17,1},{2,18},{18,2},{3,19},{19,3},{4,20},{20... | collective-permute-start | bytes 1966088 | tf_op jit(solution)/shard_map/ppermute | solution.py:29
  29.5 17.1 %collective-permute-start.6 = (bf16[160,2048]{1,0:T(8,128)(2,1)}, bf16[160,2048]{1,0:T(8,128)(2,1)}, u32[]{:S(2)}, u32[]{:S(2)}) collective-permute-start(bf16[160,2048]{1,0:T(8,128)(2,1)} %collective-permute-done.2.refs_2_.refs_1_.refs_16_), channel_id=1, source_target_pairs={{0,2},{2,0},{1,3},{3,1},{4,6},{6,4},{5,7},{7,5},{8,10},{10,8},{9,1... | collective-permute-start | bytes 1966088 | tf_op jit(solution)/shard_map/ppermute | solution.py:29
  40.6 21.4 %collective-permute-start.10 = (bf16[160,2048]{1,0:T(8,128)(2,1)}, bf16[160,2048]{1,0:T(8,128)(2,1)}, u32[]{:S(2)}, u32[]{:S(2)}) collective-permute-start(bf16[160,2048]{1,0:T(8,128)(2,1)} %get-tuple-element.1222.refs_28_), channel_id=1, source_target_pairs={{0,4},{12,8},{1,5},{13,9},{2,6},{14,10},{3,7},{15,11},{16,20},{28,... | collective-permute-start | bytes 1966088 | tf_op jit(solution)/shard_map/ppermute | solution.py:33
  44.2 26.7 %collective-permute-start.13 = (bf16[224,2048]{1,0:T(8,128)(2,1)}, bf16[224,2048]{1,0:T(8,128)(2,1)}, u32[]{:S(2)}, u32[]{:S(2)}) collective-permute-start(bf16[224,2048]{1,0:T(8,128)(2,1)} %collective-permute-done.4.refs_3_.refs_13_), channel_id=1, source_target_pairs={{4,8},{8,4},{5,9},{9,5},{6,10},{10,6},{7,11},{11,7},{20,24},{24,20... | collective-permute-start | bytes 2752520 | tf_op jit(solution)/shard_map/ppermute | solution.py:33
  46.6 27.4 %collective-permute-start.14 = (bf16[160,2048]{1,0:T(8,128)(2,1)}, bf16[160,2048]{1,0:T(8,128)(2,1)}, u32[]{:S(2)}, u32[]{:S(2)}) collective-permute-start(bf16[160,2048]{1,0:T(8,128)(2,1)} %collective-permute-done.6.refs_4_.refs_20_), channel_id=1, source_target_pairs={{0,16},{16,0},{1,17},{17,1},{2,18},{18,2},{3,19},{19,3},{4,20},{20... | collective-permute-start | bytes 1966088 | tf_op jit(solution)/shard_map/ppermute | solution.py:29
  47.9 50.0 %collective-permute-start.20 = (bf16[384,1536]{1,0:T(8,128)(2,1)}, bf16[384,1536]{1,0:T(8,128)(2,1)}, u32[]{:S(2)}, u32[]{:S(2)}) collective-permute-start(bf16[384,1536]{1,0:T(8,128)(2,1)} %get-tuple-element.1209.refs_15_), channel_id=1, source_target_pairs={{4,0},{8,12},{5,1},{9,13},{6,2},{10,14},{7,3},{11,15},{20,16},{24,... | collective-permute-start | bytes 3538952 | tf_op jit(solution)/shard_map/ppermute | solution.py:33
  53.0 4.4 %collective-permute-start.8 = (bf16[2,128,2048]{2,1,0:T(8,128)(2,1)}, bf16[2,128,2048]{2,1,0:T(8,128)(2,1)}, u32[]{:S(2)}, u32[]{:S(2)}) collective-permute-start(bf16[2,128,2048]{2,1,0:T(8,128)(2,1)} %collective-permute-done.3.refs_7_), channel_id=1, source_target_pairs={{0,1},{1,0},{2,3},{3,2},{4,5},{5,4},{6,7},{7,6},{8,9},{9,8},{10,11... | collective-permute-start | bytes 3145736 | tf_op jit(solution)/shard_map/ppermute | solution.py:29
  60.7 6.5 %collective-permute-start.11 = (bf16[384,128]{1,0:T(8,128)(2,1)}, bf16[384,128]{1,0:T(8,128)(2,1)}, u32[]{:S(2)}, u32[]{:S(2)}) collective-permute-start(bf16[384,128]{1,0:T(8,128)(2,1)} %get-tuple-element.1197.refs_3_), channel_id=1, source_target_pairs={{0,4},{12,8},{1,5},{13,9},{2,6},{14,10},{3,7},{15,11},{16,20},{28,... | collective-permute-start | bytes 294920 | tf_op jit(solution)/shard_map/ppermute | solution.py:33
  62.0 5.2 %collective-permute-start.12 = (bf16[160,2048]{1,0:T(8,128)(2,1)}, bf16[160,2048]{1,0:T(8,128)(2,1)}, u32[]{:S(2)}, u32[]{:S(2)}) collective-permute-start(bf16[160,2048]{1,0:T(8,128)(2,1)} %collective-permute-done.5.refs_6_.refs_22_), channel_id=1, source_target_pairs={{0,1},{1,0},{2,3},{3,2},{4,5},{5,4},{6,7},{7,6},{8,9},{9,8},{10,11... | collective-permute-start | bytes 1966088 | tf_op jit(solution)/shard_map/ppermute | solution.py:29
  68.7 5.7 %collective-permute-start.15 = (bf16[384,128]{1,0:T(8,128)(2,1)}, bf16[384,128]{1,0:T(8,128)(2,1)}, u32[]{:S(2)}, u32[]{:S(2)}) collective-permute-start(bf16[384,128]{1,0:T(8,128)(2,1)} %get-tuple-element.1219.refs_0_.refs_25_), channel_id=1, source_target_pairs={{4,8},{8,4},{5,9},{9,5},{6,10},{10,6},{7,11},{11,7},{20,24},{24,20... | collective-permute-start | bytes 294920 | tf_op jit(solution)/shard_map/ppermute | solution.py:33
  71.0 27.0 %collective-permute-start.18 = (bf16[160,2048]{1,0:T(8,128)(2,1)}, bf16[160,2048]{1,0:T(8,128)(2,1)}, u32[]{:S(2)}, u32[]{:S(2)}) collective-permute-start(bf16[160,2048]{1,0:T(8,128)(2,1)} %collective-permute-done.10.refs_4_.refs_14_), channel_id=1, source_target_pairs={{4,8},{8,4},{5,9},{9,5},{6,10},{10,6},{7,11},{11,7},{20,24},{24,20... | collective-permute-start | bytes 1966088 | tf_op jit(solution)/shard_map/ppermute | solution.py:33
  74.4 4.4 %collective-permute-start.16 = (bf16[160,2048]{1,0:T(8,128)(2,1)}, bf16[160,2048]{1,0:T(8,128)(2,1)}, u32[]{:S(2)}, u32[]{:S(2)}) collective-permute-start(bf16[160,2048]{1,0:T(8,128)(2,1)} %collective-permute-done.14.refs_8_.refs_18_), channel_id=1, source_target_pairs={{0,1},{1,0},{2,3},{3,2},{4,5},{5,4},{6,7},{7,6},{8,9},{9,8},{10,11... | collective-permute-start | bytes 1966088 | tf_op jit(solution)/shard_map/ppermute | solution.py:29
  79.8 18.2 %collective-permute-start.19 = (bf16[384,128]{1,0:T(8,128)(2,1)}, bf16[384,128]{1,0:T(8,128)(2,1)}, u32[]{:S(2)}, u32[]{:S(2)}) collective-permute-start(bf16[384,128]{1,0:T(8,128)(2,1)} %get-tuple-element.1232.refs_1_.refs_38_), channel_id=1, source_target_pairs={{4,0},{8,12},{5,1},{9,13},{6,2},{10,14},{7,3},{11,15},{20,16},{24,... | collective-permute-start | bytes 294920 | tf_op jit(solution)/shard_map/ppermute | solution.py:33
  81.7 16.3 %collective-permute-start.21 = (bf16[2,128,1024]{2,1,0:T(8,128)(2,1)}, bf16[2,128,1024]{2,1,0:T(8,128)(2,1)}, u32[]{:S(2)}, u32[]{:S(2)}) collective-permute-start(bf16[2,128,1024]{2,1,0:T(8,128)(2,1)} %refs_33_), channel_id=1, source_target_pairs={{0,2},{2,0},{1,3},{3,1},{4,6},{6,4},{5,7},{7,5},{8,10},{10,8},{9,1... | collective-permute-start | bytes 1572872 | tf_op jit(solution)/shard_map/ppermute | solution.py:29
  87.4 18.4 %collective-permute-start.24 = (bf16[224,1024]{1,0:T(8,128)(2,1)}, bf16[224,1024]{1,0:T(8,128)(2,1)}, u32[]{:S(2)}, u32[]{:S(2)}) collective-permute-start(bf16[224,1024]{1,0:T(8,128)(2,1)} %get-tuple-element.1204.refs_10_), channel_id=1, source_target_pairs={{4,0},{8,12},{5,1},{9,13},{6,2},{10,14},{7,3},{11,15},{20,16},{24,... | collective-permute-start | bytes 1376264 | tf_op jit(solution)/shard_map/ppermute | solution.py:33
  98.0 5.5 %collective-permute-start.22 = (bf16[2,128,1024]{2,1,0:T(8,128)(2,1)}, bf16[2,128,1024]{2,1,0:T(8,128)(2,1)}, u32[]{:S(2)}, u32[]{:S(2)}) collective-permute-start(bf16[2,128,1024]{2,1,0:T(8,128)(2,1)} %refs_33_), channel_id=1, source_target_pairs={{0,1},{1,0},{2,3},{3,2},{4,5},{5,4},{6,7},{7,6},{8,9},{9,8},{10,11... | collective-permute-start | bytes 1572872 | tf_op jit(solution)/shard_map/ppermute | solution.py:29
  98.7 4.8 %collective-permute-start.23 = (bf16[2,128,1024]{2,1,0:T(8,128)(2,1)}, bf16[2,128,1024]{2,1,0:T(8,128)(2,1)}, u32[]{:S(2)}, u32[]{:S(2)}) collective-permute-start(bf16[2,128,1024]{2,1,0:T(8,128)(2,1)} %collective-permute-done.21.refs_35_), channel_id=1, source_target_pairs={{0,1},{1,0},{2,3},{3,2},{4,5},{5,4},{6,7},{7,6},{8,9},{9,8},{10,11... | collective-permute-start | bytes 1572872 | tf_op jit(solution)/shard_map/ppermute | solution.py:29
  103.5 13.9 %collective-permute-start.25 = (bf16[160,1024]{1,0:T(8,128)(2,1)}, bf16[160,1024]{1,0:T(8,128)(2,1)}, u32[]{:S(2)}, u32[]{:S(2)}) collective-permute-start(bf16[160,1024]{1,0:T(8,128)(2,1)} %get-tuple-element.1205.refs_11_), channel_id=1, source_target_pairs={{4,0},{8,12},{5,1},{9,13},{6,2},{10,14},{7,3},{11,15},{20,16},{24,... | collective-permute-start | bytes 983048 | tf_op jit(solution)/shard_map/ppermute | solution.py:33
  (11 other events, 81.5 us)

commit v3 on v2

v3 whole, which is shorter than its diff:
```python
import itertools

import jax
import jax.numpy as jnp
import numpy as np
from jax import lax
from jax.experimental import pallas as pl
from jax.experimental.pallas import tpu as pltpu
from jax.sharding import PartitionSpec as P

MAXIMUM_RANK = 128
RBLK = 16
AXES = ("groups", "tensor", "pool", "inner")

PAIRS = [(0, 1), (1, 0), (2, 3), (3, 2)]
OUTWARD = [(1, 0), (2, 3)]
INWARD = [(0, 1), (3, 2)]


def lookup(indices, table):
    count = table.shape[0]
    match = indices[..., None] == jnp.arange(count, dtype=jnp.int32)
    return jnp.sum(jnp.where(match, table, 0), axis=-1)


def slot_and_rank(ids, slots, blocks):
    return lookup(ids, slots), RBLK * lookup(ids, blocks)


def swap(x, axis):
    return lax.ppermute(x, axis, [(0, 1), (1, 0)])


def inside(x, step):
    shape = (2, 4, 2, 2)
    pairs = []
    for place in itertools.product(*map(range, shape)):
        groups, z, pool, inner = place
        to = step(*place) if z in (1, 2) else (groups, z, pool, 1 - inner)
        pairs.append(tuple(int(np.ravel_multi_index(p, shape)) for p in (place, to)))
    return lax.ppermute(x, AXES, pairs)


def hop_middle(x):
    return inside(x, lambda g, z, p, i: (g, 3 - z, p, i))


def swap_inside(x, axis):
    steps = {
        "groups": lambda g, z, p, i: (1 - g, z, p, i),
        "pool": lambda g, z, p, i: (g, z, 1 - p, i),
        "inner": lambda g, z, p, i: (g, z, p, 1 - i),
    }
    return inside(x, steps[axis])


def hop(x, pairs):
    return lax.ppermute(x, "tensor", pairs)


VMEM = pl.BlockSpec(memory_space=pltpu.VMEM)
ANY = pl.BlockSpec(memory_space=pl.ANY)
HBM = pl.BlockSpec(memory_space=pltpu.HBM)


def call(held, body, out_shapes, operands, in_specs, out_specs=None, scratch=(), room=16, alias=None):
    single = not isinstance(out_shapes, list)
    shapes = [out_shapes] if single else out_shapes
    out_specs = out_specs or [VMEM] * len(shapes)
    ins, outs = len(operands), len(shapes)
    tick = held["tick"]

    def counted(*refs):
        into = refs[ins + 1 + outs]
        into[...] = refs[ins][...] + 1.0
        body(*refs[:ins], *refs[ins + 1 : ins + 1 + outs], *refs[ins + 2 + outs :])

    *results, held["tick"] = pl.pallas_call(
        counted,
        out_shape=[*shapes, jax.ShapeDtypeStruct(tick.shape, tick.dtype)],
        in_specs=[*in_specs, VMEM],
        out_specs=[*out_specs, VMEM],
        scratch_shapes=list(scratch),
        input_output_aliases=alias or {},
        cost_estimate=pl.CostEstimate(flops=10**12, bytes_accessed=0, transcendentals=0),
        compiler_params=pltpu.CompilerParams(vmem_limit_bytes=room << 20),
    )(*operands, tick)
    return results[0] if single else results


def fence(held):
    call(held, lambda: None, [], [], [])
    names = sorted(held)
    held.update(zip(names, lax.optimization_barrier(tuple(held[n] for n in names))))


def array(*shape, dtype=jnp.bfloat16):
    return jax.ShapeDtypeStruct(shape, dtype)


def dot(a, b):
    return jnp.dot(a, b, preferred_element_type=jnp.float32)


class Place:
    def __init__(self):
        z = lax.axis_index("tensor")
        self.own, self.partner = z, z ^ 1
        self.end = jnp.logical_or(z == 0, z == 3)
        self.near = jnp.where(self.end, 3 - self.partner, 3 - z)
        self.far = jnp.where(self.end, 3 - z, 3 - self.partner)
        self.seat = lax.axis_index(("groups", "pool", "inner"))
        self.mine = lax.axis_index(("pool", "inner"))


class Layout:
    def __init__(self, tokens, weight):
        self.tall, self.width = tokens.shape
        self.columns = weight.shape[1]
        self.deep = self.width // 8
        self.rows = self.deep // 2
        self.cut = self.tall * 7 // 12
        self.sizes = [self.cut, self.tall - self.cut]

    def sides(self, ref):
        for side in range(2):
            columns = pl.ds(side * self.columns, self.columns)
            yield side * self.rows, ref.at[:, columns]


def run_copies(copies):
    for copy in copies:
        copy.start()
    for copy in copies:
        copy.wait()


LARGE = 50


def first_rows(held, tokens, weight, layout):
    rows = layout.rows

    def body(t_ref, w_ref, out_ref, sem):
        place = Place()

        @pl.when(place.end)
        def _():
            start = place.far * layout.width + place.seat * layout.deep
            run_copies(
                [
                    pltpu.make_async_copy(
                        w_ref.at[pl.ds(pl.multiple_of(start + first, rows), rows)],
                        into,
                        sem.at[i],
                    )
                    for i, (first, into) in enumerate(layout.sides(out_ref))
                ]
            )

        @pl.when(jnp.logical_not(place.end))
        def _():
            run_copies(
                [pltpu.make_async_copy(t_ref.at[pl.ds(0, rows)], out_ref, sem.at[0])]
            )

    return call(
        held,
        body,
        array(rows, layout.width),
        [tokens, weight],
        [HBM, HBM],
        scratch=[pltpu.SemaphoreType.DMA((2,))],
        room=LARGE,
    )


def cut_up(held, tokens, layout):
    tall, width, rows, cut = layout.tall, layout.width, layout.rows, layout.cut
    cuts = [(rows, tall - rows), (0, cut), (cut, tall - cut)]

    def body(t_ref, *refs):
        *into_refs, all_ref, sem = refs
        run_copies([pltpu.make_async_copy(t_ref, all_ref, sem.at[0])])
        run_copies(
            [
                pltpu.make_async_copy(all_ref.at[pl.ds(at, size)], into, sem.at[i])
                for i, ((at, size), into) in enumerate(zip(cuts, into_refs))
            ]
        )

    return call(
        held,
        body,
        [array(size, width) for _, size in cuts],
        [tokens],
        [ANY],
        [ANY] * len(cuts),
        [pltpu.VMEM((tall, width), tokens.dtype), pltpu.SemaphoreType.DMA((3,))],
    )


PARTS = 4


class Rows:
    def __init__(self, x_ref, start, held_ref, sem):
        self.depth, self.held_ref, self.copies = held_ref.shape[0] // PARTS, held_ref, []
        for i in range(PARTS):
            some = pl.ds(pl.multiple_of(start + i * self.depth, 128), self.depth)
            self.copies.append(
                pltpu.make_async_copy(
                    x_ref.at[some], held_ref.at[pl.ds(i * self.depth, self.depth)], sem.at[i]
                )
            )
        for copy in self.copies:
            copy.start()

    def dot(self, a_ref):
        total = 0.0
        for i, copy in enumerate(self.copies):
            copy.wait()
            some = pl.ds(i * self.depth, self.depth)
            total += dot(a_ref[:, some], self.held_ref[some, :])
        return total


def started(*copies):
    for copy in copies:
        copy.start()
    return copies


def waited(copies):
    for copy in copies:
        copy.wait()


def room(count, layout):
    shape = (layout.width, layout.columns)
    return [
        x
        for _ in range(count)
        for x in (pltpu.VMEM(shape, jnp.bfloat16), pltpu.SemaphoreType.DMA((PARTS,)))
    ]


def sums(layout):
    return array(layout.tall, layout.columns, dtype=jnp.float32)


def sums_room(layout):
    return [
        pltpu.VMEM((layout.tall, layout.columns), jnp.float32),
        pltpu.SemaphoreType.DMA((9,)),
    ]


def own_block(held, tokens, weight, layout):
    def body(a_ref, w_ref, out_ref, held_ref, w_sem, a_held, sum_ref, sem):
        load = started(pltpu.make_async_copy(a_ref, a_held, sem.at[0]))
        w = Rows(w_ref, Place().own * layout.width, held_ref, w_sem)
        waited(load)
        sum_ref[...] = w.dot(a_held)
        run_copies([pltpu.make_async_copy(sum_ref, out_ref, sem.at[1])])

    return call(
        held,
        body,
        sums(layout),
        [tokens, weight],
        [ANY, HBM],
        [HBM],
        room(1, layout)
        + [pltpu.VMEM((layout.tall, layout.width), jnp.bfloat16)]
        + sums_room(layout),
        room=LARGE,
    )


def add_block(held, total, at_end, inside, weight, layout):
    width, tall = layout.width, layout.tall
    arrays = [x for side in (at_end, inside) if side for x in side[1]]

    def body(total_ref, w_ref, *refs):
        array_refs = list(refs[: len(arrays)])
        out_ref, w_held, w_sem, a_held, sum_ref, sem = refs[len(arrays) :]
        place = Place()

        def run(name, part_refs):
            w = Rows(w_ref, getattr(place, name) * width, w_held, w_sem)
            loads, start = [], 0
            for i, ref in enumerate(part_refs):
                into = a_held.at[pl.ds(start, ref.shape[0])]
                loads.append(pltpu.make_async_copy(ref, into, sem.at[i]))
                start += ref.shape[0]
            started(*loads)
            more = started(pltpu.make_async_copy(total_ref, sum_ref, sem.at[3]))
            waited(loads)
            some = w.dot(a_held)
            waited(more)
            sum_ref[...] += some
            run_copies([pltpu.make_async_copy(sum_ref, out_ref, sem.at[4])])

        for side, here in ((at_end, place.end), (inside, jnp.logical_not(place.end))):
            if side:
                mine = [array_refs.pop(0) for _ in side[1]]
                pl.when(here)(lambda side=side, mine=mine: run(side[0], mine))

    return call(
        held,
        body,
        sums(layout),
        [total, weight, *arrays],
        [ANY, HBM] + [ANY] * len(arrays),
        [ANY],
        room(1, layout) + [pltpu.VMEM((tall, width), jnp.bfloat16)] + sums_room(layout),
        room=LARGE,
        alias={0: 0},
    )


def add_last(held, total, low, use, ups, relayed, beyond, term, weight, layout):
    adapters, rank, columns = ups[0].shape
    count = len(ups)
    cut, last = layout.sizes
    tall, width = layout.tall, layout.width

    def body(hop_ref, low_ref, use_ref, *refs):
        up_refs = refs[:count]
        total_ref, relayed_ref, b0_ref, b1_ref, term_ref, w_ref = refs[count : count + 6]
        out_ref, late_ref, *scratch = refs[count + 6 :]
        w_held, w_sem, a_held, t_held, u_held, first_ref, sum_ref, sem = scratch
        place = Place()
        at_end = [pltpu.make_async_copy(relayed_ref, a_held, sem.at[0])]
        inside = [
            pltpu.make_async_copy(b0_ref, a_held.at[pl.ds(0, cut)], sem.at[0]),
            pltpu.make_async_copy(b1_ref, a_held.at[pl.ds(cut, last)], sem.at[1]),
        ]

        loads = started(
            *[
                pltpu.make_async_copy(
                    up_ref,
                    u_held.at[pl.ds(i * adapters * rank, adapters * rank)],
                    sem.at[i + 3],
                )
                for i, up_ref in enumerate(up_refs)
            ],
            pltpu.make_async_copy(total_ref, sum_ref, sem.at[2]),
        )

        @pl.when(place.end)
        def _():
            started(*at_end)

        @pl.when(jnp.logical_not(place.end))
        def _():
            started(*inside)

        w = Rows(w_ref, jnp.where(place.end, place.near, place.far) * width, w_held, w_sem)
        more = started(pltpu.make_async_copy(term_ref, t_held, sem.at[7]))
        low = jnp.where(place.end, hop_ref[...], low_ref[...])
        some = [
            jnp.where(use_ref[...] == (place.mine ^ turn) * adapters + j, low, 0)
            for turn in range(count)
            for j in range(adapters)
        ]
        spread = jnp.concatenate(some, axis=1)
        waited(loads)
        terms = dot(spread, u_held[...])
        sum_ref[...] += terms.astype(jnp.bfloat16).astype(jnp.float32)

        @pl.when(place.end)
        def _():
            waited(at_end)

        @pl.when(jnp.logical_not(place.end))
        def _():
            waited(inside)

        sum_ref[...] += w.dot(a_held)
        waited(more)
        late = started(
            pltpu.make_async_copy(sum_ref.at[pl.ds(cut, last)], late_ref, sem.at[0])
        )
        first_ref[...] = (sum_ref[:cut, :] + t_held[...].astype(jnp.float32)).astype(
            first_ref.dtype
        )
        run_copies([pltpu.make_async_copy(first_ref, out_ref.at[pl.ds(0, cut)], sem.at[1])])
        waited(late)

    return call(
        held,
        body,
        [array(tall, columns), array(last, columns, dtype=jnp.float32)],
        [*low, use, *[u.reshape(-1, columns) for u in ups]]
        + [total, relayed, *beyond, term, weight],
        [VMEM] * 3 + [ANY] * (count + 5) + [HBM],
        [ANY, ANY],
        room(1, layout)
        + [
            pltpu.VMEM((tall, width), jnp.bfloat16),
            pltpu.VMEM((cut, columns), jnp.bfloat16),
            pltpu.VMEM((count * adapters * rank, columns), jnp.bfloat16),
            pltpu.VMEM((cut, columns), jnp.bfloat16),
        ]
        + sums_room(layout),
        room=LARGE,
    )


def helped(held, beyond, pieces, layout, i):
    size, width, columns = layout.sizes[i], layout.width, layout.columns
    count, deep = len(pieces), layout.deep

    def body(beyond_ref, *refs):
        piece_refs = refs[:count]
        out_ref, b_held, w_held, sem = refs[count:]
        seat = Place().seat
        load = started(pltpu.make_async_copy(beyond_ref, b_held, sem.at[0]))
        lends = started(
            *[
                pltpu.make_async_copy(
                    part,
                    w_held.at[pl.ds(k * deep + first, layout.rows)],
                    sem.at[1 + 2 * k + side],
                )
                for k, piece_ref in enumerate(piece_refs)
                for side, (first, part) in enumerate(layout.sides(piece_ref))
            ]
        )
        waited(load)
        total = 0.0
        step = count // 4
        for first in range(0, count, step):
            blocks = [
                b_held[:, pl.ds(pl.multiple_of((seat ^ k) * deep, deep), deep)]
                for k in range(first, first + step)
            ]
            waited(lends[2 * first : 2 * (first + step)])
            some = w_held[first * deep : (first + step) * deep, :]
            total += dot(jnp.concatenate(blocks, axis=1), some)
        out_ref[...] = total.astype(out_ref.dtype)

    return call(
        held,
        body,
        array(size, columns),
        [beyond, *pieces],
        [ANY] * (1 + count),
        scratch=[
            pltpu.VMEM((size, width), jnp.bfloat16),
            pltpu.VMEM((width, columns), jnp.bfloat16),
            pltpu.SemaphoreType.DMA((1 + 2 * count,)),
        ],
    )


def finished(held, out, late, term, layout):
    kept = [held[n] for n in sorted(held) if n != "tick"]
    cut, last = layout.sizes

    def body(out_ref, late_ref, term_ref, *refs):
        into_ref, sum_ref, sem = refs[len(kept) :]
        sum_ref[...] = (late_ref[...] + term_ref[...].astype(jnp.float32)).astype(
            sum_ref.dtype
        )
        run_copies([pltpu.make_async_copy(sum_ref, into_ref.at[pl.ds(cut, last)], sem)])

    return pl.pallas_call(
        body,
        out_shape=array(*out.shape),
        in_specs=[ANY, VMEM, VMEM] + [ANY] * len(kept),
        out_specs=ANY,
        scratch_shapes=[
            pltpu.VMEM((last, layout.columns), out.dtype),
            pltpu.SemaphoreType.DMA,
        ],
        input_output_aliases={0: 0},
        compiler_params=pltpu.CompilerParams(vmem_limit_bytes=16 << 20),
    )(out, late, term, *kept)


def coords_of(held, tokens, use, downs, turns, before=None):
    adapters, rank = downs[0].shape[0], downs[0].shape[1]
    count = len(downs)

    def body(use_ref, tokens_ref, *refs):
        out_ref, sent_ref = refs[-2:]
        mine = Place().mine
        total = refs[count][...] if before is not None else 0.0
        for turn, down_ref in zip(turns, refs[:count]):
            coords = lax.dot_general(
                tokens_ref[...],
                down_ref[...],
                (((1,), (1,)), ((), ())),
                preferred_element_type=jnp.float32,
            )
            for j in range(adapters):
                some = coords[:, j * rank : (j + 1) * rank]
                mask = use_ref[...] == (mine ^ turn) * adapters + j
                total = total + jnp.where(mask, some, 0.0)
        out_ref[...] = total
        sent_ref[...] = total.astype(sent_ref.dtype)

    flat = [d.reshape(-1, d.shape[2]) for d in downs]
    more = [] if before is None else [before]
    shape = (tokens.shape[0], rank)
    return call(
        held,
        body,
        [array(*shape, dtype=jnp.float32), array(*shape)],
        [use, tokens, *flat, *more],
        [VMEM] * (2 + count + len(more)),
    )


def added(held, a, b):
    def body(a_ref, b_ref, out_ref):
        sums = a_ref[...].astype(jnp.float32) + b_ref[...].astype(jnp.float32)
        out_ref[...] = sums.astype(out_ref.dtype)

    return call(held, body, array(*a.shape), [a, b], [VMEM] * 2)


def chained(tokens, tables, weight, down, up):
    layout = Layout(tokens, weight)
    across = hop_middle(tokens)
    h = dict(tick=jnp.zeros((8, 128), jnp.float32), down=down, up=up, tokens=tokens)
    h["ids"], h["slots"], h["blocks"] = tables
    fence(h)
    down_x, down_c = swap(h["down"], "pool"), swap(h["down"], "inner")
    h["first"] = first_rows(h, h["tokens"], weight, layout)
    fence(h)
    first_p = hop(h["first"], PAIRS)
    h["rest"], h["part0"], h["part1"] = cut_up(h, h["tokens"], layout)
    slot, rank = slot_and_rank(h.pop("ids"), h.pop("slots"), h.pop("blocks"))
    row = jnp.arange(MAXIMUM_RANK, dtype=jnp.int32)[None, :]
    h["use"] = jnp.where(row < rank[:, None], slot[:, None], -1)
    h["down_c"] = down_c
    fence(h)
    inner0 = hop(h["part0"], INWARD)
    fence(h)
    rest_o = hop(h["rest"], OUTWARD)
    total = own_block(h, h["tokens"], weight, layout)
    h["lent"] = first_p
    fence(h)
    lent_y = swap_inside(h["lent"], "groups")
    h["down_x"] = down_x
    fence(h)
    down_xc = swap(h["down_x"], "inner")
    downs = [h["down"], h["down_c"], h["down_x"]]
    coords, _ = coords_of(h, h["tokens"], h["use"], downs, [0, 1, 2])
    h["down_xc"] = down_xc
    fence(h)
    lent_x = swap_inside(h["lent"], "pool")
    fence(h)
    coords, h["coords"] = coords_of(h, h["tokens"], h["use"], [h["down_xc"]], [3], coords)
    h["lent_y"] = lent_y
    fence(h)
    coords_p = hop(h["coords"], INWARD)
    h["across"] = across
    fence(h)
    relayed = hop(h["across"], OUTWARD)
    h["inner0"] = inner0
    fence(h)
    beyond0 = hop_middle(h["inner0"])
    h["rest_o"], h["coords_p"] = rest_o, coords_p
    fence(h)
    inner1 = hop(h["part1"], INWARD)
    h["lent_x"] = lent_x
    fence(h)
    lent_d = swap_inside(h["lent_x"], "groups")
    fence(h)
    h["pair"] = added(h, coords, h["coords_p"])
    fence(h)
    pair_m = hop_middle(h["pair"])
    fence(h)
    at_end = ("partner", [h["lent"], h["rest_o"]])
    total = add_block(h, total, at_end, ("near", [h["across"]]), weight, layout)
    h["lent_d"] = lent_d
    fence(h)
    lent_c = swap_inside(h["lent"], "inner")
    h["lent_c"] = lent_c
    fence(h)
    lent_yc = swap_inside(h["lent_y"], "inner")
    h["lent_yc"], h["beyond0"], h["inner1"] = lent_yc, beyond0, inner1
    fence(h)
    beyond1 = hop_middle(h["inner1"])
    fence(h)
    lent_xc, lent_dc = swap_inside(h["lent_x"], "inner"), swap_inside(h["lent_d"], "inner")
    h["pair_m"] = pair_m
    fence(h)
    h["whole"] = added(h, h["pair"], h["pair_m"])
    h["lent_xc"], h["lent_dc"] = lent_xc, lent_dc
    fence(h)
    low_o = hop(h["whole"], OUTWARD)
    fence(h)
    up_x = swap(h["up"], "pool")
    fence(h)
    names = ("lent", "lent_c", "lent_x", "lent_xc", "lent_y", "lent_yc", "lent_d", "lent_dc")
    pieces = [h[n] for n in names]
    h["help0"] = helped(h, h["beyond0"], pieces, layout, 0)
    fence(h)
    help_o0 = hop(h["help0"], OUTWARD)
    fence(h)
    halves = [h["inner0"], h["inner1"]]
    total = add_block(h, total, None, ("partner", halves), weight, layout)
    h["relayed"], h["beyond1"], h["up_x"], h["low_o"] = relayed, beyond1, up_x, low_o
    fence(h)
    up_xc, up_c = swap(h["up_x"], "inner"), swap(h["up"], "inner")
    fence(h)
    pieces = [h[n] for n in names]
    h["help1"] = helped(h, h["beyond1"], pieces, layout, 1)
    h["up_xc"], h["up_c"] = up_xc, up_c
    fence(h)
    help_o1 = hop(h["help1"], OUTWARD)
    h["help_o0"] = help_o0
    fence(h)
    out, late = add_last(
        h,
        total,
        [h["low_o"], h["whole"]],
        h["use"],
        [h["up"], h["up_c"], h["up_x"], h["up_xc"]],
        h["relayed"],
        [h["beyond0"], h["beyond1"]],
        h["help_o0"],
        weight,
        layout,
    )
    h["help_o1"] = help_o1
    fence(h)
    return finished(h, out, late, h.pop("help_o1"), layout)


def owner_mask(slot, rank, adapters):
    which = slot[:, None, None] == jnp.arange(adapters, dtype=jnp.int32)[None, :, None]
    within = jnp.arange(MAXIMUM_RANK, dtype=jnp.int32)[None, None, :] < rank[:, None, None]
    return jnp.logical_and(which, within)


def gathered(tokens, tables, weight, down, up):
    slot, rank = slot_and_rank(*tables)
    axes = ("pool", "inner")
    base = jnp.dot(
        lax.all_gather(tokens, "tensor", axis=1, tiled=True),
        weight,
        preferred_element_type=jnp.float32,
    )
    downs = lax.all_gather(down, axes, axis=0, tiled=True)
    ups = lax.all_gather(up, axes, axis=0, tiled=True)
    mask = owner_mask(slot, rank, downs.shape[0])
    coords = lax.dot_general(
        tokens,
        downs.reshape(-1, downs.shape[2]),
        (((1,), (1,)), ((), ())),
        preferred_element_type=jnp.float32,
    ).reshape(mask.shape)
    coords = jnp.sum(jnp.where(mask, coords, 0.0), axis=1)
    low_rank = lax.psum(coords, "tensor").astype(jnp.bfloat16)
    spread = jnp.where(mask, low_rank[:, None, :], jnp.zeros((), jnp.bfloat16))
    delta = jnp.dot(
        spread.reshape(spread.shape[0], -1),
        ups.reshape(-1, ups.shape[2]),
        preferred_element_type=jnp.float32,
    ).astype(jnp.bfloat16)
    return (base + delta.astype(jnp.float32)).astype(jnp.bfloat16)


def shards(
    tokens,
    token_adapter_ids,
    adapter_pool_slot,
    adapter_rank_blocks,
    query_weight,
    pool_down_factors,
    pool_up_factors,
):
    tables = (token_adapter_ids, adapter_pool_slot, adapter_rank_blocks)
    whole_chain = tuple(lax.axis_size(a) for a in AXES) == (2, 4, 2, 2)
    run = chained if whole_chain else gathered
    return run(tokens, tables, query_weight, pool_down_factors, pool_up_factors)


def solution(mesh):
    in_specs = (
        P(("groups", "pool", "inner"), "tensor"),
        P(("groups", "pool", "inner")),
        P("groups"),
        P("groups"),
        P(None, "tensor"),
        P(("groups", "pool", "inner"), None, "tensor"),
        P(("groups", "pool", "inner"), None, "tensor"),
    )
    out_specs = P(("groups", "pool", "inner"), "tensor")
    return jax.shard_map(shards, mesh=mesh, in_specs=in_specs, out_specs=out_specs, check_vma=False)
```

time: 120 us -> 105 us (0.88)
  the two profiles are of different devices: /device:TPU:17 before, /device:TPU:0 now
where the time goes in v3:
time: 105 us
  Pallas kernels  41.9 us (40%)
  starting transfers between devices  31.3 us (30%)
  waiting for transfers between devices  28.9 us (28%)
  local copies, waits for them, and re-layouts  1.79 us (2%)
    pallas_call x42, Pallas kernels, call(): pl.pallas_call(counted, out_shape=[*shapes, jax.ShapeDtypeStruct(tick.sha...  40.1 us
    ppermute x9, starting transfers between devices, hop(): return lax.ppermute(x, 'tensor', pairs)  24.7 us
    ppermute x9, waiting for transfers between devices, hop(): return lax.ppermute(x, 'tensor', pairs)  18 us
    ppermute x6, waiting for transfers between devices, swap(): return lax.ppermute(x, axis, [(0, 1), (1, 0)])  6.86 us
    ppermute x6, starting transfers between devices, swap(): return lax.ppermute(x, axis, [(0, 1), (1, 0)])  4.06 us
    ppermute x11, waiting for transfers between devices, inside(): return lax.ppermute(x, AXES, pairs)  3.98 us
    ppermute x11, starting transfers between devices, inside(): return lax.ppermute(x, AXES, pairs)  2.53 us
  transfers between devices with their start and end apart: 26, of which 12 were waited for; matrix products, arithmetic and copies ran while one was open for 0% of the time, Pallas kernels for 38%

profile of v3, /device:TPU:0, one launch (start us, length us, event | category | flops | bytes accessed | tf_op | source)
XLA Modules:
  0.0 104.6 jit_solution(7921826846263186775)
XLA Ops:
  0.0 2.9 %collective-permute-start.3 = (bf16[2,128,2048]{2,1,0:T(8,128)(2,1)}, bf16[2,128,2048]{2,1,0:T(8,128)(2,1)}, u32[]{:S(2)}, u32[]{:S(2)}) collective-permute-start(bf16[2,128,2048]{2,1,0:T(8,128)(2,1)} %refs_5_), channel_id=1, source_target_pairs={{0,2},{2,0},{1,3},{3,1},{4,6},{6,4},{5,7},{7,5},{8,10},{10,8},{9,1... | collective-permute-start | bytes 3145736 | tf_op jit(solution)/shard_map/ppermute | solution.py:31
  3.5 1.8 %shard_map.74 = (bf16[128,2048]{1,0:T(8,128)(2,1)}, f32[8,128]{1,0:T(8,128)S(1)}) custom-call(bf16[384,2048]{1,0:T(8,128)(2,1)} %refs_31_, bf16[8192,1024]{1,0:T(8,128)(2,1)} %refs_12_.1, f32[8,128]{1,0:T(8,128)S(1)} %shard_map.73.refs_2_), custom_call_target="tpu_custom_call" | custom-call | flops 999999995904 | tf_op jit(solution)/shard_map/pallas_call | solution.py:78
  5.3 2.8 %collective-permute-start.2 = (bf16[128,2048]{1,0:T(8,128)(2,1)}, bf16[128,2048]{1,0:T(8,128)(2,1)}, u32[]{:S(2)}, u32[]{:S(2)}) collective-permute-start(bf16[128,2048]{1,0:T(8,128)(2,1)} %get-tuple-element.1420.refs_9_), channel_id=1, source_target_pairs={{0,4},{4,0},{8,12},{12,8},{1,5},{5,1},{9,13},{13,9},{2,6},{6,2},{1... | collective-permute-start | bytes 1572872 | tf_op jit(solution)/shard_map/ppermute | solution.py:58
  8.1 2.9 %shard_map.76 = (bf16[256,2048]{1,0:T(8,128)(2,1)}, bf16[224,2048]{1,0:T(8,128)(2,1)}, bf16[160,2048]{1,0:T(8,128)(2,1)}, f32[8,128]{1,0:T(8,128)S(1)}) custom-call(bf16[384,2048]{1,0:T(8,128)(2,1)} %refs_31_, f32[8,128]{1,0:T(8,128)S(1)} %shard_map.75.refs_1_), custom_call_target="tpu_custom_call" | custom-call | flops 999999995904 | tf_op jit(solution)/shard_map/pallas_call | solution.py:78
  12.0 2.8 %collective-permute-start.6 = (bf16[224,2048]{1,0:T(8,128)(2,1)}, bf16[224,2048]{1,0:T(8,128)(2,1)}, u32[]{:S(2)}, u32[]{:S(2)}) collective-permute-start(bf16[224,2048]{1,0:T(8,128)(2,1)} %get-tuple-element.1437.refs_26_), channel_id=1, source_target_pairs={{0,4},{12,8},{1,5},{13,9},{2,6},{14,10},{3,7},{15,11},{16,20},{28,... | collective-permute-start | bytes 2752520 | tf_op jit(solution)/shard_map/ppermute | solution.py:58
  16.1 4.1 %shard_map.79 = (f32[384,1024]{1,0:T(8,128)S(1)}, f32[8,128]{1,0:T(8,128)S(1)}) custom-call(bf16[384,2048]{1,0:T(8,128)(2,1)} %refs_31_, bf16[8192,1024]{1,0:T(8,128)(2,1)} %refs_12_.1, f32[8,128]{1,0:T(8,128)S(1)} %shard_map.78.refs_2_), custom_call_target="tpu_custom_call" | custom-call | flops 999999995904 | tf_op jit(solution)/shard_map/pallas_call | solution.py:78
  21.1 5.3 %collective-permute-done.3.refs_7_ = bf16[2,128,2048]{2,1,0:T(8,128)(2,1)} collective-permute-done((bf16[2,128,2048]{2,1,0:T(8,128)(2,1)}, bf16[2,128,2048]{2,1,0:T(8,128)(2,1)}, u32[]{:S(2)}, u32[]{:S(2)}) %collective-permute-start.3) | collective-permute-done | bytes 1048608 | tf_op jit(solution)/shard_map/ppermute | solution.py:31
  26.4 4.4 %shard_map.82 = (f32[384,128]{1,0:T(8,128)S(1)}, bf16[384,128]{1,0:T(8,128)(2,1)}, f32[8,128]{1,0:T(8,128)S(1)}) custom-call(s32[384,128]{1,0:T(8,128)S(1)} %fusion.refs_0_.refs_2_.refs_36_, bf16[384,2048]{1,0:T(8,128)(2,1)} %refs_31_, bf16[256,2048]{1,0:T(8,128)(2,1)} %bitcast.refs_2_, bf16[256,2048]{1,0:T(8,128)(2,1)} %bitcast.1.refs_3_, ...), custom_call_target="tpu_custom_call" | custom-call | flops 999999995904 | tf_op jit(solution)/shard_map/pallas_call | solution.py:78
  31.4 2.9 %shard_map.85 = (f32[384,128]{1,0:T(8,128)S(1)}, bf16[384,128]{1,0:T(8,128)(2,1)}, f32[8,128]{1,0:T(8,128)S(1)}) custom-call(s32[384,128]{1,0:T(8,128)S(1)} %fusion.refs_0_.refs_2_.refs_36_, bf16[384,2048]{1,0:T(8,128)(2,1)} %refs_31_, bf16[256,2048]{1,0:T(8,128)(2,1)} %bitcast.3.refs_2_, f32[384,128]{1,0:T(8,128)S(1)} %get-tuple-element.809.refs_3_, ...), custom_call_target="tpu_custom_call" | custom-call | flops 999999995904 | tf_op jit(solution)/shard_map/pallas_call | solution.py:78
  34.4 5.9 %collective-permute-start.7 = (bf16[384,128]{1,0:T(8,128)(2,1)}, bf16[384,128]{1,0:T(8,128)(2,1)}, u32[]{:S(2)}, u32[]{:S(2)}) collective-permute-start(bf16[384,128]{1,0:T(8,128)(2,1)} %get-tuple-element.1414.refs_3_), channel_id=1, source_target_pairs={{0,4},{12,8},{1,5},{13,9},{2,6},{14,10},{3,7},{15,11},{16,20},{28,... | collective-permute-start | bytes 294920 | tf_op jit(solution)/shard_map/ppermute | solution.py:58
  43.2 6.5 %collective-permute-start.13 = (bf16[160,2048]{1,0:T(8,128)(2,1)}, bf16[160,2048]{1,0:T(8,128)(2,1)}, u32[]{:S(2)}, u32[]{:S(2)}) collective-permute-start(bf16[160,2048]{1,0:T(8,128)(2,1)} %get-tuple-element.1438.refs_27_), channel_id=1, source_target_pairs={{0,4},{12,8},{1,5},{13,9},{2,6},{14,10},{3,7},{15,11},{16,20},{28,... | collective-permute-start | bytes 1966088 | tf_op jit(solution)/shard_map/ppermute | solution.py:58
  49.7 1.6 %shard_map.92 = (bf16[384,128]{1,0:T(8,128)(2,1)}, f32[8,128]{1,0:T(8,128)S(1)}) custom-call(f32[384,128]{1,0:T(8,128)S(1)} %get-tuple-element.921.refs_0_, bf16[384,128]{1,0:T(8,128)(2,1)} %collective-permute-done.7.refs_1_.refs_4_, f32[8,128]{1,0:T(8,128)S(1)} %shard_map.91.refs_2_), custom_call_target="tpu_custom_call" | custom-call | flops 999999995904 | tf_op jit(solution)/shard_map/pallas_call | solution.py:78
  51.7 5.0 %shard_map.95 = (f32[384,1024]{1,0:T(8,128)S(1)}, f32[8,128]{1,0:T(8,128)S(1)}) custom-call(f32[384,1024]{1,0:T(8,128)S(1)} %get-tuple-element.970.refs_0_, bf16[8192,1024]{1,0:T(8,128)(2,1)} %refs_12_.1, bf16[128,2048]{1,0:T(8,128)(2,1)} %collective-permute-done.2.refs_2_.refs_1_.refs_15_, ...), custom_call_target="tpu_custom_call", output_to_operand_aliasing={{0}: (0, {})} | custom-call | flops 999999995904 | tf_op jit(solution)/shard_map/pallas_call | solution.py:78
  56.9 2.2 %collective-permute-done.11.refs_2_.refs_16_ = bf16[128,2048]{1,0:T(8,128)(2,1)} collective-permute-done((bf16[128,2048]{1,0:T(8,128)(2,1)}, bf16[128,2048]{1,0:T(8,128)(2,1)}, u32[]{:S(2)}, u32[]{:S(2)}) %collective-permute-start.11) | collective-permute-done | bytes 524320 | tf_op jit(solution)/shard_map/ppermute | solution.py:41
  59.3 2.9 %collective-permute-done.13.refs_3_.refs_14_ = bf16[160,2048]{1,0:T(8,128)(2,1)} collective-permute-done((bf16[160,2048]{1,0:T(8,128)(2,1)}, bf16[160,2048]{1,0:T(8,128)(2,1)}, u32[]{:S(2)}, u32[]{:S(2)}) %collective-permute-start.13) | collective-permute-done | bytes 655392 | tf_op jit(solution)/shard_map/ppermute | solution.py:58
  62.8 1.6 %shard_map.101 = (bf16[384,128]{1,0:T(8,128)(2,1)}, f32[8,128]{1,0:T(8,128)S(1)}) custom-call(bf16[384,128]{1,0:T(8,128)(2,1)} %get-tuple-element.1435.refs_0_.refs_24_, bf16[384,128]{1,0:T(8,128)(2,1)} %collective-permute-done.15.refs_1_.refs_25_, f32[8,128]{1,0:T(8,128)S(1)} %shard_map.100.refs_2_), custom_call_target="tpu_custom_call" | custom-call | flops 999999995904 | tf_op jit(solution)/shard_map/pallas_call | solution.py:78
  68.1 4.0 %shard_map.105 = (bf16[224,1024]{1,0:T(8,128)(2,1)}, f32[8,128]{1,0:T(8,128)S(1)}) custom-call(bf16[224,2048]{1,0:T(8,128)(2,1)} %collective-permute-done.12.refs_0_.refs_9_.refs_1_, bf16[128,2048]{1,0:T(8,128)(2,1)} %collective-permute-done.2.refs_2_.refs_1_.refs_15_, bf16[128,2048]{1,0:T(8,128)(2,1)} %collective-permute-done.11.refs_2_.refs_16_, ...), custom_call_target="tpu_custom_call" | custom-call | flops 999999995904 | tf_op jit(solution)/shard_map/pallas_call | solution.py:78
  74.7 4.5 %collective-permute-done.20.refs_8_.refs_28_ = bf16[384,2048]{1,0:T(8,128)(2,1)} collective-permute-done((bf16[384,2048]{1,0:T(8,128)(2,1)}, bf16[384,2048]{1,0:T(8,128)(2,1)}, u32[]{:S(2)}, u32[]{:S(2)}) %collective-permute-start.20) | collective-permute-done | bytes 1572896 | tf_op jit(solution)/shard_map/ppermute | solution.py:58
  82.3 3.6 %shard_map.111 = (bf16[160,1024]{1,0:T(8,128)(2,1)}, f32[8,128]{1,0:T(8,128)S(1)}) custom-call(bf16[160,2048]{1,0:T(8,128)(2,1)} %collective-permute-done.18.refs_0_.refs_10_.refs_2_, bf16[128,2048]{1,0:T(8,128)(2,1)} %collective-permute-done.2.refs_2_.refs_1_.refs_15_, bf16[128,2048]{1,0:T(8,128)(2,1)} %collective-permute-done.11.refs_2_.refs_16_, ...), custom_call_target="tpu_custom_call" | custom-call | flops 999999995904 | tf_op jit(solution)/shard_map/pallas_call | solution.py:78
  86.0 1.6 %collective-permute-start.25 = (bf16[160,1024]{1,0:T(8,128)(2,1)}, bf16[160,1024]{1,0:T(8,128)(2,1)}, u32[]{:S(2)}, u32[]{:S(2)}) collective-permute-start(bf16[160,1024]{1,0:T(8,128)(2,1)} %get-tuple-element.1422.refs_11_), channel_id=1, source_target_pairs={{4,0},{8,12},{5,1},{9,13},{6,2},{10,14},{7,3},{11,15},{20,16},{24,... | collective-permute-start | bytes 983048 | tf_op jit(solution)/shard_map/ppermute | solution.py:58
  87.6 3.8 %collective-permute-done.24.refs_11_.refs_12_ = bf16[224,1024]{1,0:T(8,128)(2,1)} collective-permute-done((bf16[224,1024]{1,0:T(8,128)(2,1)}, bf16[224,1024]{1,0:T(8,128)(2,1)}, u32[]{:S(2)}, u32[]{:S(2)}) %collective-permute-start.24) | collective-permute-done | bytes 458784 | tf_op jit(solution)/shard_map/ppermute | solution.py:58
  91.4 7.8 %shard_map.114 = (bf16[384,1024]{1,0:T(8,128)(2,1)}, f32[160,1024]{1,0:T(8,128)S(1)}, f32[8,128]{1,0:T(8,128)}) custom-call(bf16[384,128]{1,0:T(8,128)(2,1)} %collective-permute-done.19.refs_0_.refs_23_, bf16[384,128]{1,0:T(8,128)(2,1)} %get-tuple-element.1448.refs_1_.refs_37_, s32[384,128]{1,0:T(8,128)S(1)} %copy-done.1, bf16[256,1024]{1,0:T(8,128)(2,1)} %bitcast.4.refs_3_, ...), custom_call_target="tpu_custom_call" | custom-call | flops 999999995904 | tf_op jit(solution)/shard_map/pallas_call | solution.py:78
  99.2 3.5 %collective-permute-done.25.term_ref = bf16[160,1024]{1,0:T(8,128)(2,1)} collective-permute-done((bf16[160,1024]{1,0:T(8,128)(2,1)}, bf16[160,1024]{1,0:T(8,128)(2,1)}, u32[]{:S(2)}, u32[]{:S(2)}) %collective-permute-start.25) | collective-permute-done | bytes 327712 | tf_op jit(solution)/shard_map/ppermute | solution.py:58
  102.7 1.8 %shard_map.115 = bf16[384,1024]{1,0:T(8,128)(2,1)} custom-call(bf16[384,1024]{1,0:T(8,128)(2,1)} %get-tuple-element.1381.out_ref, f32[160,1024]{1,0:T(8,128)S(1)} %get-tuple-element.1382.late_ref, bf16[160,1024]{1,0:T(8,128)(2,1)} %collective-permute-done.25.term_ref, ...), custom_call_target="tpu_custom_call", output_to_operand_aliasing={{}: (0, {})} | custom-call | tf_op jit(solution)/shard_map/pallas_call | solution.py:471
  (87 shorter events, 17.7 us)
Async XLA Ops:
  0.0 26.4 %collective-permute-start.3 = (bf16[2,128,2048]{2,1,0:T(8,128)(2,1)}, bf16[2,128,2048]{2,1,0:T(8,128)(2,1)}, u32[]{:S(2)}, u32[]{:S(2)}) collective-permute-start(bf16[2,128,2048]{2,1,0:T(8,128)(2,1)} %refs_5_), channel_id=1, source_target_pairs={{0,2},{2,0},{1,3},{3,1},{4,6},{6,4},{5,7},{7,5},{8,10},{10,8},{9,1... | collective-permute-start | bytes 3145736 | tf_op jit(solution)/shard_map/ppermute | solution.py:31
  2.9 9.0 %collective-permute-start.1 = (bf16[2,128,2048]{2,1,0:T(8,128)(2,1)}, bf16[2,128,2048]{2,1,0:T(8,128)(2,1)}, u32[]{:S(2)}, u32[]{:S(2)}) collective-permute-start(bf16[2,128,2048]{2,1,0:T(8,128)(2,1)} %refs_5_), channel_id=1, source_target_pairs={{0,1},{1,0},{2,3},{3,2},{4,5},{5,4},{6,7},{7,6},{8,9},{9,8},{10,11... | collective-permute-start | bytes 3145736 | tf_op jit(solution)/shard_map/ppermute | solution.py:31
  3.0 37.3 %collective-permute-start = (bf16[384,2048]{1,0:T(8,128)(2,1)}, bf16[384,2048]{1,0:T(8,128)(2,1)}, u32[]{:S(2)}, u32[]{:S(2)}) collective-permute-start(bf16[384,2048]{1,0:T(8,128)(2,1)} %refs_31_), channel_id=1, source_target_pairs={{0,1},{1,0},{2,3},{3,2},{4,8},{5,9},{6,10},{7,11},{8,4},{9,5},{10,... | collective-permute-start | bytes 4718600 | tf_op jit(solution)/shard_map/ppermute | solution.py:41
  5.3 15.8 %collective-permute-start.2 = (bf16[128,2048]{1,0:T(8,128)(2,1)}, bf16[128,2048]{1,0:T(8,128)(2,1)}, u32[]{:S(2)}, u32[]{:S(2)}) collective-permute-start(bf16[128,2048]{1,0:T(8,128)(2,1)} %get-tuple-element.1420.refs_9_), channel_id=1, source_target_pairs={{0,4},{4,0},{8,12},{12,8},{1,5},{5,1},{9,13},{13,9},{2,6},{6,2},{1... | collective-permute-start | bytes 1572872 | tf_op jit(solution)/shard_map/ppermute | solution.py:58
  12.0 29.6 %collective-permute-start.6 = (bf16[224,2048]{1,0:T(8,128)(2,1)}, bf16[224,2048]{1,0:T(8,128)(2,1)}, u32[]{:S(2)}, u32[]{:S(2)}) collective-permute-start(bf16[224,2048]{1,0:T(8,128)(2,1)} %get-tuple-element.1437.refs_26_), channel_id=1, source_target_pairs={{0,4},{12,8},{1,5},{13,9},{2,6},{14,10},{3,7},{15,11},{16,20},{28,... | collective-permute-start | bytes 2752520 | tf_op jit(solution)/shard_map/ppermute | solution.py:58
  14.8 28.4 %collective-permute-start.8 = (bf16[256,2048]{1,0:T(8,128)(2,1)}, bf16[256,2048]{1,0:T(8,128)(2,1)}, u32[]{:S(2)}, u32[]{:S(2)}) collective-permute-start(bf16[256,2048]{1,0:T(8,128)(2,1)} %get-tuple-element.1440.refs_29_), channel_id=1, source_target_pairs={{4,0},{8,12},{5,1},{9,13},{6,2},{10,14},{7,3},{11,15},{20,16},{24,... | collective-permute-start | bytes 3145736 | tf_op jit(solution)/shard_map/ppermute | solution.py:58
  21.1 13.3 %collective-permute-start.5 = (bf16[128,2048]{1,0:T(8,128)(2,1)}, bf16[128,2048]{1,0:T(8,128)(2,1)}, u32[]{:S(2)}, u32[]{:S(2)}) collective-permute-start(bf16[128,2048]{1,0:T(8,128)(2,1)} %collective-permute-done.2.refs_2_.refs_1_.refs_15_), channel_id=1, source_target_pairs={{0,1},{1,0},{2,3},{3,2},{4,20},{5,21},{6,22},{7,23},{8,24},{9,25},... | collective-permute-start | bytes 1572872 | tf_op jit(solution)/shard_map/ppermute | solution.py:41
  26.4 4.4 %collective-permute-start.4 = (bf16[2,128,2048]{2,1,0:T(8,128)(2,1)}, bf16[2,128,2048]{2,1,0:T(8,128)(2,1)}, u32[]{:S(2)}, u32[]{:S(2)}) collective-permute-start(bf16[2,128,2048]{2,1,0:T(8,128)(2,1)} %collective-permute-done.3.refs_7_), channel_id=1, source_target_pairs={{0,1},{1,0},{2,3},{3,2},{4,5},{5,4},{6,7},{7,6},{8,9},{9,8},{10,11... | collective-permute-start | bytes 3145736 | tf_op jit(solution)/shard_map/ppermute | solution.py:31
  30.8 18.8 %collective-permute-start.9 = (bf16[128,2048]{1,0:T(8,128)(2,1)}, bf16[128,2048]{1,0:T(8,128)(2,1)}, u32[]{:S(2)}, u32[]{:S(2)}) collective-permute-start(bf16[128,2048]{1,0:T(8,128)(2,1)} %collective-permute-done.2.refs_2_.refs_1_.refs_15_), channel_id=1, source_target_pairs={{0,1},{1,0},{2,3},{3,2},{4,6},{5,7},{6,4},{7,5},{8,10},{9,11},{10,... | collective-permute-start | bytes 1572872 | tf_op jit(solution)/shard_map/ppermute | solution.py:41
  34.4 8.8 %collective-permute-start.7 = (bf16[384,128]{1,0:T(8,128)(2,1)}, bf16[384,128]{1,0:T(8,128)(2,1)}, u32[]{:S(2)}, u32[]{:S(2)}) collective-permute-start(bf16[384,128]{1,0:T(8,128)(2,1)} %get-tuple-element.1414.refs_3_), channel_id=1, source_target_pairs={{0,4},{12,8},{1,5},{13,9},{2,6},{14,10},{3,7},{15,11},{16,20},{28,... | collective-permute-start | bytes 294920 | tf_op jit(solution)/shard_map/ppermute | solution.py:58
  40.3 38.9 %collective-permute-start.20 = (bf16[384,2048]{1,0:T(8,128)(2,1)}, bf16[384,2048]{1,0:T(8,128)(2,1)}, u32[]{:S(2)}, u32[]{:S(2)}) collective-permute-start(bf16[384,2048]{1,0:T(8,128)(2,1)} %collective-permute-done.refs_4_.refs_0_), channel_id=1, source_target_pairs={{4,0},{8,12},{5,1},{9,13},{6,2},{10,14},{7,3},{11,15},{20,16},{24,... | collective-permute-start | bytes 4718600 | tf_op jit(solution)/shard_map/ppermute | solution.py:58
  41.6 20.5 %collective-permute-start.12 = (bf16[224,2048]{1,0:T(8,128)(2,1)}, bf16[224,2048]{1,0:T(8,128)(2,1)}, u32[]{:S(2)}, u32[]{:S(2)}) collective-permute-start(bf16[224,2048]{1,0:T(8,128)(2,1)} %collective-permute-done.6.refs_2_.refs_13_), channel_id=1, source_target_pairs={{0,1},{1,0},{2,3},{3,2},{4,8},{5,9},{6,10},{7,11},{8,4},{9,5},{10,... | collective-permute-start | bytes 2752520 | tf_op jit(solution)/shard_map/ppermute | solution.py:41
  43.2 19.0 %collective-permute-start.13 = (bf16[160,2048]{1,0:T(8,128)(2,1)}, bf16[160,2048]{1,0:T(8,128)(2,1)}, u32[]{:S(2)}, u32[]{:S(2)}) collective-permute-start(bf16[160,2048]{1,0:T(8,128)(2,1)} %get-tuple-element.1438.refs_27_), channel_id=1, source_target_pairs={{0,4},{12,8},{1,5},{13,9},{2,6},{14,10},{3,7},{15,11},{16,20},{28,... | collective-permute-start | bytes 1966088 | tf_op jit(solution)/shard_map/ppermute | solution.py:58
  49.7 7.1 %collective-permute-start.10 = (bf16[128,2048]{1,0:T(8,128)(2,1)}, bf16[128,2048]{1,0:T(8,128)(2,1)}, u32[]{:S(2)}, u32[]{:S(2)}) collective-permute-start(bf16[128,2048]{1,0:T(8,128)(2,1)} %collective-permute-done.9.refs_3_.refs_19_), channel_id=1, source_target_pairs={{0,1},{1,0},{2,3},{3,2},{4,20},{5,21},{6,22},{7,23},{8,24},{9,25},... | collective-permute-start | bytes 1572872 | tf_op jit(solution)/shard_map/ppermute | solution.py:41
  51.2 11.6 %collective-permute-start.15 = (bf16[384,128]{1,0:T(8,128)(2,1)}, bf16[384,128]{1,0:T(8,128)(2,1)}, u32[]{:S(2)}, u32[]{:S(2)}) collective-permute-start(bf16[384,128]{1,0:T(8,128)(2,1)} %get-tuple-element.1435.refs_0_.refs_24_), channel_id=1, source_target_pairs={{0,1},{1,0},{2,3},{3,2},{4,8},{5,9},{6,10},{7,11},{8,4},{9,5},{10,... | collective-permute-start | bytes 294920 | tf_op jit(solution)/shard_map/ppermute | solution.py:41
  62.2 18.1 %collective-permute-start.18 = (bf16[160,2048]{1,0:T(8,128)(2,1)}, bf16[160,2048]{1,0:T(8,128)(2,1)}, u32[]{:S(2)}, u32[]{:S(2)}) collective-permute-start(bf16[160,2048]{1,0:T(8,128)(2,1)} %collective-permute-done.13.refs_3_.refs_14_), channel_id=1, source_target_pairs={{0,1},{1,0},{2,3},{3,2},{4,8},{5,9},{6,10},{7,11},{8,4},{9,5},{10,... | collective-permute-start | bytes 1966088 | tf_op jit(solution)/shard_map/ppermute | solution.py:41
  62.3 3.2 %collective-permute-start.16 = (bf16[128,2048]{1,0:T(8,128)(2,1)}, bf16[128,2048]{1,0:T(8,128)(2,1)}, u32[]{:S(2)}, u32[]{:S(2)}) collective-permute-start(bf16[128,2048]{1,0:T(8,128)(2,1)} %collective-permute-done.10.refs_7_.refs_17_), channel_id=1, source_target_pairs={{0,1},{1,0},{2,3},{3,2},{4,5},{5,4},{6,7},{7,6},{8,9},{9,8},{10,11... | collective-permute-start | bytes 1572872 | tf_op jit(solution)/shard_map/ppermute | solution.py:41
  62.7 3.4 %collective-permute-start.17 = (bf16[128,2048]{1,0:T(8,128)(2,1)}, bf16[128,2048]{1,0:T(8,128)(2,1)}, u32[]{:S(2)}, u32[]{:S(2)}) collective-permute-start(bf16[128,2048]{1,0:T(8,128)(2,1)} %collective-permute-done.9.refs_3_.refs_19_), channel_id=1, source_target_pairs={{0,1},{1,0},{2,3},{3,2},{4,5},{5,4},{6,7},{7,6},{8,9},{9,8},{10,11... | collective-permute-start | bytes 1572872 | tf_op jit(solution)/shard_map/ppermute | solution.py:41
  66.2 14.1 %collective-permute-start.19 = (bf16[384,128]{1,0:T(8,128)(2,1)}, bf16[384,128]{1,0:T(8,128)(2,1)}, u32[]{:S(2)}, u32[]{:S(2)}) collective-permute-start(bf16[384,128]{1,0:T(8,128)(2,1)} %get-tuple-element.1448.refs_1_.refs_37_), channel_id=1, source_target_pairs={{4,0},{8,12},{5,1},{9,13},{6,2},{10,14},{7,3},{11,15},{20,16},{24,... | collective-permute-start | bytes 294920 | tf_op jit(solution)/shard_map/ppermute | solution.py:58
  67.5 14.3 %collective-permute-start.21 = (bf16[2,128,1024]{2,1,0:T(8,128)(2,1)}, bf16[2,128,1024]{2,1,0:T(8,128)(2,1)}, u32[]{:S(2)}, u32[]{:S(2)}) collective-permute-start(bf16[2,128,1024]{2,1,0:T(8,128)(2,1)} %refs_32_), channel_id=1, source_target_pairs={{0,2},{2,0},{1,3},{3,1},{4,6},{6,4},{5,7},{7,5},{8,10},{10,8},{9,1... | collective-permute-start | bytes 1572872 | tf_op jit(solution)/shard_map/ppermute | solution.py:31
  72.1 19.2 %collective-permute-start.24 = (bf16[224,1024]{1,0:T(8,128)(2,1)}, bf16[224,1024]{1,0:T(8,128)(2,1)}, u32[]{:S(2)}, u32[]{:S(2)}) collective-permute-start(bf16[224,1024]{1,0:T(8,128)(2,1)} %get-tuple-element.1421.refs_10_), channel_id=1, source_target_pairs={{4,0},{8,12},{5,1},{9,13},{6,2},{10,14},{7,3},{11,15},{20,16},{24,... | collective-permute-start | bytes 1376264 | tf_op jit(solution)/shard_map/ppermute | solution.py:58
  81.8 4.1 %collective-permute-start.22 = (bf16[2,128,1024]{2,1,0:T(8,128)(2,1)}, bf16[2,128,1024]{2,1,0:T(8,128)(2,1)}, u32[]{:S(2)}, u32[]{:S(2)}) collective-permute-start(bf16[2,128,1024]{2,1,0:T(8,128)(2,1)} %refs_32_), channel_id=1, source_target_pairs={{0,1},{1,0},{2,3},{3,2},{4,5},{5,4},{6,7},{7,6},{8,9},{9,8},{10,11... | collective-permute-start | bytes 1572872 | tf_op jit(solution)/shard_map/ppermute | solution.py:31
  81.8 4.1 %collective-permute-start.23 = (bf16[2,128,1024]{2,1,0:T(8,128)(2,1)}, bf16[2,128,1024]{2,1,0:T(8,128)(2,1)}, u32[]{:S(2)}, u32[]{:S(2)}) collective-permute-start(bf16[2,128,1024]{2,1,0:T(8,128)(2,1)} %collective-permute-done.21.refs_34_), channel_id=1, source_target_pairs={{0,1},{1,0},{2,3},{3,2},{4,5},{5,4},{6,7},{7,6},{8,9},{9,8},{10,11... | collective-permute-start | bytes 1572872 | tf_op jit(solution)/shard_map/ppermute | solution.py:31
  86.0 16.7 %collective-permute-start.25 = (bf16[160,1024]{1,0:T(8,128)(2,1)}, bf16[160,1024]{1,0:T(8,128)(2,1)}, u32[]{:S(2)}, u32[]{:S(2)}) collective-permute-start(bf16[160,1024]{1,0:T(8,128)(2,1)} %get-tuple-element.1422.refs_11_), channel_id=1, source_target_pairs={{4,0},{8,12},{5,1},{9,13},{6,2},{10,14},{7,3},{11,15},{20,16},{24,... | collective-permute-start | bytes 983048 | tf_op jit(solution)/shard_map/ppermute | solution.py:58
  (8 other events, 33.4 us)

commit v4 on v3

--- a/solution.py
+++ b/solution.py
@@ -14,7 +14,6 @@
 
 PAIRS = [(0, 1), (1, 0), (2, 3), (3, 2)]
 OUTWARD = [(1, 0), (2, 3)]
-INWARD = [(0, 1), (3, 2)]
 
 
 def lookup(indices, table):
@@ -119,7 +118,7 @@
         self.columns = weight.shape[1]
         self.deep = self.width // 8
         self.rows = self.deep // 2
-        self.cut = self.tall * 7 // 12
+        self.cut = self.tall - self.rows
         self.sizes = [self.cut, self.tall - self.cut]
 
     def sides(self, ref):
@@ -175,28 +174,95 @@
     )
 
 
-def cut_up(held, tokens, layout):
-    tall, width, rows, cut = layout.tall, layout.width, layout.rows, layout.cut
-    cuts = [(rows, tall - rows), (0, cut), (cut, tall - cut)]
-
-    def body(t_ref, *refs):
-        *into_refs, all_ref, sem = refs
-        run_copies([pltpu.make_async_copy(t_ref, all_ref, sem.at[0])])
-        run_copies(
-            [
-                pltpu.make_async_copy(all_ref.at[pl.ds(at, size)], into, sem.at[i])
-                for i, ((at, size), into) in enumerate(zip(cuts, into_refs))
-            ]
-        )
-
-    return call(
-        held,
-        body,
-        [array(size, width) for _, size in cuts],
+def later_rows(held, tokens, layout):
+    rows, cut = layout.rows, layout.cut
+
+    def body(t_ref, out_ref, sem):
+        start = pl.multiple_of(jnp.where(Place().end, 0, rows), rows)
+        run_copies([pltpu.make_async_copy(t_ref.at[pl.ds(start, cut)], out_ref, sem)])
+
+    return call(
+        held,
+        body,
+        array(cut, layout.width),
         [tokens],
         [ANY],
-        [ANY] * len(cuts),
-        [pltpu.VMEM((tall, width), tokens.dtype), pltpu.SemaphoreType.DMA((3,))],
+        scratch=[pltpu.SemaphoreType.DMA],
+    )
+
+
+TALL = 32
+
+
+def last_rows(held, tokens, across, coords, layout):
+    cut, last = layout.sizes
+    size, wide = last + TALL, coords.shape[1]
+    count = layout.tall // TALL
+
+    def body(t_ref, a_ref, c_ref, out_ref, rest_ref, sem):
+        place = Place()
+        rest = started(
+            pltpu.make_async_copy(
+                a_ref.at[pl.ds(size, layout.tall - size)], rest_ref, sem.at[0]
+            )
+        )
+
+        @pl.when(place.end)
+        def _():
+            copy = pltpu.make_async_copy(
+                t_ref.at[pl.ds(cut, last)], out_ref.at[pl.ds(0, last)], sem.at[1]
+            )
+            copy.start()
+            for i in range(layout.width // wide):
+                some = jnp.zeros((TALL, wide), out_ref.dtype)
+                if i < count:
+                    some = c_ref[i * TALL : (i + 1) * TALL, :].astype(out_ref.dtype)
+                out_ref[last:, i * wide : (i + 1) * wide] = some
+            copy.wait()
+
+        @pl.when(jnp.logical_not(place.end))
+        def _():
+            run_copies(
+                [pltpu.make_async_copy(a_ref.at[pl.ds(0, size)], out_ref, sem.at[1])]
+            )
+
+        waited(rest)
+
+    return call(
+        held,
+        body,
+        [array(size, layout.width), array(layout.tall - size, layout.width)],
+        [tokens, across, coords],
+        [ANY, ANY, VMEM],
+        scratch=[pltpu.SemaphoreType.DMA((2,))],
+    )
+
+
+def unpacked(held, coords, x, layout):
+    last, wide = layout.sizes[1], coords.shape[1]
+
+    def body(c_ref, x_ref, out_ref, rows_ref, below_ref, sem):
+        copies = started(
+            pltpu.make_async_copy(x_ref.at[pl.ds(last, TALL)], below_ref, sem.at[0]),
+            pltpu.make_async_copy(x_ref.at[pl.ds(0, last)], rows_ref, sem.at[1]),
+        )
+        copies[0].wait()
+        for i in range(layout.tall // TALL):
+            some = pl.ds(i * TALL, TALL)
+            other = below_ref[:, i * wide : (i + 1) * wide].astype(jnp.float32)
+            out_ref[some, :] = (c_ref[some, :] + other).astype(out_ref.dtype)
+        copies[1].wait()
+
+    return call(
+        held,
+        body,
+        [array(*coords.shape), array(last, layout.width)],
+        [coords, x],
+        [VMEM, ANY],
+        scratch=[
+            pltpu.VMEM((TALL, layout.width), jnp.bfloat16),
+            pltpu.SemaphoreType.DMA((2,)),
+        ],
     )
 
 
@@ -204,7 +270,7 @@
 
 
 class Rows:
-    def __init__(self, x_ref, start, held_ref, sem):
+    def __init__(self, x_ref, start, held_ref, sem, begin=True):
         self.depth, self.held_ref, self.copies = held_ref.shape[0] // PARTS, held_ref, []
         for i in range(PARTS):
             some = pl.ds(pl.multiple_of(start + i * self.depth, 128), self.depth)
@@ -213,8 +279,8 @@
                     x_ref.at[some], held_ref.at[pl.ds(i * self.depth, self.depth)], sem.at[i]
                 )
             )
-        for copy in self.copies:
-            copy.start()
+        if begin:
+            started(*self.copies)
 
     def dot(self, a_ref):
         total = 0.0
@@ -252,7 +318,7 @@
 def sums_room(layout):
     return [
         pltpu.VMEM((layout.tall, layout.columns), jnp.float32),
-        pltpu.SemaphoreType.DMA((9,)),
+        pltpu.SemaphoreType.DMA((10,)),
     ]
 
 
@@ -280,7 +346,7 @@
 
 def add_block(held, total, at_end, inside, weight, layout):
     width, tall = layout.width, layout.tall
-    arrays = [x for side in (at_end, inside) if side for x in side[1]]
+    arrays = [*at_end[1], *inside[1]]
 
     def body(total_ref, w_ref, *refs):
         array_refs = list(refs[: len(arrays)])
@@ -303,24 +369,22 @@
             run_copies([pltpu.make_async_copy(sum_ref, out_ref, sem.at[4])])
 
         for side, here in ((at_end, place.end), (inside, jnp.logical_not(place.end))):
-            if side:
-                mine = [array_refs.pop(0) for _ in side[1]]
-                pl.when(here)(lambda side=side, mine=mine: run(side[0], mine))
+            mine = [array_refs.pop(0) for _ in side[1]]
+            pl.when(here)(lambda side=side, mine=mine: run(side[0], mine))
 
     return call(
         held,
         body,
         sums(layout),
         [total, weight, *arrays],
-        [ANY, HBM] + [ANY] * len(arrays),
-        [ANY],
+        [HBM, HBM] + [ANY] * len(arrays),
+        [HBM],
         room(1, layout) + [pltpu.VMEM((tall, width), jnp.bfloat16)] + sums_room(layout),
         room=LARGE,
-        alias={0: 0},
-    )
-
-
-def add_last(held, total, low, use, ups, relayed, beyond, term, weight, layout):
+    )
+
+
+def add_last(held, total, low, use, ups, relayed, beyond, inner, weight, layout):
     adapters, rank, columns = ups[0].shape
     count = len(ups)
     cut, last = layout.sizes
@@ -328,14 +392,26 @@
 
     def body(hop_ref, low_ref, use_ref, *refs):
         up_refs = refs[:count]
-        total_ref, relayed_ref, b0_ref, b1_ref, term_ref, w_ref = refs[count : count + 6]
-        out_ref, late_ref, *scratch = refs[count + 6 :]
-        w_held, w_sem, a_held, t_held, u_held, first_ref, sum_ref, sem = scratch
+        total_ref, n0_ref, n1_ref, b0_ref, b1_ref, p0_ref, p1_ref, w_ref = refs[
+            count : count + 8
+        ]
+        out_ref, sums_ref, *scratch = refs[count + 8 :]
+        w_held, w_sem, v_held, v_sem, a_held, p_held, u_held, rows_ref, sum_ref, sem = scratch
         place = Place()
-        at_end = [pltpu.make_async_copy(relayed_ref, a_held, sem.at[0])]
+        first = n0_ref.shape[0]
+        at_end = [
+            pltpu.make_async_copy(n0_ref, a_held.at[pl.ds(0, first)], sem.at[0]),
+            pltpu.make_async_copy(n1_ref, a_held.at[pl.ds(first, tall - first)], sem.at[1]),
+        ]
         inside = [
             pltpu.make_async_copy(b0_ref, a_held.at[pl.ds(0, cut)], sem.at[0]),
             pltpu.make_async_copy(b1_ref, a_held.at[pl.ds(cut, last)], sem.at[1]),
+        ]
+        second = [
+            pltpu.make_async_copy(p0_ref, p_held.at[pl.ds(0, cut)], sem.at[8]),
+            pltpu.make_async_copy(
+                p1_ref.at[pl.ds(0, last)], p_held.at[pl.ds(cut, last)], sem.at[9]
+            ),
         ]
 
         loads = started(
@@ -359,7 +435,12 @@
             started(*inside)
 
         w = Rows(w_ref, jnp.where(place.end, place.near, place.far) * width, w_held, w_sem)
-        more = started(pltpu.make_async_copy(term_ref, t_held, sem.at[7]))
+        v = Rows(w_ref, place.partner * width, v_held, v_sem, begin=False)
+
+        @pl.when(jnp.logical_not(place.end))
+        def _():
+            started(*second, *v.copies)
+
         low = jnp.where(place.end, hop_ref[...], low_ref[...])
         some = [
             jnp.where(use_ref[...] == (place.mine ^ turn) * adapters + j, low, 0)
@@ -380,30 +461,31 @@
             waited(inside)
 
         sum_ref[...] += w.dot(a_held)
-        waited(more)
-        late = started(
-            pltpu.make_async_copy(sum_ref.at[pl.ds(cut, last)], late_ref, sem.at[0])
-        )
-        first_ref[...] = (sum_ref[:cut, :] + t_held[...].astype(jnp.float32)).astype(
-            first_ref.dtype
-        )
-        run_copies([pltpu.make_async_copy(first_ref, out_ref.at[pl.ds(0, cut)], sem.at[1])])
-        waited(late)
-
-    return call(
-        held,
-        body,
-        [array(tall, columns), array(last, columns, dtype=jnp.float32)],
+
+        @pl.when(place.end)
+        def _():
+            run_copies([pltpu.make_async_copy(sum_ref, sums_ref, sem.at[7])])
+
+        @pl.when(jnp.logical_not(place.end))
+        def _():
+            waited(second)
+            rows_ref[...] = (sum_ref[...] + v.dot(p_held)).astype(rows_ref.dtype)
+            run_copies([pltpu.make_async_copy(rows_ref, out_ref, sem.at[7])])
+
+    return call(
+        held,
+        body,
+        [array(tall, columns), sums(layout)],
         [*low, use, *[u.reshape(-1, columns) for u in ups]]
-        + [total, relayed, *beyond, term, weight],
-        [VMEM] * 3 + [ANY] * (count + 5) + [HBM],
+        + [total, *relayed, *beyond, *inner, weight],
+        [VMEM] * 3 + [ANY] * count + [HBM] + [ANY] * 6 + [HBM],
         [ANY, ANY],
-        room(1, layout)
+        room(2, layout)
         + [
             pltpu.VMEM((tall, width), jnp.bfloat16),
-            pltpu.VMEM((cut, columns), jnp.bfloat16),
+            pltpu.VMEM((tall, width), jnp.bfloat16),
             pltpu.VMEM((count * adapters * rank, columns), jnp.bfloat16),
-            pltpu.VMEM((cut, columns), jnp.bfloat16),
+            pltpu.VMEM((tall, columns), jnp.bfloat16),
         ]
         + sums_room(layout),
         room=LARGE,
@@ -457,29 +539,45 @@
     )
 
 
-def finished(held, out, late, term, layout):
-    kept = [held[n] for n in sorted(held) if n != "tick"]
-    cut, last = layout.sizes
-
-    def body(out_ref, late_ref, term_ref, *refs):
-        into_ref, sum_ref, sem = refs[len(kept) :]
-        sum_ref[...] = (late_ref[...] + term_ref[...].astype(jnp.float32)).astype(
-            sum_ref.dtype
-        )
-        run_copies([pltpu.make_async_copy(sum_ref, into_ref.at[pl.ds(cut, last)], sem)])
-
-    return pl.pallas_call(
-        body,
-        out_shape=array(*out.shape),
-        in_specs=[ANY, VMEM, VMEM] + [ANY] * len(kept),
-        out_specs=ANY,
-        scratch_shapes=[
-            pltpu.VMEM((last, layout.columns), out.dtype),
-            pltpu.SemaphoreType.DMA,
+NOT_KEPT = ("tick", "tokens", "down", "up", "use")
+
+
+def finished(held, out, total, term, i, layout, keep=False):
+    start, size = i * layout.cut, layout.sizes[i]
+    kept = [held[n] for n in sorted(held) if keep and n not in NOT_KEPT]
+
+    def body(out_ref, total_ref, term_ref, *refs):
+        into_ref, sum_ref, term_held, rows_ref, sem = refs[-5:]
+
+        @pl.when(Place().end)
+        def _():
+            loads = started(
+                pltpu.make_async_copy(total_ref.at[pl.ds(start, size)], sum_ref, sem.at[0]),
+                pltpu.make_async_copy(term_ref, term_held, sem.at[1]),
+            )
+            waited(loads)
+            rows_ref[...] = (sum_ref[...] + term_held[...].astype(jnp.float32)).astype(
+                rows_ref.dtype
+            )
+            run_copies(
+                [pltpu.make_async_copy(rows_ref, into_ref.at[pl.ds(start, size)], sem.at[2])]
+            )
+
+    return call(
+        held,
+        body,
+        array(layout.tall, layout.columns),
+        [out, total, term, *kept],
+        [ANY] * (3 + len(kept)),
+        [ANY],
+        [
+            pltpu.VMEM((size, layout.columns), jnp.float32),
+            pltpu.VMEM((size, layout.columns), jnp.bfloat16),
+            pltpu.VMEM((size, layout.columns), jnp.bfloat16),
+            pltpu.SemaphoreType.DMA((3,)),
         ],
-        input_output_aliases={0: 0},
-        compiler_params=pltpu.CompilerParams(vmem_limit_bytes=16 << 20),
-    )(out, late, term, *kept)
+        alias={0: 0},
+    )
 
 
 def coords_of(held, tokens, use, downs, turns, before=None):
@@ -529,85 +627,86 @@
     across = hop_middle(tokens)
     h = dict(tick=jnp.zeros((8, 128), jnp.float32), down=down, up=up, tokens=tokens)
     h["ids"], h["slots"], h["blocks"] = tables
-    fence(h)
-    down_x, down_c = swap(h["down"], "pool"), swap(h["down"], "inner")
-    h["first"] = first_rows(h, h["tokens"], weight, layout)
+    h["first"] = first_rows(h, tokens, weight, layout)
     fence(h)
     first_p = hop(h["first"], PAIRS)
-    h["rest"], h["part0"], h["part1"] = cut_up(h, h["tokens"], layout)
+    fence(h)
+    down_c = swap(h["down"], "inner")
+    fence(h)
+    down_x = swap(h["down"], "pool")
+    fence(h)
+    h["later"] = later_rows(h, h["tokens"], layout)
+    h["down_c"] = down_c
+    fence(h)
+    later_p = hop(h["later"], PAIRS)
+    fence(h)
     slot, rank = slot_and_rank(h.pop("ids"), h.pop("slots"), h.pop("blocks"))
     row = jnp.arange(MAXIMUM_RANK, dtype=jnp.int32)[None, :]
     h["use"] = jnp.where(row < rank[:, None], slot[:, None], -1)
-    h["down_c"] = down_c
-    fence(h)
-    inner0 = hop(h["part0"], INWARD)
-    fence(h)
-    rest_o = hop(h["rest"], OUTWARD)
     total = own_block(h, h["tokens"], weight, layout)
     h["lent"] = first_p
     fence(h)
     lent_y = swap_inside(h["lent"], "groups")
+    fence(h)
+    coords, _ = coords_of(h, h["tokens"], h["use"], [h["down"], h["down_c"]], [0, 1])
     h["down_x"] = down_x
     fence(h)
+    lent_x = swap_inside(h["lent"], "pool")
+    fence(h)
     down_xc = swap(h["down_x"], "inner")
-    downs = [h["down"], h["down_c"], h["down_x"]]
-    coords, _ = coords_of(h, h["tokens"], h["use"], downs, [0, 1, 2])
+    fence(h)
+    coords, _ = coords_of(h, h["tokens"], h["use"], [h["down_x"]], [2], coords)
     h["down_xc"] = down_xc
     fence(h)
-    lent_x = swap_inside(h["lent"], "pool")
-    fence(h)
-    coords, h["coords"] = coords_of(h, h["tokens"], h["use"], [h["down_xc"]], [3], coords)
-    h["lent_y"] = lent_y
-    fence(h)
-    coords_p = hop(h["coords"], INWARD)
+    coords, _ = coords_of(h, h["tokens"], h["use"], [h["down_xc"]], [3], coords)
     h["across"] = across
     fence(h)
-    relayed = hop(h["across"], OUTWARD)
-    h["inner0"] = inner0
-    fence(h)
-    beyond0 = hop_middle(h["inner0"])
-    h["rest_o"], h["coords_p"] = rest_o, coords_p
-    fence(h)
-    inner1 = hop(h["part1"], INWARD)
+    h["last"], h["others"] = last_rows(h, h["tokens"], h["across"], coords, layout)
+    h["later_p"], h["lent_y"] = later_p, lent_y
+    fence(h)
+    last_p = hop(h["last"], PAIRS)
+    fence(h)
+    beyond0 = hop_middle(h["later_p"])
     h["lent_x"] = lent_x
     fence(h)
     lent_d = swap_inside(h["lent_x"], "groups")
     fence(h)
-    h["pair"] = added(h, coords, h["coords_p"])
+    lent_c = swap_inside(h["lent"], "inner")
+    fence(h)
+    lent_yc = swap_inside(h["lent_y"], "inner")
+    fence(h)
+    at_end = ("partner", [h["lent"], h["later_p"]])
+    total = add_block(h, total, at_end, ("near", [h["across"]]), weight, layout)
+    h["lent_c"], h["lent_yc"] = lent_c, lent_yc
+    fence(h)
+    others_o = hop(h["others"], OUTWARD)
+    fence(h)
+    lent_xc = swap_inside(h["lent_x"], "inner")
+    h["lent_xc"], h["lent_d"] = lent_xc, lent_d
+    fence(h)
+    lent_dc = swap_inside(h["lent_d"], "inner")
+    h["lent_dc"], h["last_p"] = lent_dc, last_p
+    fence(h)
+    h["pair"], h["last_in"] = unpacked(h, coords, h["last_p"], layout)
     fence(h)
     pair_m = hop_middle(h["pair"])
     fence(h)
-    at_end = ("partner", [h["lent"], h["rest_o"]])
-    total = add_block(h, total, at_end, ("near", [h["across"]]), weight, layout)
-    h["lent_d"] = lent_d
-    fence(h)
-    lent_c = swap_inside(h["lent"], "inner")
-    h["lent_c"] = lent_c
-    fence(h)
-    lent_yc = swap_inside(h["lent_y"], "inner")
-    h["lent_yc"], h["beyond0"], h["inner1"] = lent_yc, beyond0, inner1
-    fence(h)
-    beyond1 = hop_middle(h["inner1"])
-    fence(h)
-    lent_xc, lent_dc = swap_inside(h["lent_x"], "inner"), swap_inside(h["lent_d"], "inner")
-    h["pair_m"] = pair_m
-    fence(h)
-    h["whole"] = added(h, h["pair"], h["pair_m"])
-    h["lent_xc"], h["lent_dc"] = lent_xc, lent_dc
-    fence(h)
-    low_o = hop(h["whole"], OUTWARD)
+    beyond1 = hop_middle(h["last_in"])
     fence(h)
     up_x = swap(h["up"], "pool")
+    h["beyond0"] = beyond0
     fence(h)
     names = ("lent", "lent_c", "lent_x", "lent_xc", "lent_y", "lent_yc", "lent_d", "lent_dc")
     pieces = [h[n] for n in names]
     h["help0"] = helped(h, h["beyond0"], pieces, layout, 0)
+    h["pair_m"] = pair_m
+    fence(h)
+    h["whole"] = added(h, h["pair"], h["pair_m"])
+    fence(h)
+    low_o = hop(h["whole"], OUTWARD)
     fence(h)
     help_o0 = hop(h["help0"], OUTWARD)
-    fence(h)
-    halves = [h["inner0"], h["inner1"]]
-    total = add_block(h, total, None, ("partner", halves), weight, layout)
-    h["relayed"], h["beyond1"], h["up_x"], h["low_o"] = relayed, beyond1, up_x, low_o
+    h["beyond1"], h["others_o"], h["up_x"] = beyond1, others_o, up_x
     fence(h)
     up_xc, up_c = swap(h["up_x"], "inner"), swap(h["up"], "inner")
     fence(h)
@@ -616,23 +715,28 @@
     h["up_xc"], h["up_c"] = up_xc, up_c
     fence(h)
     help_o1 = hop(h["help1"], OUTWARD)
-    h["help_o0"] = help_o0
-    fence(h)
-    out, late = add_last(
+    h["low_o"] = low_o
+    fence(h)
+    out, total = add_last(
         h,
         total,
         [h["low_o"], h["whole"]],
         h["use"],
         [h["up"], h["up_c"], h["up_x"], h["up_xc"]],
-        h["relayed"],
+        [h["last_p"], h["others_o"]],
         [h["beyond0"], h["beyond1"]],
-        h["help_o0"],
+        [h["later_p"], h["last_p"]],
         weight,
         layout,
     )
+    fence(h)
+    h["help_o0"] = help_o0
+    fence(h)
+    out = finished(h, out, total, h["help_o0"], 0, layout)
+    fence(h)
     h["help_o1"] = help_o1
     fence(h)
-    return finished(h, out, late, h.pop("help_o1"), layout)
+    return finished(h, out, total, h.pop("help_o1"), 1, layout, keep=True)
 
 
 def owner_mask(slot, rank, adapters):

time: 105 us -> 101 us (0.962)
  starting transfers between devices: 31.3 us -> 16.7 us
  local copies, waits for them, and re-layouts: 1.79 us -> 5.7 us
  waiting for transfers between devices: 28.9 us -> 32.2 us
  Pallas kernels: 41.9 us -> 45.1 us
    ppermute x9 -> x7, starting transfers between devices: 24.7 us -> 10.3 us  [hop(): return lax.ppermute(x, 'tensor', pairs)]
    pallas_call x42 -> x53, Pallas kernels: 40.1 us -> 45.1 us  [call(): pl.pallas_call(counted, out_shape=[*shapes, jax.ShapeDtypeStruct(tick.sha...]
    unnamed x12 -> x26, local copies, waits for them, and re-layouts: 1.79 us -> 5.7 us
    ppermute x6, waiting for transfers between devices: 6.86 us -> 10.3 us  [swap(): return lax.ppermute(x, axis, [(0, 1), (1, 0)])]
    pallas_call x1 -> x0, Pallas kernels: 1.78 us -> none  [finished(): pl.pallas_call(body, out_shape=array(*out.shape), in_specs=[ANY, VMEM, VM...]
    ppermute x11, waiting for transfers between devices: 3.98 us -> 2.19 us  [inside(): return lax.ppermute(x, AXES, pairs)]
    ppermute x9 -> x7, waiting for transfers between devices: 18 us -> 19.7 us  [hop(): return lax.ppermute(x, 'tensor', pairs)]
  transfers between devices with their start and end apart: 26 -> 24, of which waited for: 12 -> 9; matrix products, arithmetic and copies ran while one was open for 0% -> 0% of each run, Pallas kernels for 38% -> 43%
where the time goes in v4:
time: 101 us
  Pallas kernels  45.1 us (45%)
  waiting for transfers between devices  32.2 us (32%)
  starting transfers between devices  16.7 us (17%)
  local copies, waits for them, and re-layouts  5.7 us (6%)
    pallas_call x53, Pallas kernels, call(): pl.pallas_call(counted, out_shape=[*shapes, jax.ShapeDtypeStruct(tick.sha...  45.1 us
    ppermute x7, waiting for transfers between devices, hop(): return lax.ppermute(x, 'tensor', pairs)  19.7 us
    ppermute x7, starting transfers between devices, hop(): return lax.ppermute(x, 'tensor', pairs)  10.3 us
    ppermute x6, waiting for transfers between devices, swap(): return lax.ppermute(x, axis, [(0, 1), (1, 0)])  10.3 us
    unnamed x26, local copies, waits for them, and re-layouts  5.7 us
    ppermute x6, starting transfers between devices, swap(): return lax.ppermute(x, axis, [(0, 1), (1, 0)])  4.05 us
    ppermute x11, starting transfers between devices, inside(): return lax.ppermute(x, AXES, pairs)  2.31 us
    ppermute x11, waiting for transfers between devices, inside(): return lax.ppermute(x, AXES, pairs)  2.19 us
  transfers between devices with their start and end apart: 24, of which 9 were waited for; matrix products, arithmetic and copies ran while one was open for 0% of the time, Pallas kernels for 43%

profile of v4, /device:TPU:0, one launch (start us, length us, event | category | flops | bytes accessed | tf_op | source)
XLA Modules:
  0.0 100.5 jit_solution(15746959175660701247)
XLA Ops:
  1.9 1.8 %shard_map.73 = (bf16[128,2048]{1,0:T(8,128)(2,1)}, f32[8,128]{1,0:T(8,128)S(1)}) custom-call(bf16[384,2048]{1,0:T(8,128)(2,1)S(1)} %copy-done.3, bf16[8192,1024]{1,0:T(8,128)(2,1)} %refs_14_.1, f32[8,128]{1,0:T(8,128)S(1)} %broadcast_in_dim.34.refs_2_), custom_call_target="tpu_custom_call" | custom-call | flops 999999995904 | tf_op jit(solution)/shard_map/pallas_call | solution.py:77
  3.7 3.3 %collective-permute-start.2 = (bf16[128,2048]{1,0:T(8,128)(2,1)}, bf16[128,2048]{1,0:T(8,128)(2,1)}, u32[]{:S(2)}, u32[]{:S(2)}) collective-permute-start(bf16[128,2048]{1,0:T(8,128)(2,1)} %get-tuple-element.1515.refs_9_), channel_id=1, source_target_pairs={{0,4},{4,0},{8,12},{12,8},{1,5},{5,1},{9,13},{13,9},{2,6},{6,2},{1... | collective-permute-start | bytes 1572872 | tf_op jit(solution)/shard_map/ppermute | solution.py:57
  7.0 1.6 %collective-permute-start.3 = (bf16[2,128,2048]{2,1,0:T(8,128)(2,1)}, bf16[2,128,2048]{2,1,0:T(8,128)(2,1)}, u32[]{:S(2)}, u32[]{:S(2)}) collective-permute-start(bf16[2,128,2048]{2,1,0:T(8,128)(2,1)} %param.12), channel_id=1, source_target_pairs={{0,2},{2,0},{1,3},{3,1},{4,6},{6,4},{5,7},{7,5},{8,10},{10,8},{9,1... | collective-permute-start | bytes 3145736 | tf_op jit(solution)/shard_map/ppermute | solution.py:30
  10.1 3.8 %shard_map.81 = (f32[384,1024]{1,0:T(8,128)S(1)}, f32[8,128]{1,0:T(8,128)S(1)}) custom-call(bf16[384,2048]{1,0:T(8,128)(2,1)S(1)} %copy-done.3, bf16[8192,1024]{1,0:T(8,128)(2,1)} %refs_14_.1, f32[8,128]{1,0:T(8,128)S(1)} %shard_map.80.refs_2_), custom_call_target="tpu_custom_call" | custom-call | flops 999999995904 | tf_op jit(solution)/shard_map/pallas_call | solution.py:77
  15.3 4.8 %collective-permute-done.2.refs_2_.refs_1_.refs_18_ = bf16[128,2048]{1,0:T(8,128)(2,1)} collective-permute-done((bf16[128,2048]{1,0:T(8,128)(2,1)}, bf16[128,2048]{1,0:T(8,128)(2,1)}, u32[]{:S(2)}, u32[]{:S(2)}) %collective-permute-start.2) | collective-permute-done | bytes 524320 | tf_op jit(solution)/shard_map/ppermute | solution.py:57
  20.1 3.2 %shard_map.84 = (f32[384,128]{1,0:T(8,128)S(1)}, bf16[384,128]{1,0:T(8,128)(2,1)}, f32[8,128]{1,0:T(8,128)S(1)}) custom-call(s32[384,128]{1,0:T(8,128)S(1)} %fusion.refs_0_.refs_2_, bf16[384,2048]{1,0:T(8,128)(2,1)S(1)} %copy-done.3, bf16[256,2048]{1,0:T(8,128)(2,1)} %bitcast.refs_2_, bf16[256,2048]{1,0:T(8,128)(2,1)} %bitcast.1.refs_3_, ...), custom_call_target="tpu_custom_call" | custom-call | flops 999999995904 | tf_op jit(solution)/shard_map/pallas_call | solution.py:77
  23.3 9.6 %collective-permute-done.3.refs_7_ = bf16[2,128,2048]{2,1,0:T(8,128)(2,1)} collective-permute-done((bf16[2,128,2048]{2,1,0:T(8,128)(2,1)}, bf16[2,128,2048]{2,1,0:T(8,128)(2,1)}, u32[]{:S(2)}, u32[]{:S(2)}) %collective-permute-start.3) | collective-permute-done | bytes 1048608 | tf_op jit(solution)/shard_map/ppermute | solution.py:30
  33.8 2.5 %shard_map.88 = (f32[384,128]{1,0:T(8,128)S(1)}, bf16[384,128]{1,0:T(8,128)(2,1)}, f32[8,128]{1,0:T(8,128)S(1)}) custom-call(s32[384,128]{1,0:T(8,128)S(1)} %copy-done.1, bf16[384,2048]{1,0:T(8,128)(2,1)S(1)} %copy-done.3, bf16[256,2048]{1,0:T(8,128)(2,1)} %bitcast.2.refs_2_, f32[384,128]{1,0:T(8,128)S(1)} %get-tuple-element.878.refs_3_, ...), custom_call_target="tpu_custom_call" | custom-call | flops 999999995904 | tf_op jit(solution)/shard_map/pallas_call | solution.py:77
  36.6 2.5 %shard_map.90 = (f32[384,128]{1,0:T(8,128)S(1)}, bf16[384,128]{1,0:T(8,128)(2,1)}, f32[8,128]{1,0:T(8,128)S(1)}) custom-call(s32[384,128]{1,0:T(8,128)S(1)} %copy-done.1, bf16[384,2048]{1,0:T(8,128)(2,1)S(1)} %copy-done.3, bf16[256,2048]{1,0:T(8,128)(2,1)} %bitcast.3.refs_2_, f32[384,128]{1,0:T(8,128)S(1)} %get-tuple-element.891.refs_3_, ...), custom_call_target="tpu_custom_call" | custom-call | flops 999999995904 | tf_op jit(solution)/shard_map/pallas_call | solution.py:77
  39.8 2.4 %shard_map.92 = (bf16[160,2048]{1,0:T(8,128)(2,1)}, bf16[224,2048]{1,0:T(8,128)(2,1)}, f32[8,128]{1,0:T(8,128)S(1)}) custom-call(bf16[384,2048]{1,0:T(8,128)(2,1)S(1)} %copy-done.3, bf16[384,2048]{1,0:T(8,128)(2,1)} %collective-permute-done.refs_1_.refs_4_.refs_3_, f32[384,128]{1,0:T(8,128)S(1)} %get-tuple-element.902.refs_2_.refs_0_, ...), custom_call_target="tpu_custom_call" | custom-call | flops 999999995904 | tf_op jit(solution)/shard_map/pallas_call | solution.py:77
  42.2 1.5 %collective-permute-start.12 = (bf16[160,2048]{1,0:T(8,128)(2,1)}, bf16[160,2048]{1,0:T(8,128)(2,1)}, u32[]{:S(2)}, u32[]{:S(2)}) collective-permute-start(bf16[160,2048]{1,0:T(8,128)(2,1)} %get-tuple-element.1519.refs_13_), channel_id=1, source_target_pairs={{0,4},{4,0},{8,12},{12,8},{1,5},{5,1},{9,13},{13,9},{2,6},{6,2},{1... | collective-permute-start | bytes 1966088 | tf_op jit(solution)/shard_map/ppermute | solution.py:57
  44.7 4.7 %shard_map.99 = (f32[384,1024]{1,0:T(8,128)S(1)}, f32[8,128]{1,0:T(8,128)S(1)}) custom-call(f32[384,1024]{1,0:T(8,128)} %copy-done.7, bf16[8192,1024]{1,0:T(8,128)(2,1)} %refs_14_.1, bf16[128,2048]{1,0:T(8,128)(2,1)} %collective-permute-done.2.refs_2_.refs_1_.refs_18_, bf16[256,2048]{1,0:T(8,128)(2,1)} %collective-permute-done.5.refs_3_.refs_12_.refs_17_, ...), custom_call_target="tpu_custom_call" | custom-call | flops 999999995904 | tf_op jit(solution)/shard_map/pallas_call | solution.py:77
  52.1 2.2 %collective-permute-done.11.refs_4_.refs_23_ = bf16[128,2048]{1,0:T(8,128)(2,1)} collective-permute-done((bf16[128,2048]{1,0:T(8,128)(2,1)}, bf16[128,2048]{1,0:T(8,128)(2,1)}, u32[]{:S(2)}, u32[]{:S(2)}) %collective-permute-start.11) | collective-permute-done | bytes 524320 | tf_op jit(solution)/shard_map/ppermute | solution.py:40
  54.4 5.8 %collective-permute-done.12.refs_1_.refs_8_.refs_13_.refs_15_ = bf16[160,2048]{1,0:T(8,128)(2,1)} collective-permute-done((bf16[160,2048]{1,0:T(8,128)(2,1)}, bf16[160,2048]{1,0:T(8,128)(2,1)}, u32[]{:S(2)}, u32[]{:S(2)}) %collective-permute-start.12) | collective-permute-done | bytes 655392 | tf_op jit(solution)/shard_map/ppermute | solution.py:57
  60.1 2.0 %shard_map.104 = (bf16[384,128]{1,0:T(8,128)(2,1)}, bf16[128,2048]{1,0:T(8,128)(2,1)}, f32[8,128]{1,0:T(8,128)S(1)}) custom-call(f32[384,128]{1,0:T(8,128)S(1)} %copy-done.9, bf16[160,2048]{1,0:T(8,128)(2,1)} %collective-permute-done.12.refs_1_.refs_8_.refs_13_.refs_15_, f32[8,128]{1,0:T(8,128)S(1)} %shard_map.103.refs_2_), custom_call_target="tpu_custom_call" | custom-call | flops 999999995904 | tf_op jit(solution)/shard_map/pallas_call | solution.py:77
  64.2 4.2 %shard_map.109 = (bf16[256,1024]{1,0:T(8,128)(2,1)}, f32[8,128]{1,0:T(8,128)S(1)}) custom-call(bf16[256,2048]{1,0:T(8,128)(2,1)} %collective-permute-done.14.refs_0_.refs_10_.refs_4_, bf16[128,2048]{1,0:T(8,128)(2,1)} %collective-permute-done.2.refs_2_.refs_1_.refs_18_, bf16[128,2048]{1,0:T(8,128)(2,1)} %collective-permute-done.8.refs_2_.refs_19_, ...), custom_call_target="tpu_custom_call" | custom-call | flops 999999995904 | tf_op jit(solution)/shard_map/pallas_call | solution.py:77
  68.5 1.6 %shard_map.111 = (bf16[384,128]{1,0:T(8,128)(2,1)}, f32[8,128]{1,0:T(8,128)S(1)}) custom-call(bf16[384,128]{1,0:T(8,128)(2,1)} %get-tuple-element.1535.refs_0_.refs_29_, bf16[384,128]{1,0:T(8,128)(2,1)} %collective-permute-done.15.refs_1_.refs_30_, f32[8,128]{1,0:T(8,128)S(1)} %shard_map.110.refs_2_), custom_call_target="tpu_custom_call" | custom-call | flops 999999995904 | tf_op jit(solution)/shard_map/pallas_call | solution.py:77
  72.7 7.1 %collective-permute-done.17.refs_9_.refs_28_ = bf16[224,2048]{1,0:T(8,128)(2,1)} collective-permute-done((bf16[224,2048]{1,0:T(8,128)(2,1)}, bf16[224,2048]{1,0:T(8,128)(2,1)}, u32[]{:S(2)}, u32[]{:S(2)}) %collective-permute-start.17) | collective-permute-done | bytes 917536 | tf_op jit(solution)/shard_map/ppermute | solution.py:57
  80.3 3.5 %shard_map.116 = (bf16[128,1024]{1,0:T(8,128)(2,1)}, f32[8,128]{1,0:T(8,128)S(1)}) custom-call(bf16[128,2048]{1,0:T(8,128)(2,1)} %collective-permute-done.16.refs_0_.refs_11_.refs_5_, bf16[128,2048]{1,0:T(8,128)(2,1)} %collective-permute-done.2.refs_2_.refs_1_.refs_18_, bf16[128,2048]{1,0:T(8,128)(2,1)} %collective-permute-done.8.refs_2_.refs_19_, ...), custom_call_target="tpu_custom_call" | custom-call | flops 999999995904 | tf_op jit(solution)/shard_map/pallas_call | solution.py:77
  83.8 1.6 %collective-permute-start.23 = (bf16[128,1024]{1,0:T(8,128)(2,1)}, bf16[128,1024]{1,0:T(8,128)(2,1)}, u32[]{:S(2)}, u32[]{:S(2)}) collective-permute-start(bf16[128,1024]{1,0:T(8,128)(2,1)} %get-tuple-element.1517.refs_11_), channel_id=1, source_target_pairs={{4,0},{8,12},{5,1},{9,13},{6,2},{10,14},{7,3},{11,15},{20,16},{24,... | collective-permute-start | bytes 786440 | tf_op jit(solution)/shard_map/ppermute | solution.py:57
  85.5 7.4 %shard_map.119 = (bf16[384,1024]{1,0:T(8,128)(2,1)}, f32[384,1024]{1,0:T(8,128)}, f32[8,128]{1,0:T(8,128)S(1)}) custom-call(bf16[384,128]{1,0:T(8,128)(2,1)} %collective-permute-done.21.refs_0_.refs_26_, bf16[384,128]{1,0:T(8,128)(2,1)} %get-tuple-element.1540.refs_1_.refs_34_, s32[384,128]{1,0:T(8,128)S(1)} %copy-done.2, bf16[256,1024]{1,0:T(8,128)(2,1)} %bitcast.4.refs_3_, ...), custom_call_target="tpu_custom_call" | custom-call | flops 999999995904 | tf_op jit(solution)/shard_map/pallas_call | solution.py:77
  94.3 2.0 %shard_map.122 = (bf16[384,1024]{1,0:T(8,128)(2,1)}, f32[8,128]{1,0:T(8,128)S(1)}) custom-call(bf16[384,1024]{1,0:T(8,128)(2,1)} %get-tuple-element.1384.refs_0_, f32[384,1024]{1,0:T(8,128)S(1)} %copy-done.5, bf16[256,1024]{1,0:T(8,128)(2,1)} %collective-permute-done.22.refs_2_.refs_12_, ...), custom_call_target="tpu_custom_call", output_to_operand_aliasing={{0}: (0, {})} | custom-call | flops 999999995904 | tf_op jit(solution)/shard_map/pallas_call | solution.py:77
  96.4 1.6 %collective-permute-done.23.refs_2_ = bf16[128,1024]{1,0:T(8,128)(2,1)} collective-permute-done((bf16[128,1024]{1,0:T(8,128)(2,1)}, bf16[128,1024]{1,0:T(8,128)(2,1)}, u32[]{:S(2)}, u32[]{:S(2)}) %collective-permute-start.23) | collective-permute-done | bytes 262176 | tf_op jit(solution)/shard_map/ppermute | solution.py:57
  98.0 2.4 %shard_map.125 = (bf16[384,1024]{1,0:T(8,128)(2,1)}, f32[8,128]{1,0:T(8,128)}) custom-call(bf16[384,1024]{1,0:T(8,128)(2,1)} %get-tuple-element.1442.refs_0_, f32[384,1024]{1,0:T(8,128)S(1)} %copy-done.6, bf16[128,1024]{1,0:T(8,128)(2,1)} %collective-permute-done.23.refs_2_, ...), custom_call_target="tpu_custom_call", output_to_operand_aliasing={{0}: (0, {})} | custom-call | flops 999999995904 | tf_op jit(solution)/shard_map/pallas_call | solution.py:77
  (107 shorter events, 17.1 us)
Async XLA Ops:
  0.0 39.1 %collective-permute-start = (bf16[384,2048]{1,0:T(8,128)(2,1)}, bf16[384,2048]{1,0:T(8,128)(2,1)}, u32[]{:S(2)}, u32[]{:S(2)}) collective-permute-start(bf16[384,2048]{1,0:T(8,128)(2,1)} %refs_0_.4), channel_id=1, source_target_pairs={{0,1},{1,0},{2,3},{3,2},{4,8},{5,9},{6,10},{7,11},{8,4},{9,5},{10,... | collective-permute-start | bytes 4718600 | tf_op jit(solution)/shard_map/ppermute | solution.py:40
  3.7 16.4 %collective-permute-start.2 = (bf16[128,2048]{1,0:T(8,128)(2,1)}, bf16[128,2048]{1,0:T(8,128)(2,1)}, u32[]{:S(2)}, u32[]{:S(2)}) collective-permute-start(bf16[128,2048]{1,0:T(8,128)(2,1)} %get-tuple-element.1515.refs_9_), channel_id=1, source_target_pairs={{0,4},{4,0},{8,12},{12,8},{1,5},{5,1},{9,13},{13,9},{2,6},{6,2},{1... | collective-permute-start | bytes 1572872 | tf_op jit(solution)/shard_map/ppermute | solution.py:57
  7.0 3.0 %collective-permute-start.1 = (bf16[2,128,2048]{2,1,0:T(8,128)(2,1)}, bf16[2,128,2048]{2,1,0:T(8,128)(2,1)}, u32[]{:S(2)}, u32[]{:S(2)}) collective-permute-start(bf16[2,128,2048]{2,1,0:T(8,128)(2,1)} %param.12), channel_id=1, source_target_pairs={{0,1},{1,0},{2,3},{3,2},{4,5},{5,4},{6,7},{7,6},{8,9},{9,8},{10,11... | collective-permute-start | bytes 3145736 | tf_op jit(solution)/shard_map/ppermute | solution.py:30
  7.0 25.9 %collective-permute-start.3 = (bf16[2,128,2048]{2,1,0:T(8,128)(2,1)}, bf16[2,128,2048]{2,1,0:T(8,128)(2,1)}, u32[]{:S(2)}, u32[]{:S(2)}) collective-permute-start(bf16[2,128,2048]{2,1,0:T(8,128)(2,1)} %param.12), channel_id=1, source_target_pairs={{0,2},{2,0},{1,3},{3,1},{4,6},{6,4},{5,7},{7,5},{8,10},{10,8},{9,1... | collective-permute-start | bytes 3145736 | tf_op jit(solution)/shard_map/ppermute | solution.py:30
  10.0 32.2 %collective-permute-start.5 = (bf16[256,2048]{1,0:T(8,128)(2,1)}, bf16[256,2048]{1,0:T(8,128)(2,1)}, u32[]{:S(2)}, u32[]{:S(2)}) collective-permute-start(bf16[256,2048]{1,0:T(8,128)(2,1)} %get-tuple-element.1522.refs_16_), channel_id=1, source_target_pairs={{0,4},{4,0},{8,12},{12,8},{1,5},{5,1},{9,13},{13,9},{2,6},{6,2},{1... | collective-permute-start | bytes 3145736 | tf_op jit(solution)/shard_map/ppermute | solution.py:57
  20.1 22.1 %collective-permute-start.6 = (bf16[128,2048]{1,0:T(8,128)(2,1)}, bf16[128,2048]{1,0:T(8,128)(2,1)}, u32[]{:S(2)}, u32[]{:S(2)}) collective-permute-start(bf16[128,2048]{1,0:T(8,128)(2,1)} %collective-permute-done.2.refs_2_.refs_1_.refs_18_), channel_id=1, source_target_pairs={{0,1},{1,0},{2,3},{3,2},{4,20},{5,21},{6,22},{7,23},{8,24},{9,25},... | collective-permute-start | bytes 1572872 | tf_op jit(solution)/shard_map/ppermute | solution.py:40
  32.9 10.8 %collective-permute-start.7 = (bf16[128,2048]{1,0:T(8,128)(2,1)}, bf16[128,2048]{1,0:T(8,128)(2,1)}, u32[]{:S(2)}, u32[]{:S(2)}) collective-permute-start(bf16[128,2048]{1,0:T(8,128)(2,1)} %collective-permute-done.2.refs_2_.refs_1_.refs_18_), channel_id=1, source_target_pairs={{0,1},{1,0},{2,3},{3,2},{4,6},{5,7},{6,4},{7,5},{8,10},{9,11},{10,... | collective-permute-start | bytes 1572872 | tf_op jit(solution)/shard_map/ppermute | solution.py:40
  32.9 3.7 %collective-permute-start.4 = (bf16[2,128,2048]{2,1,0:T(8,128)(2,1)}, bf16[2,128,2048]{2,1,0:T(8,128)(2,1)}, u32[]{:S(2)}, u32[]{:S(2)}) collective-permute-start(bf16[2,128,2048]{2,1,0:T(8,128)(2,1)} %collective-permute-done.3.refs_7_), channel_id=1, source_target_pairs={{0,1},{1,0},{2,3},{3,2},{4,5},{5,4},{6,7},{7,6},{8,9},{9,8},{10,11... | collective-permute-start | bytes 3145736 | tf_op jit(solution)/shard_map/ppermute | solution.py:30
  42.2 18.0 %collective-permute-start.12 = (bf16[160,2048]{1,0:T(8,128)(2,1)}, bf16[160,2048]{1,0:T(8,128)(2,1)}, u32[]{:S(2)}, u32[]{:S(2)}) collective-permute-start(bf16[160,2048]{1,0:T(8,128)(2,1)} %get-tuple-element.1519.refs_13_), channel_id=1, source_target_pairs={{0,4},{4,0},{8,12},{12,8},{1,5},{5,1},{9,13},{13,9},{2,6},{6,2},{1... | collective-permute-start | bytes 1966088 | tf_op jit(solution)/shard_map/ppermute | solution.py:57
  43.7 20.5 %collective-permute-start.14 = (bf16[256,2048]{1,0:T(8,128)(2,1)}, bf16[256,2048]{1,0:T(8,128)(2,1)}, u32[]{:S(2)}, u32[]{:S(2)}) collective-permute-start(bf16[256,2048]{1,0:T(8,128)(2,1)} %collective-permute-done.5.refs_3_.refs_12_.refs_17_), channel_id=1, source_target_pairs={{0,1},{1,0},{2,3},{3,2},{4,8},{5,9},{6,10},{7,11},{8,4},{9,5},{10,... | collective-permute-start | bytes 3145736 | tf_op jit(solution)/shard_map/ppermute | solution.py:40
  43.7 8.4 %collective-permute-start.10 = (bf16[128,2048]{1,0:T(8,128)(2,1)}, bf16[128,2048]{1,0:T(8,128)(2,1)}, u32[]{:S(2)}, u32[]{:S(2)}) collective-permute-start(bf16[128,2048]{1,0:T(8,128)(2,1)} %collective-permute-done.7.refs_3_.refs_22_), channel_id=1, source_target_pairs={{0,1},{1,0},{2,3},{3,2},{4,20},{5,21},{6,22},{7,23},{8,24},{9,25},... | collective-permute-start | bytes 1572872 | tf_op jit(solution)/shard_map/ppermute | solution.py:40
  44.2 6.4 %collective-permute-start.8 = (bf16[128,2048]{1,0:T(8,128)(2,1)}, bf16[128,2048]{1,0:T(8,128)(2,1)}, u32[]{:S(2)}, u32[]{:S(2)}) collective-permute-start(bf16[128,2048]{1,0:T(8,128)(2,1)} %collective-permute-done.2.refs_2_.refs_1_.refs_18_), channel_id=1, source_target_pairs={{0,1},{1,0},{2,3},{3,2},{4,5},{5,4},{6,7},{7,6},{8,9},{9,8},{10,11... | collective-permute-start | bytes 1572872 | tf_op jit(solution)/shard_map/ppermute | solution.py:40
  44.3 6.3 %collective-permute-start.9 = (bf16[128,2048]{1,0:T(8,128)(2,1)}, bf16[128,2048]{1,0:T(8,128)(2,1)}, u32[]{:S(2)}, u32[]{:S(2)}) collective-permute-start(bf16[128,2048]{1,0:T(8,128)(2,1)} %collective-permute-done.6.refs_5_.refs_24_), channel_id=1, source_target_pairs={{0,1},{1,0},{2,3},{3,2},{4,5},{5,4},{6,7},{7,6},{8,9},{9,8},{10,11... | collective-permute-start | bytes 1572872 | tf_op jit(solution)/shard_map/ppermute | solution.py:40
  50.6 29.2 %collective-permute-start.17 = (bf16[224,2048]{1,0:T(8,128)(2,1)}, bf16[224,2048]{1,0:T(8,128)(2,1)}, u32[]{:S(2)}, u32[]{:S(2)}) collective-permute-start(bf16[224,2048]{1,0:T(8,128)(2,1)} %get-tuple-element.1533.refs_27_), channel_id=1, source_target_pairs={{4,0},{8,12},{5,1},{9,13},{6,2},{10,14},{7,3},{11,15},{20,16},{24,... | collective-permute-start | bytes 2752520 | tf_op jit(solution)/shard_map/ppermute | solution.py:57
  51.9 2.3 %collective-permute-start.11 = (bf16[128,2048]{1,0:T(8,128)(2,1)}, bf16[128,2048]{1,0:T(8,128)(2,1)}, u32[]{:S(2)}, u32[]{:S(2)}) collective-permute-start(bf16[128,2048]{1,0:T(8,128)(2,1)} %collective-permute-done.7.refs_3_.refs_22_), channel_id=1, source_target_pairs={{0,1},{1,0},{2,3},{3,2},{4,5},{5,4},{6,7},{7,6},{8,9},{9,8},{10,11... | collective-permute-start | bytes 1572872 | tf_op jit(solution)/shard_map/ppermute | solution.py:40
  54.2 5.9 %collective-permute-start.13 = (bf16[128,2048]{1,0:T(8,128)(2,1)}, bf16[128,2048]{1,0:T(8,128)(2,1)}, u32[]{:S(2)}, u32[]{:S(2)}) collective-permute-start(bf16[128,2048]{1,0:T(8,128)(2,1)} %collective-permute-done.10.refs_7_.refs_20_), channel_id=1, source_target_pairs={{0,1},{1,0},{2,3},{3,2},{4,5},{5,4},{6,7},{7,6},{8,9},{9,8},{10,11... | collective-permute-start | bytes 1572872 | tf_op jit(solution)/shard_map/ppermute | solution.py:40
  62.2 6.3 %collective-permute-start.15 = (bf16[384,128]{1,0:T(8,128)(2,1)}, bf16[384,128]{1,0:T(8,128)(2,1)}, u32[]{:S(2)}, u32[]{:S(2)}) collective-permute-start(bf16[384,128]{1,0:T(8,128)(2,1)} %get-tuple-element.1535.refs_0_.refs_29_), channel_id=1, source_target_pairs={{0,1},{1,0},{2,3},{3,2},{4,8},{5,9},{6,10},{7,11},{8,4},{9,5},{10,... | collective-permute-start | bytes 294920 | tf_op jit(solution)/shard_map/ppermute | solution.py:40
  62.2 17.6 %collective-permute-start.16 = (bf16[128,2048]{1,0:T(8,128)(2,1)}, bf16[128,2048]{1,0:T(8,128)(2,1)}, u32[]{:S(2)}, u32[]{:S(2)}) collective-permute-start(bf16[128,2048]{1,0:T(8,128)(2,1)} %get-tuple-element.1520.refs_14_), channel_id=1, source_target_pairs={{0,1},{1,0},{2,3},{3,2},{4,8},{5,9},{6,10},{7,11},{8,4},{9,5},{10,... | collective-permute-start | bytes 1572872 | tf_op jit(solution)/shard_map/ppermute | solution.py:40
  62.7 17.1 %collective-permute-start.18 = (bf16[2,128,1024]{2,1,0:T(8,128)(2,1)}, bf16[2,128,1024]{2,1,0:T(8,128)(2,1)}, u32[]{:S(2)}, u32[]{:S(2)}) collective-permute-start(bf16[2,128,1024]{2,1,0:T(8,128)(2,1)} %param.13), channel_id=1, source_target_pairs={{0,2},{2,0},{1,3},{3,1},{4,6},{6,4},{5,7},{7,5},{8,10},{10,8},{9,1... | collective-permute-start | bytes 1572872 | tf_op jit(solution)/shard_map/ppermute | solution.py:30
  70.1 15.4 %collective-permute-start.21 = (bf16[384,128]{1,0:T(8,128)(2,1)}, bf16[384,128]{1,0:T(8,128)(2,1)}, u32[]{:S(2)}, u32[]{:S(2)}) collective-permute-start(bf16[384,128]{1,0:T(8,128)(2,1)} %get-tuple-element.1540.refs_1_.refs_34_), channel_id=1, source_target_pairs={{4,0},{8,12},{5,1},{9,13},{6,2},{10,14},{7,3},{11,15},{20,16},{24,... | collective-permute-start | bytes 294920 | tf_op jit(solution)/shard_map/ppermute | solution.py:57
  71.4 22.0 %collective-permute-start.22 = (bf16[256,1024]{1,0:T(8,128)(2,1)}, bf16[256,1024]{1,0:T(8,128)(2,1)}, u32[]{:S(2)}, u32[]{:S(2)}) collective-permute-start(bf16[256,1024]{1,0:T(8,128)(2,1)} %get-tuple-element.1516.refs_10_), channel_id=1, source_target_pairs={{4,0},{8,12},{5,1},{9,13},{6,2},{10,14},{7,3},{11,15},{20,16},{24,... | collective-permute-start | bytes 1572872 | tf_op jit(solution)/shard_map/ppermute | solution.py:57
  79.8 4.0 %collective-permute-start.19 = (bf16[2,128,1024]{2,1,0:T(8,128)(2,1)}, bf16[2,128,1024]{2,1,0:T(8,128)(2,1)}, u32[]{:S(2)}, u32[]{:S(2)}) collective-permute-start(bf16[2,128,1024]{2,1,0:T(8,128)(2,1)} %param.13), channel_id=1, source_target_pairs={{0,1},{1,0},{2,3},{3,2},{4,5},{5,4},{6,7},{7,6},{8,9},{9,8},{10,11... | collective-permute-start | bytes 1572872 | tf_op jit(solution)/shard_map/ppermute | solution.py:30
  79.8 4.0 %collective-permute-start.20 = (bf16[2,128,1024]{2,1,0:T(8,128)(2,1)}, bf16[2,128,1024]{2,1,0:T(8,128)(2,1)}, u32[]{:S(2)}, u32[]{:S(2)}) collective-permute-start(bf16[2,128,1024]{2,1,0:T(8,128)(2,1)} %collective-permute-done.18.refs_32_), channel_id=1, source_target_pairs={{0,1},{1,0},{2,3},{3,2},{4,5},{5,4},{6,7},{7,6},{8,9},{9,8},{10,11... | collective-permute-start | bytes 1572872 | tf_op jit(solution)/shard_map/ppermute | solution.py:30
  83.8 14.1 %collective-permute-start.23 = (bf16[128,1024]{1,0:T(8,128)(2,1)}, bf16[128,1024]{1,0:T(8,128)(2,1)}, u32[]{:S(2)}, u32[]{:S(2)}) collective-permute-start(bf16[128,1024]{1,0:T(8,128)(2,1)} %get-tuple-element.1517.refs_11_), channel_id=1, source_target_pairs={{4,0},{8,12},{5,1},{9,13},{6,2},{10,14},{7,3},{11,15},{20,16},{24,... | collective-permute-start | bytes 786440 | tf_op jit(solution)/shard_map/ppermute | solution.py:57
  (13 other events, 24.0 us)

commit v5 on v4

--- a/solution.py
+++ b/solution.py
@@ -196,21 +196,17 @@
 
 def last_rows(held, tokens, across, coords, layout):
     cut, last = layout.sizes
-    size, wide = last + TALL, coords.shape[1]
+    size = last + TALL
+    wide = coords.shape[1]
     count = layout.tall // TALL
 
-    def body(t_ref, a_ref, c_ref, out_ref, rest_ref, sem):
+    def body(t_ref, a_ref, c_ref, out_ref, sem):
         place = Place()
-        rest = started(
-            pltpu.make_async_copy(
-                a_ref.at[pl.ds(size, layout.tall - size)], rest_ref, sem.at[0]
-            )
-        )
 
         @pl.when(place.end)
         def _():
             copy = pltpu.make_async_copy(
-                t_ref.at[pl.ds(cut, last)], out_ref.at[pl.ds(0, last)], sem.at[1]
+                t_ref.at[pl.ds(cut, last)], out_ref.at[pl.ds(0, last)], sem
             )
             copy.start()
             for i in range(layout.width // wide):
@@ -222,19 +218,32 @@
 
         @pl.when(jnp.logical_not(place.end))
         def _():
-            run_copies(
-                [pltpu.make_async_copy(a_ref.at[pl.ds(0, size)], out_ref, sem.at[1])]
-            )
-
-        waited(rest)
-
-    return call(
-        held,
-        body,
-        [array(size, layout.width), array(layout.tall - size, layout.width)],
+            run_copies([pltpu.make_async_copy(a_ref.at[pl.ds(0, size)], out_ref, sem)])
+
+    return call(
+        held,
+        body,
+        array(size, layout.width),
         [tokens, across, coords],
         [ANY, ANY, VMEM],
-        scratch=[pltpu.SemaphoreType.DMA((2,))],
+        scratch=[pltpu.SemaphoreType.DMA],
+    )
+
+
+def other_rows(held, across, layout):
+    size = layout.sizes[1] + TALL
+    rest = layout.tall - size
+
+    def body(a_ref, out_ref, sem):
+        run_copies([pltpu.make_async_copy(a_ref.at[pl.ds(size, rest)], out_ref, sem)])
+
+    return call(
+        held,
+        body,
+        array(rest, layout.width),
+        [across],
+        [ANY],
+        scratch=[pltpu.SemaphoreType.DMA],
     )
 
 
@@ -384,13 +393,26 @@
     )
 
 
+def spread_of(use, low, place, count, adapters):
+    some = [
+        jnp.where(use == (place.mine ^ turn) * adapters + j, low, 0)
+        for turn in range(count)
+        for j in range(adapters)
+    ]
+    return jnp.concatenate(some, axis=1)
+
+
+def terms_of(spread, ups_held):
+    return dot(spread, ups_held).astype(jnp.bfloat16).astype(jnp.float32)
+
+
 def add_last(held, total, low, use, ups, relayed, beyond, inner, weight, layout):
     adapters, rank, columns = ups[0].shape
     count = len(ups)
     cut, last = layout.sizes
     tall, width = layout.tall, layout.width
 
-    def body(hop_ref, low_ref, use_ref, *refs):
+    def body(low_ref, use_ref, *refs):
         up_refs = refs[:count]
         total_ref, n0_ref, n1_ref, b0_ref, b1_ref, p0_ref, p1_ref, w_ref = refs[
             count : count + 8
@@ -399,76 +421,53 @@
         w_held, w_sem, v_held, v_sem, a_held, p_held, u_held, rows_ref, sum_ref, sem = scratch
         place = Place()
         first = n0_ref.shape[0]
-        at_end = [
-            pltpu.make_async_copy(n0_ref, a_held.at[pl.ds(0, first)], sem.at[0]),
-            pltpu.make_async_copy(n1_ref, a_held.at[pl.ds(first, tall - first)], sem.at[1]),
-        ]
-        inside = [
-            pltpu.make_async_copy(b0_ref, a_held.at[pl.ds(0, cut)], sem.at[0]),
-            pltpu.make_async_copy(b1_ref, a_held.at[pl.ds(cut, last)], sem.at[1]),
-        ]
-        second = [
-            pltpu.make_async_copy(p0_ref, p_held.at[pl.ds(0, cut)], sem.at[8]),
-            pltpu.make_async_copy(
-                p1_ref.at[pl.ds(0, last)], p_held.at[pl.ds(cut, last)], sem.at[9]
-            ),
-        ]
-
-        loads = started(
-            *[
-                pltpu.make_async_copy(
-                    up_ref,
-                    u_held.at[pl.ds(i * adapters * rank, adapters * rank)],
-                    sem.at[i + 3],
-                )
-                for i, up_ref in enumerate(up_refs)
-            ],
-            pltpu.make_async_copy(total_ref, sum_ref, sem.at[2]),
-        )
+        load = pltpu.make_async_copy(total_ref, sum_ref, sem.at[2])
+        load.start()
 
         @pl.when(place.end)
         def _():
-            started(*at_end)
+            w = Rows(w_ref, place.near * width, w_held, w_sem)
+            loads = started(
+                pltpu.make_async_copy(n0_ref, a_held.at[pl.ds(0, first)], sem.at[0]),
+                pltpu.make_async_copy(n1_ref, a_held.at[pl.ds(first, tall - first)], sem.at[1]),
+            )
+            waited(loads)
+            load.wait()
+            sum_ref[...] += w.dot(a_held)
+            run_copies([pltpu.make_async_copy(sum_ref, sums_ref, sem.at[7])])
 
         @pl.when(jnp.logical_not(place.end))
         def _():
-            started(*inside)
-
-        w = Rows(w_ref, jnp.where(place.end, place.near, place.far) * width, w_held, w_sem)
-        v = Rows(w_ref, place.partner * width, v_held, v_sem, begin=False)
-
-        @pl.when(jnp.logical_not(place.end))
-        def _():
-            started(*second, *v.copies)
-
-        low = jnp.where(place.end, hop_ref[...], low_ref[...])
-        some = [
-            jnp.where(use_ref[...] == (place.mine ^ turn) * adapters + j, low, 0)
-            for turn in range(count)
-            for j in range(adapters)
-        ]
-        spread = jnp.concatenate(some, axis=1)
-        waited(loads)
-        terms = dot(spread, u_held[...])
-        sum_ref[...] += terms.astype(jnp.bfloat16).astype(jnp.float32)
-
-        @pl.when(place.end)
-        def _():
-            waited(at_end)
-
-        @pl.when(jnp.logical_not(place.end))
-        def _():
-            waited(inside)
-
-        sum_ref[...] += w.dot(a_held)
-
-        @pl.when(place.end)
-        def _():
-            run_copies([pltpu.make_async_copy(sum_ref, sums_ref, sem.at[7])])
-
-        @pl.when(jnp.logical_not(place.end))
-        def _():
-            waited(second)
+            loads = started(
+                *[
+                    pltpu.make_async_copy(
+                        up_ref,
+                        u_held.at[pl.ds(i * adapters * rank, adapters * rank)],
+                        sem.at[i + 3],
+                    )
+                    for i, up_ref in enumerate(up_refs)
+                ]
+            )
+            beyonds = started(
+                pltpu.make_async_copy(b0_ref, a_held.at[pl.ds(0, cut)], sem.at[0]),
+                pltpu.make_async_copy(b1_ref, a_held.at[pl.ds(cut, last)], sem.at[1]),
+            )
+            w = Rows(w_ref, place.far * width, w_held, w_sem)
+            inners = started(
+                pltpu.make_async_copy(p0_ref, p_held.at[pl.ds(0, cut)], sem.at[8]),
+                pltpu.make_async_copy(
+                    p1_ref.at[pl.ds(0, last)], p_held.at[pl.ds(cut, last)], sem.at[9]
+                ),
+            )
+            v = Rows(w_ref, place.partner * width, v_held, v_sem)
+            spread = spread_of(use_ref[...], low_ref[...], place, count, adapters)
+            waited(loads)
+            terms = terms_of(spread, u_held[...])
+            load.wait()
+            sum_ref[...] += terms
+            waited(beyonds)
+            sum_ref[...] += w.dot(a_held)
+            waited(inners)
             rows_ref[...] = (sum_ref[...] + v.dot(p_held)).astype(rows_ref.dtype)
             run_copies([pltpu.make_async_copy(rows_ref, out_ref, sem.at[7])])
 
@@ -476,10 +475,10 @@
         held,
         body,
         [array(tall, columns), sums(layout)],
-        [*low, use, *[u.reshape(-1, columns) for u in ups]]
+        [low, use, *[u.reshape(-1, columns) for u in ups]]
         + [total, *relayed, *beyond, *inner, weight],
-        [VMEM] * 3 + [ANY] * count + [HBM] + [ANY] * 6 + [HBM],
-        [ANY, ANY],
+        [VMEM] * 2 + [ANY] * count + [HBM] + [ANY] * 6 + [HBM],
+        [ANY, HBM],
         room(2, layout)
         + [
             pltpu.VMEM((tall, width), jnp.bfloat16),
@@ -499,31 +498,35 @@
     def body(beyond_ref, *refs):
         piece_refs = refs[:count]
         out_ref, b_held, w_held, sem = refs[count:]
-        seat = Place().seat
-        load = started(pltpu.make_async_copy(beyond_ref, b_held, sem.at[0]))
-        lends = started(
-            *[
-                pltpu.make_async_copy(
-                    part,
-                    w_held.at[pl.ds(k * deep + first, layout.rows)],
-                    sem.at[1 + 2 * k + side],
-                )
-                for k, piece_ref in enumerate(piece_refs)
-                for side, (first, part) in enumerate(layout.sides(piece_ref))
-            ]
-        )
-        waited(load)
-        total = 0.0
-        step = count // 4
-        for first in range(0, count, step):
-            blocks = [
-                b_held[:, pl.ds(pl.multiple_of((seat ^ k) * deep, deep), deep)]
-                for k in range(first, first + step)
-            ]
-            waited(lends[2 * first : 2 * (first + step)])
-            some = w_held[first * deep : (first + step) * deep, :]
-            total += dot(jnp.concatenate(blocks, axis=1), some)
-        out_ref[...] = total.astype(out_ref.dtype)
+        place = Place()
+        seat = place.seat
+
+        @pl.when(jnp.logical_not(place.end))
+        def _():
+            load = started(pltpu.make_async_copy(beyond_ref, b_held, sem.at[0]))
+            lends = started(
+                *[
+                    pltpu.make_async_copy(
+                        part,
+                        w_held.at[pl.ds(k * deep + first, layout.rows)],
+                        sem.at[1 + 2 * k + side],
+                    )
+                    for k, piece_ref in enumerate(piece_refs)
+                    for side, (first, part) in enumerate(layout.sides(piece_ref))
+                ]
+            )
+            waited(load)
+            total = 0.0
+            step = count // 4
+            for first in range(0, count, step):
+                blocks = [
+                    b_held[:, pl.ds(pl.multiple_of((seat ^ k) * deep, deep), deep)]
+                    for k in range(first, first + step)
+                ]
+                waited(lends[2 * first : 2 * (first + step)])
+                some = w_held[first * deep : (first + step) * deep, :]
+                total += dot(jnp.concatenate(blocks, axis=1), some)
+            out_ref[...] = total.astype(out_ref.dtype)
 
     return call(
         held,
@@ -542,38 +545,102 @@
 NOT_KEPT = ("tick", "tokens", "down", "up", "use")
 
 
-def finished(held, out, total, term, i, layout, keep=False):
-    start, size = i * layout.cut, layout.sizes[i]
-    kept = [held[n] for n in sorted(held) if keep and n not in NOT_KEPT]
-
-    def body(out_ref, total_ref, term_ref, *refs):
-        into_ref, sum_ref, term_held, rows_ref, sem = refs[-5:]
+def first_finished(held, out, total, term, low, use, ups, layout):
+    adapters, rank, columns = ups[0].shape
+    count = len(ups)
+    cut, last = layout.sizes
+
+    def body(out_ref, total_ref, term_ref, low_ref, use_ref, *refs):
+        up_refs = refs[:count]
+        into_ref, late_ref, sum_ref, term_held, u_held, rows_ref, low_held, use_held, sem = refs[
+            count:
+        ]
+        place = Place()
+
+        @pl.when(place.end)
+        def _():
+            first = started(
+                pltpu.make_async_copy(low_ref, low_held, sem.at[count + 2]),
+                pltpu.make_async_copy(use_ref, use_held, sem.at[count + 3]),
+            )
+            loads = started(
+                *[
+                    pltpu.make_async_copy(
+                        up_ref,
+                        u_held.at[pl.ds(i * adapters * rank, adapters * rank)],
+                        sem.at[i],
+                    )
+                    for i, up_ref in enumerate(up_refs)
+                ],
+                pltpu.make_async_copy(total_ref, sum_ref, sem.at[count]),
+                pltpu.make_async_copy(term_ref, term_held, sem.at[count + 1]),
+            )
+            waited(first)
+            spread = spread_of(use_held[...], low_held[...], place, count, adapters)
+            waited(loads)
+            sum_ref[...] += terms_of(spread, u_held[...])
+            stores = started(
+                pltpu.make_async_copy(sum_ref.at[pl.ds(cut, last)], late_ref, sem.at[0])
+            )
+            rows_ref[...] = (sum_ref[:cut, :] + term_held[...].astype(jnp.float32)).astype(
+                rows_ref.dtype
+            )
+            run_copies([pltpu.make_async_copy(rows_ref, into_ref.at[pl.ds(0, cut)], sem.at[1])])
+            waited(stores)
+
+    return call(
+        held,
+        body,
+        [array(layout.tall, columns), array(last, columns, dtype=jnp.float32)],
+        [out, total, term, low, use, *[u.reshape(-1, columns) for u in ups]],
+        [ANY, HBM] + [ANY] * (3 + count),
+        [ANY, ANY],
+        [
+            pltpu.VMEM((layout.tall, columns), jnp.float32),
+            pltpu.VMEM((cut, columns), jnp.bfloat16),
+            pltpu.VMEM((count * adapters * rank, columns), jnp.bfloat16),
+            pltpu.VMEM((cut, columns), jnp.bfloat16),
+            pltpu.VMEM(low.shape, low.dtype),
+            pltpu.VMEM(use.shape, use.dtype),
+            pltpu.SemaphoreType.DMA((count + 4,)),
+        ],
+        alias={0: 0},
+    )
+
+
+def last_finished(held, out, late, term, layout):
+    kept = [held[n] for n in sorted(held) if n.startswith("lent")]
+    cut, last = layout.sizes
+
+    def body(out_ref, late_ref, term_ref, *refs):
+        into_ref, late_held, term_held, rows_ref, sem = refs[-5:]
 
         @pl.when(Place().end)
         def _():
-            loads = started(
-                pltpu.make_async_copy(total_ref.at[pl.ds(start, size)], sum_ref, sem.at[0]),
-                pltpu.make_async_copy(term_ref, term_held, sem.at[1]),
-            )
-            waited(loads)
-            rows_ref[...] = (sum_ref[...] + term_held[...].astype(jnp.float32)).astype(
+            run_copies(
+                [
+                    pltpu.make_async_copy(late_ref, late_held, sem.at[0]),
+                    pltpu.make_async_copy(term_ref, term_held, sem.at[1]),
+                ]
+            )
+            rows_ref[...] = (late_held[...] + term_held[...].astype(jnp.float32)).astype(
                 rows_ref.dtype
             )
             run_copies(
-                [pltpu.make_async_copy(rows_ref, into_ref.at[pl.ds(start, size)], sem.at[2])]
-            )
-
-    return call(
-        held,
-        body,
-        array(layout.tall, layout.columns),
-        [out, total, term, *kept],
+                [pltpu.make_async_copy(rows_ref, into_ref.at[pl.ds(cut, last)], sem.at[2])]
+            )
+
+    return call(
+        held,
+        body,
+        array(*out.shape),
+        [out, late, term, *kept],
         [ANY] * (3 + len(kept)),
         [ANY],
         [
-            pltpu.VMEM((size, layout.columns), jnp.float32),
-            pltpu.VMEM((size, layout.columns), jnp.bfloat16),
-            pltpu.VMEM((size, layout.columns), jnp.bfloat16),
+            pltpu.VMEM((last, layout.columns), jnp.float32),
+            pltpu.VMEM((last, layout.columns), out.dtype),
+            pltpu.VMEM((last, layout.columns), out.dtype),
             pltpu.SemaphoreType.DMA((3,)),
         ],
         alias={0: 0},
@@ -661,7 +728,7 @@
     coords, _ = coords_of(h, h["tokens"], h["use"], [h["down_xc"]], [3], coords)
     h["across"] = across
     fence(h)
-    h["last"], h["others"] = last_rows(h, h["tokens"], h["across"], coords, layout)
+    h["last"] = last_rows(h, h["tokens"], h["across"], coords, layout)
     h["later_p"], h["lent_y"] = later_p, lent_y
     fence(h)
     last_p = hop(h["last"], PAIRS)
@@ -675,13 +742,15 @@
     fence(h)
     lent_yc = swap_inside(h["lent_y"], "inner")
     fence(h)
+    h["others"] = other_rows(h, h["across"], layout)
+    h["lent_c"], h["lent_yc"] = lent_c, lent_yc
+    fence(h)
+    others_o = hop(h["others"], OUTWARD)
+    fence(h)
+    lent_xc = swap_inside(h["lent_x"], "inner")
+    fence(h)
     at_end = ("partner", [h["lent"], h["later_p"]])
     total = add_block(h, total, at_end, ("near", [h["across"]]), weight, layout)
-    h["lent_c"], h["lent_yc"] = lent_c, lent_yc
-    fence(h)
-    others_o = hop(h["others"], OUTWARD)
-    fence(h)
-    lent_xc = swap_inside(h["lent_x"], "inner")
     h["lent_xc"], h["lent_d"] = lent_xc, lent_d
     fence(h)
     lent_dc = swap_inside(h["lent_d"], "inner")
@@ -701,11 +770,11 @@
     h["help0"] = helped(h, h["beyond0"], pieces, layout, 0)
     h["pair_m"] = pair_m
     fence(h)
+    help_o0 = hop(h["help0"], OUTWARD)
+    fence(h)
     h["whole"] = added(h, h["pair"], h["pair_m"])
     fence(h)
     low_o = hop(h["whole"], OUTWARD)
-    fence(h)
-    help_o0 = hop(h["help0"], OUTWARD)
     h["beyond1"], h["others_o"], h["up_x"] = beyond1, others_o, up_x
     fence(h)
     up_xc, up_c = swap(h["up_x"], "inner"), swap(h["up"], "inner")
@@ -715,14 +784,14 @@
     h["up_xc"], h["up_c"] = up_xc, up_c
     fence(h)
     help_o1 = hop(h["help1"], OUTWARD)
-    h["low_o"] = low_o
-    fence(h)
+    fence(h)
+    ups = [h["up"], h["up_c"], h["up_x"], h["up_xc"]]
     out, total = add_last(
         h,
         total,
-        [h["low_o"], h["whole"]],
+        h["whole"],
         h["use"],
-        [h["up"], h["up_c"], h["up_x"], h["up_xc"]],
+        ups,
         [h["last_p"], h["others_o"]],
         [h["beyond0"], h["beyond1"]],
         [h["later_p"], h["last_p"]],
@@ -730,13 +799,14 @@
         layout,
     )
     fence(h)
-    h["help_o0"] = help_o0
-    fence(h)
-    out = finished(h, out, total, h["help_o0"], 0, layout)
+    h["help_o0"], h["low_o"] = help_o0, low_o
+    fence(h)
+    ups = [h["up"], h["up_c"], h["up_x"], h["up_xc"]]
+    out, late = first_finished(h, out, total, h["help_o0"], h["low_o"], h["use"], ups, layout)
     fence(h)
     h["help_o1"] = help_o1
     fence(h)
-    return finished(h, out, total, h.pop("help_o1"), 1, layout, keep=True)
+    return last_finished(h, out, late, h.pop("help_o1"), layout)
 
 
 def owner_mask(slot, rank, adapters):

time: 101 us -> 99.8 us (0.988)
  Pallas kernels: 45.1 us -> 41.8 us
  waiting for transfers between devices: 32.2 us -> 34.2 us
    pallas_call x53 -> x55, Pallas kernels: 45.1 us -> 41.8 us  [call(): pl.pallas_call(counted, out_shape=[*shapes, jax.ShapeDtypeStruct(tick.sha...]
    ppermute x6, waiting for transfers between devices: 10.3 us -> 11.9 us  [swap(): return lax.ppermute(x, axis, [(0, 1), (1, 0)])]
    unnamed x26 -> x24, local copies, waits for them, and re-layouts: 5.7 us -> 4.76 us
  transfers between devices with their start and end apart: 24 -> 24, of which waited for: 9 -> 12; matrix products, arithmetic and copies ran while one was open for 0% -> 0% of each run, Pallas kernels for 43% -> 40%
where the time goes in v5:
time: 99.8 us; the launch traced here: 99.2 us
  Pallas kernels  41.8 us (42%)
  waiting for transfers between devices  34.2 us (34%)
  starting transfers between devices  17.5 us (18%)
  local copies, waits for them, and re-layouts  4.76 us (5%)
    pallas_call x55, Pallas kernels, call(): pl.pallas_call(counted, out_shape=[*shapes, jax.ShapeDtypeStruct(tick.sha...  41.8 us
    ppermute x7, waiting for transfers between devices, hop(): return lax.ppermute(x, 'tensor', pairs)  20.3 us
    ppermute x6, waiting for transfers between devices, swap(): return lax.ppermute(x, axis, [(0, 1), (1, 0)])  11.9 us
    ppermute x7, starting transfers between devices, hop(): return lax.ppermute(x, 'tensor', pairs)  10.3 us
    unnamed x24, local copies, waits for them, and re-layouts  4.76 us
    ppermute x6, starting transfers between devices, swap(): return lax.ppermute(x, axis, [(0, 1), (1, 0)])  4.57 us
    ppermute x11, starting transfers between devices, inside(): return lax.ppermute(x, AXES, pairs)  2.61 us
    ppermute x11, waiting for transfers between devices, inside(): return lax.ppermute(x, AXES, pairs)  2.04 us
  transfers between devices with their start and end apart: 24, of which 12 were waited for; matrix products, arithmetic and copies ran while one was open for 0% of the time, Pallas kernels for 40%

profile of v5, /device:TPU:0, one launch (start us, length us, event | category | flops | bytes accessed | tf_op | source)
XLA Modules:
  0.0 99.2 jit_solution(3526764197473054175)
XLA Ops:
  0.5 1.4 %copy-done.3 = bf16[384,2048]{1,0:T(8,128)(2,1)S(1)} copy-done((bf16[384,2048]{1,0:T(8,128)(2,1)S(1)}, bf16[384,2048]{1,0:T(8,128)(2,1)}, u32[]{:S(2)}) %copy-start.3) | copy-done | bytes 1572888
  1.9 1.8 %shard_map.73 = (bf16[128,2048]{1,0:T(8,128)(2,1)}, f32[8,128]{1,0:T(8,128)S(1)}) custom-call(bf16[384,2048]{1,0:T(8,128)(2,1)S(1)} %copy-done.3, bf16[8192,1024]{1,0:T(8,128)(2,1)} %refs_13_.1, f32[8,128]{1,0:T(8,128)S(1)} %broadcast_in_dim.34.refs_2_), custom_call_target="tpu_custom_call" | custom-call | flops 999999995904 | tf_op jit(solution)/shard_map/pallas_call | solution.py:77
  3.7 3.3 %collective-permute-start.2 = (bf16[128,2048]{1,0:T(8,128)(2,1)}, bf16[128,2048]{1,0:T(8,128)(2,1)}, u32[]{:S(2)}, u32[]{:S(2)}) collective-permute-start(bf16[128,2048]{1,0:T(8,128)(2,1)} %get-tuple-element.638), channel_id=1, source_target_pairs={{0,4},{4,0},{8,12},{12,8},{1,5},{5,1},{9,13},{13,9},{2,6},{6,2},{1... | collective-permute-start | bytes 1572872 | tf_op jit(solution)/shard_map/ppermute | solution.py:57
  7.0 1.6 %collective-permute-start.3 = (bf16[2,128,2048]{2,1,0:T(8,128)(2,1)}, bf16[2,128,2048]{2,1,0:T(8,128)(2,1)}, u32[]{:S(2)}, u32[]{:S(2)}) collective-permute-start(bf16[2,128,2048]{2,1,0:T(8,128)(2,1)} %param.12), channel_id=1, source_target_pairs={{0,2},{2,0},{1,3},{3,1},{4,6},{6,4},{5,7},{7,5},{8,10},{10,8},{9,1... | collective-permute-start | bytes 3145736 | tf_op jit(solution)/shard_map/ppermute | solution.py:30
  10.1 3.8 %shard_map.81 = (f32[384,1024]{1,0:T(8,128)S(1)}, f32[8,128]{1,0:T(8,128)S(1)}) custom-call(bf16[384,2048]{1,0:T(8,128)(2,1)S(1)} %copy-done.3, bf16[8192,1024]{1,0:T(8,128)(2,1)} %refs_13_.1, f32[8,128]{1,0:T(8,128)S(1)} %shard_map.80.refs_2_), custom_call_target="tpu_custom_call" | custom-call | flops 999999995904 | tf_op jit(solution)/shard_map/pallas_call | solution.py:77
  15.3 4.8 %collective-permute-done.2.refs_2_.refs_1_.refs_3_ = bf16[128,2048]{1,0:T(8,128)(2,1)} collective-permute-done((bf16[128,2048]{1,0:T(8,128)(2,1)}, bf16[128,2048]{1,0:T(8,128)(2,1)}, u32[]{:S(2)}, u32[]{:S(2)}) %collective-permute-start.2) | collective-permute-done | bytes 524320 | tf_op jit(solution)/shard_map/ppermute | solution.py:57
  20.1 3.2 %shard_map.84 = (f32[384,128]{1,0:T(8,128)S(1)}, bf16[384,128]{1,0:T(8,128)(2,1)}, f32[8,128]{1,0:T(8,128)S(1)}) custom-call(s32[384,128]{1,0:T(8,128)S(1)} %fusion.refs_0_.refs_1_.refs_4_, bf16[384,2048]{1,0:T(8,128)(2,1)S(1)} %copy-done.3, bf16[256,2048]{1,0:T(8,128)(2,1)} %bitcast.refs_2_, bf16[256,2048]{1,0:T(8,128)(2,1)} %bitcast.1.refs_3_, ...), custom_call_target="tpu_custom_call" | custom-call | flops 999999995904 | tf_op jit(solution)/shard_map/pallas_call | solution.py:77
  23.3 9.6 %collective-permute-done.3 = bf16[2,128,2048]{2,1,0:T(8,128)(2,1)} collective-permute-done((bf16[2,128,2048]{2,1,0:T(8,128)(2,1)}, bf16[2,128,2048]{2,1,0:T(8,128)(2,1)}, u32[]{:S(2)}, u32[]{:S(2)}) %collective-permute-start.3) | collective-permute-done | bytes 1048608 | tf_op jit(solution)/shard_map/ppermute | solution.py:30
  33.8 2.5 %shard_map.88 = (f32[384,128]{1,0:T(8,128)S(1)}, bf16[384,128]{1,0:T(8,128)(2,1)}, f32[8,128]{1,0:T(8,128)S(1)}) custom-call(s32[384,128]{1,0:T(8,128)S(1)} %copy-done.1, bf16[384,2048]{1,0:T(8,128)(2,1)S(1)} %copy-done.3, bf16[256,2048]{1,0:T(8,128)(2,1)} %bitcast.2.refs_2_, f32[384,128]{1,0:T(8,128)S(1)} %get-tuple-element.694.refs_3_, ...), custom_call_target="tpu_custom_call" | custom-call | flops 999999995904 | tf_op jit(solution)/shard_map/pallas_call | solution.py:77
  36.6 2.5 %shard_map.90 = (f32[384,128]{1,0:T(8,128)S(1)}, bf16[384,128]{1,0:T(8,128)(2,1)}, f32[8,128]{1,0:T(8,128)S(1)}) custom-call(s32[384,128]{1,0:T(8,128)S(1)} %copy-done.1, bf16[384,2048]{1,0:T(8,128)(2,1)S(1)} %copy-done.3, bf16[256,2048]{1,0:T(8,128)(2,1)} %bitcast.3.refs_2_, f32[384,128]{1,0:T(8,128)S(1)} %get-tuple-element.707.refs_3_, ...), custom_call_target="tpu_custom_call" | custom-call | flops 999999995904 | tf_op jit(solution)/shard_map/pallas_call | solution.py:77
  41.4 1.7 %collective-permute-start.13 = (bf16[160,2048]{1,0:T(8,128)(2,1)}, bf16[160,2048]{1,0:T(8,128)(2,1)}, u32[]{:S(2)}, u32[]{:S(2)}) collective-permute-start(bf16[160,2048]{1,0:T(8,128)(2,1)} %get-tuple-element.732), channel_id=1, source_target_pairs={{0,4},{4,0},{8,12},{12,8},{1,5},{5,1},{9,13},{13,9},{2,6},{6,2},{1... | collective-permute-start | bytes 1966088 | tf_op jit(solution)/shard_map/ppermute | solution.py:57
  44.2 2.2 %shard_map.99 = (bf16[224,2048]{1,0:T(8,128)(2,1)}, f32[8,128]{1,0:T(8,128)S(1)}) custom-call(bf16[384,2048]{1,0:T(8,128)(2,1)} %collective-permute-done.refs_1_.refs_0_.refs_4_, f32[8,128]{1,0:T(8,128)S(1)} %shard_map.98.refs_1_), custom_call_target="tpu_custom_call" | custom-call | flops 999999995904 | tf_op jit(solution)/shard_map/pallas_call | solution.py:77
  46.4 2.0 %collective-permute-done.10.refs_6_.refs_10_ = bf16[128,2048]{1,0:T(8,128)(2,1)} collective-permute-done((bf16[128,2048]{1,0:T(8,128)(2,1)}, bf16[128,2048]{1,0:T(8,128)(2,1)}, u32[]{:S(2)}, u32[]{:S(2)}) %collective-permute-start.10) | collective-permute-done | bytes 524320 | tf_op jit(solution)/shard_map/ppermute | solution.py:40
  49.9 4.7 %shard_map.103 = (f32[384,1024]{1,0:T(8,128)S(1)}, f32[8,128]{1,0:T(8,128)S(1)}) custom-call(f32[384,1024]{1,0:T(8,128)} %copy-done.6, bf16[8192,1024]{1,0:T(8,128)(2,1)} %refs_13_.1, bf16[128,2048]{1,0:T(8,128)(2,1)} %collective-permute-done.2.refs_2_.refs_1_.refs_3_, bf16[256,2048]{1,0:T(8,128)(2,1)} %collective-permute-done.5.refs_3_.refs_11_, ...), custom_call_target="tpu_custom_call" | custom-call | flops 999999995904 | tf_op jit(solution)/shard_map/pallas_call | solution.py:77
  56.2 3.2 %collective-permute-done.13.refs_1_.refs_7_.refs_12_ = bf16[160,2048]{1,0:T(8,128)(2,1)} collective-permute-done((bf16[160,2048]{1,0:T(8,128)(2,1)}, bf16[160,2048]{1,0:T(8,128)(2,1)}, u32[]{:S(2)}, u32[]{:S(2)}) %collective-permute-start.13) | collective-permute-done | bytes 655392 | tf_op jit(solution)/shard_map/ppermute | solution.py:57
  59.4 2.0 %shard_map.106 = (bf16[384,128]{1,0:T(8,128)(2,1)}, bf16[128,2048]{1,0:T(8,128)(2,1)}, f32[8,128]{1,0:T(8,128)S(1)}) custom-call(f32[384,128]{1,0:T(8,128)S(1)} %copy-done.8, bf16[160,2048]{1,0:T(8,128)(2,1)} %collective-permute-done.13.refs_1_.refs_7_.refs_12_, f32[8,128]{1,0:T(8,128)S(1)} %shard_map.105.refs_2_), custom_call_target="tpu_custom_call" | custom-call | flops 999999995904 | tf_op jit(solution)/shard_map/pallas_call | solution.py:77
  62.0 2.0 %collective-permute-start.18 = (bf16[2,128,1024]{2,1,0:T(8,128)(2,1)}, bf16[2,128,1024]{2,1,0:T(8,128)(2,1)}, u32[]{:S(2)}, u32[]{:S(2)}) collective-permute-start(bf16[2,128,1024]{2,1,0:T(8,128)(2,1)} %param.13), channel_id=1, source_target_pairs={{0,2},{2,0},{1,3},{3,1},{4,6},{6,4},{5,7},{7,5},{8,10},{10,8},{9,1... | collective-permute-start | bytes 1572872 | tf_op jit(solution)/shard_map/ppermute | solution.py:30
  66.3 1.6 %shard_map.114 = (bf16[384,128]{1,0:T(8,128)(2,1)}, f32[8,128]{1,0:T(8,128)S(1)}) custom-call(bf16[384,128]{1,0:T(8,128)(2,1)} %get-tuple-element.1017.refs_0_, bf16[384,128]{1,0:T(8,128)(2,1)} %collective-permute-done.15.refs_1_, f32[8,128]{1,0:T(8,128)S(1)} %shard_map.113.refs_2_), custom_call_target="tpu_custom_call" | custom-call | flops 999999995904 | tf_op jit(solution)/shard_map/pallas_call | solution.py:77
  69.2 9.9 %collective-permute-done.17.refs_8_ = bf16[224,2048]{1,0:T(8,128)(2,1)} collective-permute-done((bf16[224,2048]{1,0:T(8,128)(2,1)}, bf16[224,2048]{1,0:T(8,128)(2,1)}, u32[]{:S(2)}, u32[]{:S(2)}) %collective-permute-start.17) | collective-permute-done | bytes 917536 | tf_op jit(solution)/shard_map/ppermute | solution.py:57
  82.1 1.4 %collective-permute-start.23 = (bf16[128,1024]{1,0:T(8,128)(2,1)}, bf16[128,1024]{1,0:T(8,128)(2,1)}, u32[]{:S(2)}, u32[]{:S(2)}) collective-permute-start(bf16[128,1024]{1,0:T(8,128)(2,1)} %get-tuple-element.1079), channel_id=1, source_target_pairs={{4,0},{8,12},{5,1},{9,13},{6,2},{10,14},{7,3},{11,15},{20,16},{24,... | collective-permute-start | bytes 786440 | tf_op jit(solution)/shard_map/ppermute | solution.py:57
  83.5 7.4 %shard_map.121 = (bf16[384,1024]{1,0:T(8,128)(2,1)}, f32[384,1024]{1,0:T(8,128)}, f32[8,128]{1,0:T(8,128)S(1)}) custom-call(bf16[384,128]{1,0:T(8,128)(2,1)} %get-tuple-element.1098.refs_0_, s32[384,128]{1,0:T(8,128)S(1)} %copy-done.2, bf16[256,1024]{1,0:T(8,128)(2,1)} %bitcast.4.refs_2_, bf16[256,1024]{1,0:T(8,128)(2,1)} %bitcast.5.refs_3_, ...), custom_call_target="tpu_custom_call" | custom-call | flops 999999995904 | tf_op jit(solution)/shard_map/pallas_call | solution.py:77
  90.9 1.4 %collective-permute-done.22.refs_3_ = bf16[384,128]{1,0:T(8,128)(2,1)} collective-permute-done((bf16[384,128]{1,0:T(8,128)(2,1)}, bf16[384,128]{1,0:T(8,128)(2,1)}, u32[]{:S(2)}, u32[]{:S(2)}) %collective-permute-start.22) | collective-permute-done | bytes 98336 | tf_op jit(solution)/shard_map/ppermute | solution.py:57
  92.3 3.9 %shard_map.124 = (bf16[384,1024]{1,0:T(8,128)(2,1)}, f32[128,1024]{1,0:T(8,128)S(1)}, f32[8,128]{1,0:T(8,128)S(1)}) custom-call(bf16[384,1024]{1,0:T(8,128)(2,1)} %get-tuple-element.1111.refs_0_, f32[384,1024]{1,0:T(8,128)S(1)} %copy-done.5, bf16[256,1024]{1,0:T(8,128)(2,1)} %collective-permute-done.21.refs_2_, ...), custom_call_target="tpu_custom_call", output_to_operand_aliasing={{0}: (0, {})} | custom-call | flops 999999995904 | tf_op jit(solution)/shard_map/pallas_call | solution.py:77
  96.6 2.3 %shard_map.127 = (bf16[384,1024]{1,0:T(8,128)(2,1)}, f32[8,128]{1,0:T(8,128)}) custom-call(bf16[384,1024]{1,0:T(8,128)(2,1)} %get-tuple-element.1144.refs_0_, f32[128,1024]{1,0:T(8,128)S(1)} %get-tuple-element.1145.refs_1_, bf16[128,1024]{1,0:T(8,128)(2,1)} %collective-permute-done.23.refs_2_, ...), custom_call_target="tpu_custom_call", output_to_operand_aliasing={{0}: (0, {})} | custom-call | flops 999999995904 | tf_op jit(solution)/shard_map/pallas_call | solution.py:77
  (107 shorter events, 18.5 us)
Async XLA Ops:
  0.0 39.1 %collective-permute-start = (bf16[384,2048]{1,0:T(8,128)(2,1)}, bf16[384,2048]{1,0:T(8,128)(2,1)}, u32[]{:S(2)}, u32[]{:S(2)}) collective-permute-start(bf16[384,2048]{1,0:T(8,128)(2,1)} %refs_0_.4), channel_id=1, source_target_pairs={{0,1},{1,0},{2,3},{3,2},{4,8},{5,9},{6,10},{7,11},{8,4},{9,5},{10,... | collective-permute-start | bytes 4718600 | tf_op jit(solution)/shard_map/ppermute | solution.py:40
  3.7 16.4 %collective-permute-start.2 = (bf16[128,2048]{1,0:T(8,128)(2,1)}, bf16[128,2048]{1,0:T(8,128)(2,1)}, u32[]{:S(2)}, u32[]{:S(2)}) collective-permute-start(bf16[128,2048]{1,0:T(8,128)(2,1)} %get-tuple-element.638), channel_id=1, source_target_pairs={{0,4},{4,0},{8,12},{12,8},{1,5},{5,1},{9,13},{13,9},{2,6},{6,2},{1... | collective-permute-start | bytes 1572872 | tf_op jit(solution)/shard_map/ppermute | solution.py:57
  7.0 3.0 %collective-permute-start.1 = (bf16[2,128,2048]{2,1,0:T(8,128)(2,1)}, bf16[2,128,2048]{2,1,0:T(8,128)(2,1)}, u32[]{:S(2)}, u32[]{:S(2)}) collective-permute-start(bf16[2,128,2048]{2,1,0:T(8,128)(2,1)} %param.12), channel_id=1, source_target_pairs={{0,1},{1,0},{2,3},{3,2},{4,5},{5,4},{6,7},{7,6},{8,9},{9,8},{10,11... | collective-permute-start | bytes 3145736 | tf_op jit(solution)/shard_map/ppermute | solution.py:30
  7.0 25.9 %collective-permute-start.3 = (bf16[2,128,2048]{2,1,0:T(8,128)(2,1)}, bf16[2,128,2048]{2,1,0:T(8,128)(2,1)}, u32[]{:S(2)}, u32[]{:S(2)}) collective-permute-start(bf16[2,128,2048]{2,1,0:T(8,128)(2,1)} %param.12), channel_id=1, source_target_pairs={{0,2},{2,0},{1,3},{3,1},{4,6},{6,4},{5,7},{7,5},{8,10},{10,8},{9,1... | collective-permute-start | bytes 3145736 | tf_op jit(solution)/shard_map/ppermute | solution.py:30
  10.0 31.4 %collective-permute-start.5 = (bf16[256,2048]{1,0:T(8,128)(2,1)}, bf16[256,2048]{1,0:T(8,128)(2,1)}, u32[]{:S(2)}, u32[]{:S(2)}) collective-permute-start(bf16[256,2048]{1,0:T(8,128)(2,1)} %get-tuple-element.639), channel_id=1, source_target_pairs={{0,4},{4,0},{8,12},{12,8},{1,5},{5,1},{9,13},{13,9},{2,6},{6,2},{1... | collective-permute-start | bytes 3145736 | tf_op jit(solution)/shard_map/ppermute | solution.py:57
  20.1 20.6 %collective-permute-start.6 = (bf16[128,2048]{1,0:T(8,128)(2,1)}, bf16[128,2048]{1,0:T(8,128)(2,1)}, u32[]{:S(2)}, u32[]{:S(2)}) collective-permute-start(bf16[128,2048]{1,0:T(8,128)(2,1)} %collective-permute-done.2.refs_2_.refs_1_.refs_3_), channel_id=1, source_target_pairs={{0,1},{1,0},{2,3},{3,2},{4,20},{5,21},{6,22},{7,23},{8,24},{9,25},... | collective-permute-start | bytes 1572872 | tf_op jit(solution)/shard_map/ppermute | solution.py:40
  32.9 10.3 %collective-permute-start.8 = (bf16[128,2048]{1,0:T(8,128)(2,1)}, bf16[128,2048]{1,0:T(8,128)(2,1)}, u32[]{:S(2)}, u32[]{:S(2)}) collective-permute-start(bf16[128,2048]{1,0:T(8,128)(2,1)} %collective-permute-done.2.refs_2_.refs_1_.refs_3_), channel_id=1, source_target_pairs={{0,1},{1,0},{2,3},{3,2},{4,6},{5,7},{6,4},{7,5},{8,10},{9,11},{10,... | collective-permute-start | bytes 1572872 | tf_op jit(solution)/shard_map/ppermute | solution.py:40
  32.9 3.7 %collective-permute-start.4 = (bf16[2,128,2048]{2,1,0:T(8,128)(2,1)}, bf16[2,128,2048]{2,1,0:T(8,128)(2,1)}, u32[]{:S(2)}, u32[]{:S(2)}) collective-permute-start(bf16[2,128,2048]{2,1,0:T(8,128)(2,1)} %collective-permute-done.3), channel_id=1, source_target_pairs={{0,1},{1,0},{2,3},{3,2},{4,5},{5,4},{6,7},{7,6},{8,9},{9,8},{10,11... | collective-permute-start | bytes 3145736 | tf_op jit(solution)/shard_map/ppermute | solution.py:30
  41.4 18.0 %collective-permute-start.13 = (bf16[160,2048]{1,0:T(8,128)(2,1)}, bf16[160,2048]{1,0:T(8,128)(2,1)}, u32[]{:S(2)}, u32[]{:S(2)}) collective-permute-start(bf16[160,2048]{1,0:T(8,128)(2,1)} %get-tuple-element.732), channel_id=1, source_target_pairs={{0,4},{4,0},{8,12},{12,8},{1,5},{5,1},{9,13},{13,9},{2,6},{6,2},{1... | collective-permute-start | bytes 1966088 | tf_op jit(solution)/shard_map/ppermute | solution.py:57
  43.2 20.8 %collective-permute-start.7 = (bf16[256,2048]{1,0:T(8,128)(2,1)}, bf16[256,2048]{1,0:T(8,128)(2,1)}, u32[]{:S(2)}, u32[]{:S(2)}) collective-permute-start(bf16[256,2048]{1,0:T(8,128)(2,1)} %collective-permute-done.5.refs_3_.refs_11_), channel_id=1, source_target_pairs={{0,1},{1,0},{2,3},{3,2},{4,8},{5,9},{6,10},{7,11},{8,4},{9,5},{10,... | collective-permute-start | bytes 3145736 | tf_op jit(solution)/shard_map/ppermute | solution.py:40
  43.2 12.6 %collective-permute-start.11 = (bf16[128,2048]{1,0:T(8,128)(2,1)}, bf16[128,2048]{1,0:T(8,128)(2,1)}, u32[]{:S(2)}, u32[]{:S(2)}) collective-permute-start(bf16[128,2048]{1,0:T(8,128)(2,1)} %collective-permute-done.8.refs_3_.refs_7_), channel_id=1, source_target_pairs={{0,1},{1,0},{2,3},{3,2},{4,20},{5,21},{6,22},{7,23},{8,24},{9,25},... | collective-permute-start | bytes 1572872 | tf_op jit(solution)/shard_map/ppermute | solution.py:40
  43.7 4.7 %collective-permute-start.9 = (bf16[128,2048]{1,0:T(8,128)(2,1)}, bf16[128,2048]{1,0:T(8,128)(2,1)}, u32[]{:S(2)}, u32[]{:S(2)}) collective-permute-start(bf16[128,2048]{1,0:T(8,128)(2,1)} %collective-permute-done.2.refs_2_.refs_1_.refs_3_), channel_id=1, source_target_pairs={{0,1},{1,0},{2,3},{3,2},{4,5},{5,4},{6,7},{7,6},{8,9},{9,8},{10,11... | collective-permute-start | bytes 1572872 | tf_op jit(solution)/shard_map/ppermute | solution.py:40
  43.8 4.7 %collective-permute-start.10 = (bf16[128,2048]{1,0:T(8,128)(2,1)}, bf16[128,2048]{1,0:T(8,128)(2,1)}, u32[]{:S(2)}, u32[]{:S(2)}) collective-permute-start(bf16[128,2048]{1,0:T(8,128)(2,1)} %collective-permute-done.6.refs_5_.refs_9_), channel_id=1, source_target_pairs={{0,1},{1,0},{2,3},{3,2},{4,5},{5,4},{6,7},{7,6},{8,9},{9,8},{10,11... | collective-permute-start | bytes 1572872 | tf_op jit(solution)/shard_map/ppermute | solution.py:40
  48.4 30.6 %collective-permute-start.17 = (bf16[224,2048]{1,0:T(8,128)(2,1)}, bf16[224,2048]{1,0:T(8,128)(2,1)}, u32[]{:S(2)}, u32[]{:S(2)}) collective-permute-start(bf16[224,2048]{1,0:T(8,128)(2,1)} %get-tuple-element.836), channel_id=1, source_target_pairs={{4,0},{8,12},{5,1},{9,13},{6,2},{10,14},{7,3},{11,15},{20,16},{24,... | collective-permute-start | bytes 2752520 | tf_op jit(solution)/shard_map/ppermute | solution.py:57
  49.7 6.1 %collective-permute-start.12 = (bf16[128,2048]{1,0:T(8,128)(2,1)}, bf16[128,2048]{1,0:T(8,128)(2,1)}, u32[]{:S(2)}, u32[]{:S(2)}) collective-permute-start(bf16[128,2048]{1,0:T(8,128)(2,1)} %collective-permute-done.8.refs_3_.refs_7_), channel_id=1, source_target_pairs={{0,1},{1,0},{2,3},{3,2},{4,5},{5,4},{6,7},{7,6},{8,9},{9,8},{10,11... | collective-permute-start | bytes 1572872 | tf_op jit(solution)/shard_map/ppermute | solution.py:40
  55.8 3.6 %collective-permute-start.14 = (bf16[128,2048]{1,0:T(8,128)(2,1)}, bf16[128,2048]{1,0:T(8,128)(2,1)}, u32[]{:S(2)}, u32[]{:S(2)}) collective-permute-start(bf16[128,2048]{1,0:T(8,128)(2,1)} %collective-permute-done.11.refs_7_.refs_5_), channel_id=1, source_target_pairs={{0,1},{1,0},{2,3},{3,2},{4,5},{5,4},{6,7},{7,6},{8,9},{9,8},{10,11... | collective-permute-start | bytes 1572872 | tf_op jit(solution)/shard_map/ppermute | solution.py:40
  61.4 3.6 %collective-permute-start.15 = (bf16[384,128]{1,0:T(8,128)(2,1)}, bf16[384,128]{1,0:T(8,128)(2,1)}, u32[]{:S(2)}, u32[]{:S(2)}) collective-permute-start(bf16[384,128]{1,0:T(8,128)(2,1)} %get-tuple-element.1017.refs_0_), channel_id=1, source_target_pairs={{0,1},{1,0},{2,3},{3,2},{4,8},{5,9},{6,10},{7,11},{8,4},{9,5},{10,... | collective-permute-start | bytes 294920 | tf_op jit(solution)/shard_map/ppermute | solution.py:40
  61.5 17.6 %collective-permute-start.16 = (bf16[128,2048]{1,0:T(8,128)(2,1)}, bf16[128,2048]{1,0:T(8,128)(2,1)}, u32[]{:S(2)}, u32[]{:S(2)}) collective-permute-start(bf16[128,2048]{1,0:T(8,128)(2,1)} %get-tuple-element.943), channel_id=1, source_target_pairs={{0,1},{1,0},{2,3},{3,2},{4,8},{5,9},{6,10},{7,11},{8,4},{9,5},{10,... | collective-permute-start | bytes 1572872 | tf_op jit(solution)/shard_map/ppermute | solution.py:40
  62.0 17.1 %collective-permute-start.18 = (bf16[2,128,1024]{2,1,0:T(8,128)(2,1)}, bf16[2,128,1024]{2,1,0:T(8,128)(2,1)}, u32[]{:S(2)}, u32[]{:S(2)}) collective-permute-start(bf16[2,128,1024]{2,1,0:T(8,128)(2,1)} %param.13), channel_id=1, source_target_pairs={{0,2},{2,0},{1,3},{3,1},{4,6},{6,4},{5,7},{7,5},{8,10},{10,8},{9,1... | collective-permute-start | bytes 1572872 | tf_op jit(solution)/shard_map/ppermute | solution.py:30
  65.0 27.4 %collective-permute-start.21 = (bf16[256,1024]{1,0:T(8,128)(2,1)}, bf16[256,1024]{1,0:T(8,128)(2,1)}, u32[]{:S(2)}, u32[]{:S(2)}) collective-permute-start(bf16[256,1024]{1,0:T(8,128)(2,1)} %get-tuple-element.990), channel_id=1, source_target_pairs={{4,0},{8,12},{5,1},{9,13},{6,2},{10,14},{7,3},{11,15},{20,16},{24,... | collective-permute-start | bytes 1572872 | tf_op jit(solution)/shard_map/ppermute | solution.py:57
  67.9 24.4 %collective-permute-start.22 = (bf16[384,128]{1,0:T(8,128)(2,1)}, bf16[384,128]{1,0:T(8,128)(2,1)}, u32[]{:S(2)}, u32[]{:S(2)}) collective-permute-start(bf16[384,128]{1,0:T(8,128)(2,1)} %get-tuple-element.1098.refs_0_), channel_id=1, source_target_pairs={{4,0},{8,12},{5,1},{9,13},{6,2},{10,14},{7,3},{11,15},{20,16},{24,... | collective-permute-start | bytes 294920 | tf_op jit(solution)/shard_map/ppermute | solution.py:57
  79.0 2.3 %collective-permute-start.19 = (bf16[2,128,1024]{2,1,0:T(8,128)(2,1)}, bf16[2,128,1024]{2,1,0:T(8,128)(2,1)}, u32[]{:S(2)}, u32[]{:S(2)}) collective-permute-start(bf16[2,128,1024]{2,1,0:T(8,128)(2,1)} %param.13), channel_id=1, source_target_pairs={{0,1},{1,0},{2,3},{3,2},{4,5},{5,4},{6,7},{7,6},{8,9},{9,8},{10,11... | collective-permute-start | bytes 1572872 | tf_op jit(solution)/shard_map/ppermute | solution.py:30
  79.1 3.0 %collective-permute-start.20 = (bf16[2,128,1024]{2,1,0:T(8,128)(2,1)}, bf16[2,128,1024]{2,1,0:T(8,128)(2,1)}, u32[]{:S(2)}, u32[]{:S(2)}) collective-permute-start(bf16[2,128,1024]{2,1,0:T(8,128)(2,1)} %collective-permute-done.18), channel_id=1, source_target_pairs={{0,1},{1,0},{2,3},{3,2},{4,5},{5,4},{6,7},{7,6},{8,9},{9,8},{10,11... | collective-permute-start | bytes 1572872 | tf_op jit(solution)/shard_map/ppermute | solution.py:30
  82.1 14.6 %collective-permute-start.23 = (bf16[128,1024]{1,0:T(8,128)(2,1)}, bf16[128,1024]{1,0:T(8,128)(2,1)}, u32[]{:S(2)}, u32[]{:S(2)}) collective-permute-start(bf16[128,1024]{1,0:T(8,128)(2,1)} %get-tuple-element.1079), channel_id=1, source_target_pairs={{4,0},{8,12},{5,1},{9,13},{6,2},{10,14},{7,3},{11,15},{20,16},{24,... | collective-permute-start | bytes 786440 | tf_op jit(solution)/shard_map/ppermute | solution.py:57
  (12 other events, 19.5 us)

commit v6 on v5

--- a/solution.py
+++ b/solution.py
@@ -698,9 +698,9 @@
     fence(h)
     first_p = hop(h["first"], PAIRS)
     fence(h)
+    down_x = swap(h["down"], "pool")
+    fence(h)
     down_c = swap(h["down"], "inner")
-    fence(h)
-    down_x = swap(h["down"], "pool")
     fence(h)
     h["later"] = later_rows(h, h["tokens"], layout)
     h["down_c"] = down_c

time: 99.8 us -> 99.3 us (level)
  waiting for transfers between devices: 34.2 us -> 32.8 us
  local copies, waits for them, and re-layouts: 4.76 us -> 5.76 us
    ppermute x7, waiting for transfers between devices: 20.3 us -> 18.6 us  [hop(): return lax.ppermute(x, 'tensor', pairs)]
    unnamed x24, local copies, waits for them, and re-layouts: 4.76 us -> 5.76 us
  transfers between devices with their start and end apart: 24 -> 24, of which waited for: 12 -> 11; matrix products, arithmetic and copies ran while one was open for 0% -> 0% of each run, Pallas kernels for 40% -> 40%
where the time goes in v6:
time: 99.3 us; the launch traced here: 98.7 us
  Pallas kernels  41.8 us (42%)
  waiting for transfers between devices  32.8 us (33%)
  starting transfers between devices  17.4 us (18%)
  local copies, waits for them, and re-layouts  5.76 us (6%)
    pallas_call x55, Pallas kernels, call(): pl.pallas_call(counted, out_shape=[*shapes, jax.ShapeDtypeStruct(tick.sha...  41.8 us
    ppermute x7, waiting for transfers between devices, hop(): return lax.ppermute(x, 'tensor', pairs)  18.6 us
    ppermute x6, waiting for transfers between devices, swap(): return lax.ppermute(x, axis, [(0, 1), (1, 0)])  12.2 us
    ppermute x7, starting transfers between devices, hop(): return lax.ppermute(x, 'tensor', pairs)  10.3 us
    unnamed x24, local copies, waits for them, and re-layouts  5.76 us
    ppermute x6, starting transfers between devices, swap(): return lax.ppermute(x, axis, [(0, 1), (1, 0)])  4.48 us
    ppermute x11, starting transfers between devices, inside(): return lax.ppermute(x, AXES, pairs)  2.61 us
    ppermute x11, waiting for transfers between devices, inside(): return lax.ppermute(x, AXES, pairs)  2.04 us
  transfers between devices with their start and end apart: 24, of which 11 were waited for; matrix products, arithmetic and copies ran while one was open for 0% of the time, Pallas kernels for 40%

profile of v6, /device:TPU:0, one launch (start us, length us, event | category | flops | bytes accessed | tf_op | source)
XLA Modules:
  0.0 98.7 jit_solution(16920323414682436787)
XLA Ops:
  1.9 1.8 %shard_map.73 = (bf16[128,2048]{1,0:T(8,128)(2,1)}, f32[8,128]{1,0:T(8,128)S(1)}) custom-call(bf16[384,2048]{1,0:T(8,128)(2,1)S(1)} %copy-done.3, bf16[8192,1024]{1,0:T(8,128)(2,1)} %refs_13_.1, f32[8,128]{1,0:T(8,128)S(1)} %broadcast_in_dim.34.refs_2_), custom_call_target="tpu_custom_call" | custom-call | flops 999999995904 | tf_op jit(solution)/shard_map/pallas_call | solution.py:77
  3.7 3.3 %collective-permute-start.2 = (bf16[128,2048]{1,0:T(8,128)(2,1)}, bf16[128,2048]{1,0:T(8,128)(2,1)}, u32[]{:S(2)}, u32[]{:S(2)}) collective-permute-start(bf16[128,2048]{1,0:T(8,128)(2,1)} %get-tuple-element.638), channel_id=1, source_target_pairs={{0,4},{4,0},{8,12},{12,8},{1,5},{5,1},{9,13},{13,9},{2,6},{6,2},{1... | collective-permute-start | bytes 1572872 | tf_op jit(solution)/shard_map/ppermute | solution.py:57
  7.0 1.5 %collective-permute-start.3 = (bf16[2,128,2048]{2,1,0:T(8,128)(2,1)}, bf16[2,128,2048]{2,1,0:T(8,128)(2,1)}, u32[]{:S(2)}, u32[]{:S(2)}) collective-permute-start(bf16[2,128,2048]{2,1,0:T(8,128)(2,1)} %param.12), channel_id=1, source_target_pairs={{0,2},{2,0},{1,3},{3,1},{4,6},{6,4},{5,7},{7,5},{8,10},{10,8},{9,1... | collective-permute-start | bytes 3145736 | tf_op jit(solution)/shard_map/ppermute | solution.py:30
  9.6 1.9 %collective-permute-done.1 = bf16[2,128,2048]{2,1,0:T(8,128)(2,1)} collective-permute-done((bf16[2,128,2048]{2,1,0:T(8,128)(2,1)}, bf16[2,128,2048]{2,1,0:T(8,128)(2,1)}, u32[]{:S(2)}, u32[]{:S(2)}) %collective-permute-start.1) | collective-permute-done | bytes 1048608 | tf_op jit(solution)/shard_map/ppermute | solution.py:30
  11.6 3.8 %shard_map.81 = (f32[384,1024]{1,0:T(8,128)S(1)}, f32[8,128]{1,0:T(8,128)S(1)}) custom-call(bf16[384,2048]{1,0:T(8,128)(2,1)S(1)} %copy-done.3, bf16[8192,1024]{1,0:T(8,128)(2,1)} %refs_13_.1, f32[8,128]{1,0:T(8,128)S(1)} %shard_map.80.refs_2_), custom_call_target="tpu_custom_call" | custom-call | flops 999999995904 | tf_op jit(solution)/shard_map/pallas_call | solution.py:77
  16.8 3.3 %collective-permute-done.2.refs_2_.refs_1_.refs_3_ = bf16[128,2048]{1,0:T(8,128)(2,1)} collective-permute-done((bf16[128,2048]{1,0:T(8,128)(2,1)}, bf16[128,2048]{1,0:T(8,128)(2,1)}, u32[]{:S(2)}, u32[]{:S(2)}) %collective-permute-start.2) | collective-permute-done | bytes 524320 | tf_op jit(solution)/shard_map/ppermute | solution.py:57
  20.1 3.2 %shard_map.84 = (f32[384,128]{1,0:T(8,128)S(1)}, bf16[384,128]{1,0:T(8,128)(2,1)}, f32[8,128]{1,0:T(8,128)S(1)}) custom-call(s32[384,128]{1,0:T(8,128)S(1)} %fusion.refs_0_.refs_1_.refs_4_, bf16[384,2048]{1,0:T(8,128)(2,1)S(1)} %copy-done.3, bf16[256,2048]{1,0:T(8,128)(2,1)} %bitcast.refs_2_, bf16[256,2048]{1,0:T(8,128)(2,1)} %bitcast.1.refs_3_, ...), custom_call_target="tpu_custom_call" | custom-call | flops 999999995904 | tf_op jit(solution)/shard_map/pallas_call | solution.py:77
  23.3 8.3 %collective-permute-done.3 = bf16[2,128,2048]{2,1,0:T(8,128)(2,1)} collective-permute-done((bf16[2,128,2048]{2,1,0:T(8,128)(2,1)}, bf16[2,128,2048]{2,1,0:T(8,128)(2,1)}, u32[]{:S(2)}, u32[]{:S(2)}) %collective-permute-start.3) | collective-permute-done | bytes 1048608 | tf_op jit(solution)/shard_map/ppermute | solution.py:30
  32.6 2.5 %shard_map.88 = (f32[384,128]{1,0:T(8,128)S(1)}, bf16[384,128]{1,0:T(8,128)(2,1)}, f32[8,128]{1,0:T(8,128)S(1)}) custom-call(s32[384,128]{1,0:T(8,128)S(1)} %copy-done.1, bf16[384,2048]{1,0:T(8,128)(2,1)S(1)} %copy-done.3, bf16[256,2048]{1,0:T(8,128)(2,1)} %bitcast.2.refs_2_, f32[384,128]{1,0:T(8,128)S(1)} %get-tuple-element.694.refs_3_, ...), custom_call_target="tpu_custom_call" | custom-call | flops 999999995904 | tf_op jit(solution)/shard_map/pallas_call | solution.py:77
  35.4 2.5 %shard_map.90 = (f32[384,128]{1,0:T(8,128)S(1)}, bf16[384,128]{1,0:T(8,128)(2,1)}, f32[8,128]{1,0:T(8,128)S(1)}) custom-call(s32[384,128]{1,0:T(8,128)S(1)} %copy-done.1, bf16[384,2048]{1,0:T(8,128)(2,1)S(1)} %copy-done.3, bf16[256,2048]{1,0:T(8,128)(2,1)} %bitcast.3.refs_2_, f32[384,128]{1,0:T(8,128)S(1)} %get-tuple-element.707.refs_3_, ...), custom_call_target="tpu_custom_call" | custom-call | flops 999999995904 | tf_op jit(solution)/shard_map/pallas_call | solution.py:77
  39.5 1.9 %collective-permute-done.5.refs_3_.refs_11_ = bf16[256,2048]{1,0:T(8,128)(2,1)} collective-permute-done((bf16[256,2048]{1,0:T(8,128)(2,1)}, bf16[256,2048]{1,0:T(8,128)(2,1)}, u32[]{:S(2)}, u32[]{:S(2)}) %collective-permute-start.5) | collective-permute-done | bytes 1048608 | tf_op jit(solution)/shard_map/ppermute | solution.py:57
  41.4 1.7 %collective-permute-start.13 = (bf16[160,2048]{1,0:T(8,128)(2,1)}, bf16[160,2048]{1,0:T(8,128)(2,1)}, u32[]{:S(2)}, u32[]{:S(2)}) collective-permute-start(bf16[160,2048]{1,0:T(8,128)(2,1)} %get-tuple-element.732), channel_id=1, source_target_pairs={{0,4},{4,0},{8,12},{12,8},{1,5},{5,1},{9,13},{13,9},{2,6},{6,2},{1... | collective-permute-start | bytes 1966088 | tf_op jit(solution)/shard_map/ppermute | solution.py:57
  44.2 2.2 %shard_map.99 = (bf16[224,2048]{1,0:T(8,128)(2,1)}, f32[8,128]{1,0:T(8,128)S(1)}) custom-call(bf16[384,2048]{1,0:T(8,128)(2,1)} %collective-permute-done.refs_1_.refs_0_.refs_4_, f32[8,128]{1,0:T(8,128)S(1)} %shard_map.98.refs_1_), custom_call_target="tpu_custom_call" | custom-call | flops 999999995904 | tf_op jit(solution)/shard_map/pallas_call | solution.py:77
  46.4 2.0 %collective-permute-done.10.refs_6_.refs_10_ = bf16[128,2048]{1,0:T(8,128)(2,1)} collective-permute-done((bf16[128,2048]{1,0:T(8,128)(2,1)}, bf16[128,2048]{1,0:T(8,128)(2,1)}, u32[]{:S(2)}, u32[]{:S(2)}) %collective-permute-start.10) | collective-permute-done | bytes 524320 | tf_op jit(solution)/shard_map/ppermute | solution.py:40
  49.9 4.7 %shard_map.103 = (f32[384,1024]{1,0:T(8,128)S(1)}, f32[8,128]{1,0:T(8,128)S(1)}) custom-call(f32[384,1024]{1,0:T(8,128)} %copy-done.6, bf16[8192,1024]{1,0:T(8,128)(2,1)} %refs_13_.1, bf16[128,2048]{1,0:T(8,128)(2,1)} %collective-permute-done.2.refs_2_.refs_1_.refs_3_, bf16[256,2048]{1,0:T(8,128)(2,1)} %collective-permute-done.5.refs_3_.refs_11_, ...), custom_call_target="tpu_custom_call" | custom-call | flops 999999995904 | tf_op jit(solution)/shard_map/pallas_call | solution.py:77
  56.2 3.2 %collective-permute-done.13.refs_1_.refs_7_.refs_12_ = bf16[160,2048]{1,0:T(8,128)(2,1)} collective-permute-done((bf16[160,2048]{1,0:T(8,128)(2,1)}, bf16[160,2048]{1,0:T(8,128)(2,1)}, u32[]{:S(2)}, u32[]{:S(2)}) %collective-permute-start.13) | collective-permute-done | bytes 655392 | tf_op jit(solution)/shard_map/ppermute | solution.py:57
  59.4 2.0 %shard_map.106 = (bf16[384,128]{1,0:T(8,128)(2,1)}, bf16[128,2048]{1,0:T(8,128)(2,1)}, f32[8,128]{1,0:T(8,128)S(1)}) custom-call(f32[384,128]{1,0:T(8,128)S(1)} %copy-done.8, bf16[160,2048]{1,0:T(8,128)(2,1)} %collective-permute-done.13.refs_1_.refs_7_.refs_12_, f32[8,128]{1,0:T(8,128)S(1)} %shard_map.105.refs_2_), custom_call_target="tpu_custom_call" | custom-call | flops 999999995904 | tf_op jit(solution)/shard_map/pallas_call | solution.py:77
  62.0 2.0 %collective-permute-start.18 = (bf16[2,128,1024]{2,1,0:T(8,128)(2,1)}, bf16[2,128,1024]{2,1,0:T(8,128)(2,1)}, u32[]{:S(2)}, u32[]{:S(2)}) collective-permute-start(bf16[2,128,1024]{2,1,0:T(8,128)(2,1)} %param.13), channel_id=1, source_target_pairs={{0,2},{2,0},{1,3},{3,1},{4,6},{6,4},{5,7},{7,5},{8,10},{10,8},{9,1... | collective-permute-start | bytes 1572872 | tf_op jit(solution)/shard_map/ppermute | solution.py:30
  66.3 1.6 %shard_map.114 = (bf16[384,128]{1,0:T(8,128)(2,1)}, f32[8,128]{1,0:T(8,128)S(1)}) custom-call(bf16[384,128]{1,0:T(8,128)(2,1)} %get-tuple-element.1017.refs_0_, bf16[384,128]{1,0:T(8,128)(2,1)} %collective-permute-done.15.refs_1_, f32[8,128]{1,0:T(8,128)S(1)} %shard_map.113.refs_2_), custom_call_target="tpu_custom_call" | custom-call | flops 999999995904 | tf_op jit(solution)/shard_map/pallas_call | solution.py:77
  69.2 9.8 %collective-permute-done.17.refs_8_ = bf16[224,2048]{1,0:T(8,128)(2,1)} collective-permute-done((bf16[224,2048]{1,0:T(8,128)(2,1)}, bf16[224,2048]{1,0:T(8,128)(2,1)}, u32[]{:S(2)}, u32[]{:S(2)}) %collective-permute-start.17) | collective-permute-done | bytes 917536 | tf_op jit(solution)/shard_map/ppermute | solution.py:57
  81.9 1.4 %collective-permute-start.23 = (bf16[128,1024]{1,0:T(8,128)(2,1)}, bf16[128,1024]{1,0:T(8,128)(2,1)}, u32[]{:S(2)}, u32[]{:S(2)}) collective-permute-start(bf16[128,1024]{1,0:T(8,128)(2,1)} %get-tuple-element.1079), channel_id=1, source_target_pairs={{4,0},{8,12},{5,1},{9,13},{6,2},{10,14},{7,3},{11,15},{20,16},{24,... | collective-permute-start | bytes 786440 | tf_op jit(solution)/shard_map/ppermute | solution.py:57
  83.4 7.4 %shard_map.121 = (bf16[384,1024]{1,0:T(8,128)(2,1)}, f32[384,1024]{1,0:T(8,128)}, f32[8,128]{1,0:T(8,128)S(1)}) custom-call(bf16[384,128]{1,0:T(8,128)(2,1)} %get-tuple-element.1098.refs_0_, s32[384,128]{1,0:T(8,128)S(1)} %copy-done.2, bf16[256,1024]{1,0:T(8,128)(2,1)} %bitcast.4.refs_2_, bf16[256,1024]{1,0:T(8,128)(2,1)} %bitcast.5.refs_3_, ...), custom_call_target="tpu_custom_call" | custom-call | flops 999999995904 | tf_op jit(solution)/shard_map/pallas_call | solution.py:77
  92.2 3.9 %shard_map.124 = (bf16[384,1024]{1,0:T(8,128)(2,1)}, f32[128,1024]{1,0:T(8,128)S(1)}, f32[8,128]{1,0:T(8,128)S(1)}) custom-call(bf16[384,1024]{1,0:T(8,128)(2,1)} %get-tuple-element.1111.refs_0_, f32[384,1024]{1,0:T(8,128)S(1)} %copy-done.5, bf16[256,1024]{1,0:T(8,128)(2,1)} %collective-permute-done.21.refs_2_, ...), custom_call_target="tpu_custom_call", output_to_operand_aliasing={{0}: (0, {})} | custom-call | flops 999999995904 | tf_op jit(solution)/shard_map/pallas_call | solution.py:77
  96.2 2.4 %shard_map.127 = (bf16[384,1024]{1,0:T(8,128)(2,1)}, f32[8,128]{1,0:T(8,128)}) custom-call(bf16[384,1024]{1,0:T(8,128)(2,1)} %get-tuple-element.1144.refs_0_, f32[128,1024]{1,0:T(8,128)S(1)} %get-tuple-element.1145.refs_1_, bf16[128,1024]{1,0:T(8,128)(2,1)} %collective-permute-done.23.refs_2_, ...), custom_call_target="tpu_custom_call", output_to_operand_aliasing={{0}: (0, {})} | custom-call | flops 999999995904 | tf_op jit(solution)/shard_map/pallas_call | solution.py:77
  (107 shorter events, 19.8 us)
Async XLA Ops:
  0.0 37.9 %collective-permute-start = (bf16[384,2048]{1,0:T(8,128)(2,1)}, bf16[384,2048]{1,0:T(8,128)(2,1)}, u32[]{:S(2)}, u32[]{:S(2)}) collective-permute-start(bf16[384,2048]{1,0:T(8,128)(2,1)} %refs_0_.4), channel_id=1, source_target_pairs={{0,1},{1,0},{2,3},{3,2},{4,8},{5,9},{6,10},{7,11},{8,4},{9,5},{10,... | collective-permute-start | bytes 4718600 | tf_op jit(solution)/shard_map/ppermute | solution.py:40
  3.7 16.4 %collective-permute-start.2 = (bf16[128,2048]{1,0:T(8,128)(2,1)}, bf16[128,2048]{1,0:T(8,128)(2,1)}, u32[]{:S(2)}, u32[]{:S(2)}) collective-permute-start(bf16[128,2048]{1,0:T(8,128)(2,1)} %get-tuple-element.638), channel_id=1, source_target_pairs={{0,4},{4,0},{8,12},{12,8},{1,5},{5,1},{9,13},{13,9},{2,6},{6,2},{1... | collective-permute-start | bytes 1572872 | tf_op jit(solution)/shard_map/ppermute | solution.py:57
  7.0 24.7 %collective-permute-start.3 = (bf16[2,128,2048]{2,1,0:T(8,128)(2,1)}, bf16[2,128,2048]{2,1,0:T(8,128)(2,1)}, u32[]{:S(2)}, u32[]{:S(2)}) collective-permute-start(bf16[2,128,2048]{2,1,0:T(8,128)(2,1)} %param.12), channel_id=1, source_target_pairs={{0,2},{2,0},{1,3},{3,1},{4,6},{6,4},{5,7},{7,5},{8,10},{10,8},{9,1... | collective-permute-start | bytes 3145736 | tf_op jit(solution)/shard_map/ppermute | solution.py:30
  8.5 3.0 %collective-permute-start.1 = (bf16[2,128,2048]{2,1,0:T(8,128)(2,1)}, bf16[2,128,2048]{2,1,0:T(8,128)(2,1)}, u32[]{:S(2)}, u32[]{:S(2)}) collective-permute-start(bf16[2,128,2048]{2,1,0:T(8,128)(2,1)} %param.12), channel_id=1, source_target_pairs={{0,1},{1,0},{2,3},{3,2},{4,5},{5,4},{6,7},{7,6},{8,9},{9,8},{10,11... | collective-permute-start | bytes 3145736 | tf_op jit(solution)/shard_map/ppermute | solution.py:30
  11.5 29.9 %collective-permute-start.5 = (bf16[256,2048]{1,0:T(8,128)(2,1)}, bf16[256,2048]{1,0:T(8,128)(2,1)}, u32[]{:S(2)}, u32[]{:S(2)}) collective-permute-start(bf16[256,2048]{1,0:T(8,128)(2,1)} %get-tuple-element.639), channel_id=1, source_target_pairs={{0,4},{4,0},{8,12},{12,8},{1,5},{5,1},{9,13},{13,9},{2,6},{6,2},{1... | collective-permute-start | bytes 3145736 | tf_op jit(solution)/shard_map/ppermute | solution.py:57
  20.1 19.4 %collective-permute-start.6 = (bf16[128,2048]{1,0:T(8,128)(2,1)}, bf16[128,2048]{1,0:T(8,128)(2,1)}, u32[]{:S(2)}, u32[]{:S(2)}) collective-permute-start(bf16[128,2048]{1,0:T(8,128)(2,1)} %collective-permute-done.2.refs_2_.refs_1_.refs_3_), channel_id=1, source_target_pairs={{0,1},{1,0},{2,3},{3,2},{4,20},{5,21},{6,22},{7,23},{8,24},{9,25},... | collective-permute-start | bytes 1572872 | tf_op jit(solution)/shard_map/ppermute | solution.py:40
  31.6 11.5 %collective-permute-start.8 = (bf16[128,2048]{1,0:T(8,128)(2,1)}, bf16[128,2048]{1,0:T(8,128)(2,1)}, u32[]{:S(2)}, u32[]{:S(2)}) collective-permute-start(bf16[128,2048]{1,0:T(8,128)(2,1)} %collective-permute-done.2.refs_2_.refs_1_.refs_3_), channel_id=1, source_target_pairs={{0,1},{1,0},{2,3},{3,2},{4,6},{5,7},{6,4},{7,5},{8,10},{9,11},{10,... | collective-permute-start | bytes 1572872 | tf_op jit(solution)/shard_map/ppermute | solution.py:40
  31.7 3.7 %collective-permute-start.4 = (bf16[2,128,2048]{2,1,0:T(8,128)(2,1)}, bf16[2,128,2048]{2,1,0:T(8,128)(2,1)}, u32[]{:S(2)}, u32[]{:S(2)}) collective-permute-start(bf16[2,128,2048]{2,1,0:T(8,128)(2,1)} %collective-permute-done.3), channel_id=1, source_target_pairs={{0,1},{1,0},{2,3},{3,2},{4,5},{5,4},{6,7},{7,6},{8,9},{9,8},{10,11... | collective-permute-start | bytes 3145736 | tf_op jit(solution)/shard_map/ppermute | solution.py:30
  41.4 18.0 %collective-permute-start.13 = (bf16[160,2048]{1,0:T(8,128)(2,1)}, bf16[160,2048]{1,0:T(8,128)(2,1)}, u32[]{:S(2)}, u32[]{:S(2)}) collective-permute-start(bf16[160,2048]{1,0:T(8,128)(2,1)} %get-tuple-element.732), channel_id=1, source_target_pairs={{0,4},{4,0},{8,12},{12,8},{1,5},{5,1},{9,13},{13,9},{2,6},{6,2},{1... | collective-permute-start | bytes 1966088 | tf_op jit(solution)/shard_map/ppermute | solution.py:57
  43.2 20.8 %collective-permute-start.7 = (bf16[256,2048]{1,0:T(8,128)(2,1)}, bf16[256,2048]{1,0:T(8,128)(2,1)}, u32[]{:S(2)}, u32[]{:S(2)}) collective-permute-start(bf16[256,2048]{1,0:T(8,128)(2,1)} %collective-permute-done.5.refs_3_.refs_11_), channel_id=1, source_target_pairs={{0,1},{1,0},{2,3},{3,2},{4,8},{5,9},{6,10},{7,11},{8,4},{9,5},{10,... | collective-permute-start | bytes 3145736 | tf_op jit(solution)/shard_map/ppermute | solution.py:40
  43.2 12.6 %collective-permute-start.11 = (bf16[128,2048]{1,0:T(8,128)(2,1)}, bf16[128,2048]{1,0:T(8,128)(2,1)}, u32[]{:S(2)}, u32[]{:S(2)}) collective-permute-start(bf16[128,2048]{1,0:T(8,128)(2,1)} %collective-permute-done.8.refs_3_.refs_7_), channel_id=1, source_target_pairs={{0,1},{1,0},{2,3},{3,2},{4,20},{5,21},{6,22},{7,23},{8,24},{9,25},... | collective-permute-start | bytes 1572872 | tf_op jit(solution)/shard_map/ppermute | solution.py:40
  43.7 4.7 %collective-permute-start.9 = (bf16[128,2048]{1,0:T(8,128)(2,1)}, bf16[128,2048]{1,0:T(8,128)(2,1)}, u32[]{:S(2)}, u32[]{:S(2)}) collective-permute-start(bf16[128,2048]{1,0:T(8,128)(2,1)} %collective-permute-done.2.refs_2_.refs_1_.refs_3_), channel_id=1, source_target_pairs={{0,1},{1,0},{2,3},{3,2},{4,5},{5,4},{6,7},{7,6},{8,9},{9,8},{10,11... | collective-permute-start | bytes 1572872 | tf_op jit(solution)/shard_map/ppermute | solution.py:40
  43.8 4.7 %collective-permute-start.10 = (bf16[128,2048]{1,0:T(8,128)(2,1)}, bf16[128,2048]{1,0:T(8,128)(2,1)}, u32[]{:S(2)}, u32[]{:S(2)}) collective-permute-start(bf16[128,2048]{1,0:T(8,128)(2,1)} %collective-permute-done.6.refs_5_.refs_9_), channel_id=1, source_target_pairs={{0,1},{1,0},{2,3},{3,2},{4,5},{5,4},{6,7},{7,6},{8,9},{9,8},{10,11... | collective-permute-start | bytes 1572872 | tf_op jit(solution)/shard_map/ppermute | solution.py:40
  48.4 30.5 %collective-permute-start.17 = (bf16[224,2048]{1,0:T(8,128)(2,1)}, bf16[224,2048]{1,0:T(8,128)(2,1)}, u32[]{:S(2)}, u32[]{:S(2)}) collective-permute-start(bf16[224,2048]{1,0:T(8,128)(2,1)} %get-tuple-element.836), channel_id=1, source_target_pairs={{4,0},{8,12},{5,1},{9,13},{6,2},{10,14},{7,3},{11,15},{20,16},{24,... | collective-permute-start | bytes 2752520 | tf_op jit(solution)/shard_map/ppermute | solution.py:57
  49.7 6.1 %collective-permute-start.12 = (bf16[128,2048]{1,0:T(8,128)(2,1)}, bf16[128,2048]{1,0:T(8,128)(2,1)}, u32[]{:S(2)}, u32[]{:S(2)}) collective-permute-start(bf16[128,2048]{1,0:T(8,128)(2,1)} %collective-permute-done.8.refs_3_.refs_7_), channel_id=1, source_target_pairs={{0,1},{1,0},{2,3},{3,2},{4,5},{5,4},{6,7},{7,6},{8,9},{9,8},{10,11... | collective-permute-start | bytes 1572872 | tf_op jit(solution)/shard_map/ppermute | solution.py:40
  55.8 3.6 %collective-permute-start.14 = (bf16[128,2048]{1,0:T(8,128)(2,1)}, bf16[128,2048]{1,0:T(8,128)(2,1)}, u32[]{:S(2)}, u32[]{:S(2)}) collective-permute-start(bf16[128,2048]{1,0:T(8,128)(2,1)} %collective-permute-done.11.refs_7_.refs_5_), channel_id=1, source_target_pairs={{0,1},{1,0},{2,3},{3,2},{4,5},{5,4},{6,7},{7,6},{8,9},{9,8},{10,11... | collective-permute-start | bytes 1572872 | tf_op jit(solution)/shard_map/ppermute | solution.py:40
  61.4 3.5 %collective-permute-start.15 = (bf16[384,128]{1,0:T(8,128)(2,1)}, bf16[384,128]{1,0:T(8,128)(2,1)}, u32[]{:S(2)}, u32[]{:S(2)}) collective-permute-start(bf16[384,128]{1,0:T(8,128)(2,1)} %get-tuple-element.1017.refs_0_), channel_id=1, source_target_pairs={{0,1},{1,0},{2,3},{3,2},{4,8},{5,9},{6,10},{7,11},{8,4},{9,5},{10,... | collective-permute-start | bytes 294920 | tf_op jit(solution)/shard_map/ppermute | solution.py:40
  61.5 17.5 %collective-permute-start.16 = (bf16[128,2048]{1,0:T(8,128)(2,1)}, bf16[128,2048]{1,0:T(8,128)(2,1)}, u32[]{:S(2)}, u32[]{:S(2)}) collective-permute-start(bf16[128,2048]{1,0:T(8,128)(2,1)} %get-tuple-element.943), channel_id=1, source_target_pairs={{0,1},{1,0},{2,3},{3,2},{4,8},{5,9},{6,10},{7,11},{8,4},{9,5},{10,... | collective-permute-start | bytes 1572872 | tf_op jit(solution)/shard_map/ppermute | solution.py:40
  62.0 17.0 %collective-permute-start.18 = (bf16[2,128,1024]{2,1,0:T(8,128)(2,1)}, bf16[2,128,1024]{2,1,0:T(8,128)(2,1)}, u32[]{:S(2)}, u32[]{:S(2)}) collective-permute-start(bf16[2,128,1024]{2,1,0:T(8,128)(2,1)} %param.13), channel_id=1, source_target_pairs={{0,2},{2,0},{1,3},{3,1},{4,6},{6,4},{5,7},{7,5},{8,10},{10,8},{9,1... | collective-permute-start | bytes 1572872 | tf_op jit(solution)/shard_map/ppermute | solution.py:30
  65.0 26.2 %collective-permute-start.21 = (bf16[256,1024]{1,0:T(8,128)(2,1)}, bf16[256,1024]{1,0:T(8,128)(2,1)}, u32[]{:S(2)}, u32[]{:S(2)}) collective-permute-start(bf16[256,1024]{1,0:T(8,128)(2,1)} %get-tuple-element.990), channel_id=1, source_target_pairs={{4,0},{8,12},{5,1},{9,13},{6,2},{10,14},{7,3},{11,15},{20,16},{24,... | collective-permute-start | bytes 1572872 | tf_op jit(solution)/shard_map/ppermute | solution.py:57
  67.9 23.3 %collective-permute-start.22 = (bf16[384,128]{1,0:T(8,128)(2,1)}, bf16[384,128]{1,0:T(8,128)(2,1)}, u32[]{:S(2)}, u32[]{:S(2)}) collective-permute-start(bf16[384,128]{1,0:T(8,128)(2,1)} %get-tuple-element.1098.refs_0_), channel_id=1, source_target_pairs={{4,0},{8,12},{5,1},{9,13},{6,2},{10,14},{7,3},{11,15},{20,16},{24,... | collective-permute-start | bytes 294920 | tf_op jit(solution)/shard_map/ppermute | solution.py:57
  78.9 2.3 %collective-permute-start.19 = (bf16[2,128,1024]{2,1,0:T(8,128)(2,1)}, bf16[2,128,1024]{2,1,0:T(8,128)(2,1)}, u32[]{:S(2)}, u32[]{:S(2)}) collective-permute-start(bf16[2,128,1024]{2,1,0:T(8,128)(2,1)} %param.13), channel_id=1, source_target_pairs={{0,1},{1,0},{2,3},{3,2},{4,5},{5,4},{6,7},{7,6},{8,9},{9,8},{10,11... | collective-permute-start | bytes 1572872 | tf_op jit(solution)/shard_map/ppermute | solution.py:30
  79.0 3.0 %collective-permute-start.20 = (bf16[2,128,1024]{2,1,0:T(8,128)(2,1)}, bf16[2,128,1024]{2,1,0:T(8,128)(2,1)}, u32[]{:S(2)}, u32[]{:S(2)}) collective-permute-start(bf16[2,128,1024]{2,1,0:T(8,128)(2,1)} %collective-permute-done.18), channel_id=1, source_target_pairs={{0,1},{1,0},{2,3},{3,2},{4,5},{5,4},{6,7},{7,6},{8,9},{9,8},{10,11... | collective-permute-start | bytes 1572872 | tf_op jit(solution)/shard_map/ppermute | solution.py:30
  81.9 14.2 %collective-permute-start.23 = (bf16[128,1024]{1,0:T(8,128)(2,1)}, bf16[128,1024]{1,0:T(8,128)(2,1)}, u32[]{:S(2)}, u32[]{:S(2)}) collective-permute-start(bf16[128,1024]{1,0:T(8,128)(2,1)} %get-tuple-element.1079), channel_id=1, source_target_pairs={{4,0},{8,12},{5,1},{9,13},{6,2},{10,14},{7,3},{11,15},{20,16},{24,... | collective-permute-start | bytes 786440 | tf_op jit(solution)/shard_map/ppermute | solution.py:57
  (12 other events, 18.1 us)

commit v7 on v6

--- a/solution.py
+++ b/solution.py
@@ -609,7 +609,7 @@
 
 
 def last_finished(held, out, late, term, layout):
-    kept = [held[n] for n in sorted(held) if n.startswith("lent")]
+    kept = []
     cut, last = layout.sizes
 
     def body(out_ref, late_ref, term_ref, *refs):

time: 99.3 us -> 99.3 us (level)
  no operation moved by 1% of the time
where the time goes in v7:
time: 99.3 us; the launch traced here: 98.7 us
  Pallas kernels  41.8 us (42%)
  waiting for transfers between devices  32.7 us (33%)
  starting transfers between devices  17.4 us (18%)
  local copies, waits for them, and re-layouts  5.88 us (6%)
    pallas_call x55, Pallas kernels, call(): pl.pallas_call(counted, out_shape=[*shapes, jax.ShapeDtypeStruct(tick.sha...  41.8 us
    ppermute x7, waiting for transfers between devices, hop(): return lax.ppermute(x, 'tensor', pairs)  18.4 us
    ppermute x6, waiting for transfers between devices, swap(): return lax.ppermute(x, axis, [(0, 1), (1, 0)])  12.2 us
    ppermute x7, starting transfers between devices, hop(): return lax.ppermute(x, 'tensor', pairs)  10.3 us
    unnamed x24, local copies, waits for them, and re-layouts  5.88 us
    ppermute x6, starting transfers between devices, swap(): return lax.ppermute(x, axis, [(0, 1), (1, 0)])  4.48 us
    ppermute x11, starting transfers between devices, inside(): return lax.ppermute(x, AXES, pairs)  2.61 us
    ppermute x11, waiting for transfers between devices, inside(): return lax.ppermute(x, AXES, pairs)  2.13 us
  transfers between devices with their start and end apart: 24, of which 11 were waited for; matrix products, arithmetic and copies ran while one was open for 0% of the time, Pallas kernels for 40%

profile of v7, /device:TPU:0, one launch (start us, length us, event | category | flops | bytes accessed | tf_op | source)
XLA Modules:
  0.0 98.7 jit_solution(6478107197123940593)
XLA Ops:
  1.9 1.8 %shard_map.73 = (bf16[128,2048]{1,0:T(8,128)(2,1)}, f32[8,128]{1,0:T(8,128)S(1)}) custom-call(bf16[384,2048]{1,0:T(8,128)(2,1)S(1)} %copy-done.3, bf16[8192,1024]{1,0:T(8,128)(2,1)} %refs_13_.1, f32[8,128]{1,0:T(8,128)S(1)} %broadcast_in_dim.34.refs_2_), custom_call_target="tpu_custom_call" | custom-call | flops 999999995904 | tf_op jit(solution)/shard_map/pallas_call | solution.py:77
  3.7 3.3 %collective-permute-start.2 = (bf16[128,2048]{1,0:T(8,128)(2,1)}, bf16[128,2048]{1,0:T(8,128)(2,1)}, u32[]{:S(2)}, u32[]{:S(2)}) collective-permute-start(bf16[128,2048]{1,0:T(8,128)(2,1)} %get-tuple-element.590), channel_id=1, source_target_pairs={{0,4},{4,0},{8,12},{12,8},{1,5},{5,1},{9,13},{13,9},{2,6},{6,2},{1... | collective-permute-start | bytes 1572872 | tf_op jit(solution)/shard_map/ppermute | solution.py:57
  7.0 1.5 %collective-permute-start.3 = (bf16[2,128,2048]{2,1,0:T(8,128)(2,1)}, bf16[2,128,2048]{2,1,0:T(8,128)(2,1)}, u32[]{:S(2)}, u32[]{:S(2)}) collective-permute-start(bf16[2,128,2048]{2,1,0:T(8,128)(2,1)} %param.12), channel_id=1, source_target_pairs={{0,2},{2,0},{1,3},{3,1},{4,6},{6,4},{5,7},{7,5},{8,10},{10,8},{9,1... | collective-permute-start | bytes 3145736 | tf_op jit(solution)/shard_map/ppermute | solution.py:30
  9.6 1.9 %collective-permute-done.1 = bf16[2,128,2048]{2,1,0:T(8,128)(2,1)} collective-permute-done((bf16[2,128,2048]{2,1,0:T(8,128)(2,1)}, bf16[2,128,2048]{2,1,0:T(8,128)(2,1)}, u32[]{:S(2)}, u32[]{:S(2)}) %collective-permute-start.1) | collective-permute-done | bytes 1048608 | tf_op jit(solution)/shard_map/ppermute | solution.py:30
  11.6 3.8 %shard_map.81 = (f32[384,1024]{1,0:T(8,128)S(1)}, f32[8,128]{1,0:T(8,128)S(1)}) custom-call(bf16[384,2048]{1,0:T(8,128)(2,1)S(1)} %copy-done.3, bf16[8192,1024]{1,0:T(8,128)(2,1)} %refs_13_.1, f32[8,128]{1,0:T(8,128)S(1)} %shard_map.80.refs_2_), custom_call_target="tpu_custom_call" | custom-call | flops 999999995904 | tf_op jit(solution)/shard_map/pallas_call | solution.py:77
  16.9 3.2 %collective-permute-done.2.refs_2_.refs_1_ = bf16[128,2048]{1,0:T(8,128)(2,1)} collective-permute-done((bf16[128,2048]{1,0:T(8,128)(2,1)}, bf16[128,2048]{1,0:T(8,128)(2,1)}, u32[]{:S(2)}, u32[]{:S(2)}) %collective-permute-start.2) | collective-permute-done | bytes 524320 | tf_op jit(solution)/shard_map/ppermute | solution.py:57
  20.1 3.2 %shard_map.84 = (f32[384,128]{1,0:T(8,128)S(1)}, bf16[384,128]{1,0:T(8,128)(2,1)}, f32[8,128]{1,0:T(8,128)S(1)}) custom-call(s32[384,128]{1,0:T(8,128)S(1)} %fusion.refs_0_.refs_1_.refs_4_, bf16[384,2048]{1,0:T(8,128)(2,1)S(1)} %copy-done.3, bf16[256,2048]{1,0:T(8,128)(2,1)} %bitcast.refs_2_, bf16[256,2048]{1,0:T(8,128)(2,1)} %bitcast.1.refs_3_, ...), custom_call_target="tpu_custom_call" | custom-call | flops 999999995904 | tf_op jit(solution)/shard_map/pallas_call | solution.py:77
  23.3 8.3 %collective-permute-done.3 = bf16[2,128,2048]{2,1,0:T(8,128)(2,1)} collective-permute-done((bf16[2,128,2048]{2,1,0:T(8,128)(2,1)}, bf16[2,128,2048]{2,1,0:T(8,128)(2,1)}, u32[]{:S(2)}, u32[]{:S(2)}) %collective-permute-start.3) | collective-permute-done | bytes 1048608 | tf_op jit(solution)/shard_map/ppermute | solution.py:30
  32.6 2.5 %shard_map.88 = (f32[384,128]{1,0:T(8,128)S(1)}, bf16[384,128]{1,0:T(8,128)(2,1)}, f32[8,128]{1,0:T(8,128)S(1)}) custom-call(s32[384,128]{1,0:T(8,128)S(1)} %copy-done.1, bf16[384,2048]{1,0:T(8,128)(2,1)S(1)} %copy-done.3, bf16[256,2048]{1,0:T(8,128)(2,1)} %bitcast.2.refs_2_, f32[384,128]{1,0:T(8,128)S(1)} %get-tuple-element.646.refs_3_, ...), custom_call_target="tpu_custom_call" | custom-call | flops 999999995904 | tf_op jit(solution)/shard_map/pallas_call | solution.py:77
  35.4 2.5 %shard_map.90 = (f32[384,128]{1,0:T(8,128)S(1)}, bf16[384,128]{1,0:T(8,128)(2,1)}, f32[8,128]{1,0:T(8,128)S(1)}) custom-call(s32[384,128]{1,0:T(8,128)S(1)} %copy-done.1, bf16[384,2048]{1,0:T(8,128)(2,1)S(1)} %copy-done.3, bf16[256,2048]{1,0:T(8,128)(2,1)} %bitcast.3.refs_2_, f32[384,128]{1,0:T(8,128)S(1)} %get-tuple-element.659.refs_3_, ...), custom_call_target="tpu_custom_call" | custom-call | flops 999999995904 | tf_op jit(solution)/shard_map/pallas_call | solution.py:77
  39.5 1.9 %collective-permute-done.5.refs_3_.refs_11_ = bf16[256,2048]{1,0:T(8,128)(2,1)} collective-permute-done((bf16[256,2048]{1,0:T(8,128)(2,1)}, bf16[256,2048]{1,0:T(8,128)(2,1)}, u32[]{:S(2)}, u32[]{:S(2)}) %collective-permute-start.5) | collective-permute-done | bytes 1048608 | tf_op jit(solution)/shard_map/ppermute | solution.py:57
  41.4 1.7 %collective-permute-start.13 = (bf16[160,2048]{1,0:T(8,128)(2,1)}, bf16[160,2048]{1,0:T(8,128)(2,1)}, u32[]{:S(2)}, u32[]{:S(2)}) collective-permute-start(bf16[160,2048]{1,0:T(8,128)(2,1)} %get-tuple-element.684), channel_id=1, source_target_pairs={{0,4},{4,0},{8,12},{12,8},{1,5},{5,1},{9,13},{13,9},{2,6},{6,2},{1... | collective-permute-start | bytes 1966088 | tf_op jit(solution)/shard_map/ppermute | solution.py:57
  44.2 2.1 %shard_map.99 = (bf16[224,2048]{1,0:T(8,128)(2,1)}, f32[8,128]{1,0:T(8,128)S(1)}) custom-call(bf16[384,2048]{1,0:T(8,128)(2,1)} %collective-permute-done.refs_1_.refs_0_.refs_4_, f32[8,128]{1,0:T(8,128)S(1)} %shard_map.98.refs_1_), custom_call_target="tpu_custom_call" | custom-call | flops 999999995904 | tf_op jit(solution)/shard_map/pallas_call | solution.py:77
  46.3 2.1 %collective-permute-done.10.refs_6_ = bf16[128,2048]{1,0:T(8,128)(2,1)} collective-permute-done((bf16[128,2048]{1,0:T(8,128)(2,1)}, bf16[128,2048]{1,0:T(8,128)(2,1)}, u32[]{:S(2)}, u32[]{:S(2)}) %collective-permute-start.10) | collective-permute-done | bytes 524320 | tf_op jit(solution)/shard_map/ppermute | solution.py:40
  49.9 4.7 %shard_map.103 = (f32[384,1024]{1,0:T(8,128)S(1)}, f32[8,128]{1,0:T(8,128)S(1)}) custom-call(f32[384,1024]{1,0:T(8,128)} %copy-done.6, bf16[8192,1024]{1,0:T(8,128)(2,1)} %refs_13_.1, bf16[128,2048]{1,0:T(8,128)(2,1)} %collective-permute-done.2.refs_2_.refs_1_, bf16[256,2048]{1,0:T(8,128)(2,1)} %collective-permute-done.5.refs_3_.refs_11_, ...), custom_call_target="tpu_custom_call" | custom-call | flops 999999995904 | tf_op jit(solution)/shard_map/pallas_call | solution.py:77
  56.2 3.2 %collective-permute-done.13.refs_1_.refs_7_.refs_12_ = bf16[160,2048]{1,0:T(8,128)(2,1)} collective-permute-done((bf16[160,2048]{1,0:T(8,128)(2,1)}, bf16[160,2048]{1,0:T(8,128)(2,1)}, u32[]{:S(2)}, u32[]{:S(2)}) %collective-permute-start.13) | collective-permute-done | bytes 655392 | tf_op jit(solution)/shard_map/ppermute | solution.py:57
  59.4 2.0 %shard_map.106 = (bf16[384,128]{1,0:T(8,128)(2,1)}, bf16[128,2048]{1,0:T(8,128)(2,1)}, f32[8,128]{1,0:T(8,128)S(1)}) custom-call(f32[384,128]{1,0:T(8,128)S(1)} %copy-done.8, bf16[160,2048]{1,0:T(8,128)(2,1)} %collective-permute-done.13.refs_1_.refs_7_.refs_12_, f32[8,128]{1,0:T(8,128)S(1)} %shard_map.105.refs_2_), custom_call_target="tpu_custom_call" | custom-call | flops 999999995904 | tf_op jit(solution)/shard_map/pallas_call | solution.py:77
  62.0 2.0 %collective-permute-start.18 = (bf16[2,128,1024]{2,1,0:T(8,128)(2,1)}, bf16[2,128,1024]{2,1,0:T(8,128)(2,1)}, u32[]{:S(2)}, u32[]{:S(2)}) collective-permute-start(bf16[2,128,1024]{2,1,0:T(8,128)(2,1)} %param.13), channel_id=1, source_target_pairs={{0,2},{2,0},{1,3},{3,1},{4,6},{6,4},{5,7},{7,5},{8,10},{10,8},{9,1... | collective-permute-start | bytes 1572872 | tf_op jit(solution)/shard_map/ppermute | solution.py:30
  66.3 1.6 %shard_map.114 = (bf16[384,128]{1,0:T(8,128)(2,1)}, f32[8,128]{1,0:T(8,128)S(1)}) custom-call(bf16[384,128]{1,0:T(8,128)(2,1)} %get-tuple-element.969.refs_0_, bf16[384,128]{1,0:T(8,128)(2,1)} %collective-permute-done.15.refs_1_, f32[8,128]{1,0:T(8,128)S(1)} %shard_map.113.refs_2_), custom_call_target="tpu_custom_call" | custom-call | flops 999999995904 | tf_op jit(solution)/shard_map/pallas_call | solution.py:77
  69.2 9.7 %collective-permute-done.17.refs_8_ = bf16[224,2048]{1,0:T(8,128)(2,1)} collective-permute-done((bf16[224,2048]{1,0:T(8,128)(2,1)}, bf16[224,2048]{1,0:T(8,128)(2,1)}, u32[]{:S(2)}, u32[]{:S(2)}) %collective-permute-start.17) | collective-permute-done | bytes 917536 | tf_op jit(solution)/shard_map/ppermute | solution.py:57
  81.9 1.4 %collective-permute-start.23 = (bf16[128,1024]{1,0:T(8,128)(2,1)}, bf16[128,1024]{1,0:T(8,128)(2,1)}, u32[]{:S(2)}, u32[]{:S(2)}) collective-permute-start(bf16[128,1024]{1,0:T(8,128)(2,1)} %get-tuple-element.1031), channel_id=1, source_target_pairs={{4,0},{8,12},{5,1},{9,13},{6,2},{10,14},{7,3},{11,15},{20,16},{24,... | collective-permute-start | bytes 786440 | tf_op jit(solution)/shard_map/ppermute | solution.py:57
  83.4 7.5 %shard_map.121 = (bf16[384,1024]{1,0:T(8,128)(2,1)}, f32[384,1024]{1,0:T(8,128)}, f32[8,128]{1,0:T(8,128)S(1)}) custom-call(bf16[384,128]{1,0:T(8,128)(2,1)} %get-tuple-element.1042.refs_0_, s32[384,128]{1,0:T(8,128)S(1)} %copy-done.2, bf16[256,1024]{1,0:T(8,128)(2,1)} %bitcast.4.refs_2_, bf16[256,1024]{1,0:T(8,128)(2,1)} %bitcast.5.refs_3_, ...), custom_call_target="tpu_custom_call" | custom-call | flops 999999995904 | tf_op jit(solution)/shard_map/pallas_call | solution.py:77
  92.2 3.9 %shard_map.124 = (bf16[384,1024]{1,0:T(8,128)(2,1)}, f32[128,1024]{1,0:T(8,128)S(1)}, f32[8,128]{1,0:T(8,128)S(1)}) custom-call(bf16[384,1024]{1,0:T(8,128)(2,1)} %get-tuple-element.1055.refs_0_, f32[384,1024]{1,0:T(8,128)S(1)} %copy-done.5, bf16[256,1024]{1,0:T(8,128)(2,1)} %collective-permute-done.21.refs_2_, ...), custom_call_target="tpu_custom_call", output_to_operand_aliasing={{0}: (0, {})} | custom-call | flops 999999995904 | tf_op jit(solution)/shard_map/pallas_call | solution.py:77
  96.2 2.4 %shard_map.127 = (bf16[384,1024]{1,0:T(8,128)(2,1)}, f32[8,128]{1,0:T(8,128)}) custom-call(bf16[384,1024]{1,0:T(8,128)(2,1)} %get-tuple-element.1072.refs_0_, f32[128,1024]{1,0:T(8,128)S(1)} %get-tuple-element.1073.refs_1_, bf16[128,1024]{1,0:T(8,128)(2,1)} %collective-permute-done.23.refs_2_, ...), custom_call_target="tpu_custom_call", output_to_operand_aliasing={{0}: (0, {})} | custom-call | flops 999999995904 | tf_op jit(solution)/shard_map/pallas_call | solution.py:77
  (107 shorter events, 19.9 us)
Async XLA Ops:
  0.0 37.9 %collective-permute-start = (bf16[384,2048]{1,0:T(8,128)(2,1)}, bf16[384,2048]{1,0:T(8,128)(2,1)}, u32[]{:S(2)}, u32[]{:S(2)}) collective-permute-start(bf16[384,2048]{1,0:T(8,128)(2,1)} %refs_0_.4), channel_id=1, source_target_pairs={{0,1},{1,0},{2,3},{3,2},{4,8},{5,9},{6,10},{7,11},{8,4},{9,5},{10,... | collective-permute-start | bytes 4718600 | tf_op jit(solution)/shard_map/ppermute | solution.py:40
  3.7 16.4 %collective-permute-start.2 = (bf16[128,2048]{1,0:T(8,128)(2,1)}, bf16[128,2048]{1,0:T(8,128)(2,1)}, u32[]{:S(2)}, u32[]{:S(2)}) collective-permute-start(bf16[128,2048]{1,0:T(8,128)(2,1)} %get-tuple-element.590), channel_id=1, source_target_pairs={{0,4},{4,0},{8,12},{12,8},{1,5},{5,1},{9,13},{13,9},{2,6},{6,2},{1... | collective-permute-start | bytes 1572872 | tf_op jit(solution)/shard_map/ppermute | solution.py:57
  7.0 24.7 %collective-permute-start.3 = (bf16[2,128,2048]{2,1,0:T(8,128)(2,1)}, bf16[2,128,2048]{2,1,0:T(8,128)(2,1)}, u32[]{:S(2)}, u32[]{:S(2)}) collective-permute-start(bf16[2,128,2048]{2,1,0:T(8,128)(2,1)} %param.12), channel_id=1, source_target_pairs={{0,2},{2,0},{1,3},{3,1},{4,6},{6,4},{5,7},{7,5},{8,10},{10,8},{9,1... | collective-permute-start | bytes 3145736 | tf_op jit(solution)/shard_map/ppermute | solution.py:30
  8.5 3.0 %collective-permute-start.1 = (bf16[2,128,2048]{2,1,0:T(8,128)(2,1)}, bf16[2,128,2048]{2,1,0:T(8,128)(2,1)}, u32[]{:S(2)}, u32[]{:S(2)}) collective-permute-start(bf16[2,128,2048]{2,1,0:T(8,128)(2,1)} %param.12), channel_id=1, source_target_pairs={{0,1},{1,0},{2,3},{3,2},{4,5},{5,4},{6,7},{7,6},{8,9},{9,8},{10,11... | collective-permute-start | bytes 3145736 | tf_op jit(solution)/shard_map/ppermute | solution.py:30
  11.5 29.9 %collective-permute-start.5 = (bf16[256,2048]{1,0:T(8,128)(2,1)}, bf16[256,2048]{1,0:T(8,128)(2,1)}, u32[]{:S(2)}, u32[]{:S(2)}) collective-permute-start(bf16[256,2048]{1,0:T(8,128)(2,1)} %get-tuple-element.591), channel_id=1, source_target_pairs={{0,4},{4,0},{8,12},{12,8},{1,5},{5,1},{9,13},{13,9},{2,6},{6,2},{1... | collective-permute-start | bytes 3145736 | tf_op jit(solution)/shard_map/ppermute | solution.py:57
  20.1 19.4 %collective-permute-start.6 = (bf16[128,2048]{1,0:T(8,128)(2,1)}, bf16[128,2048]{1,0:T(8,128)(2,1)}, u32[]{:S(2)}, u32[]{:S(2)}) collective-permute-start(bf16[128,2048]{1,0:T(8,128)(2,1)} %collective-permute-done.2.refs_2_.refs_1_), channel_id=1, source_target_pairs={{0,1},{1,0},{2,3},{3,2},{4,20},{5,21},{6,22},{7,23},{8,24},{9,25},... | collective-permute-start | bytes 1572872 | tf_op jit(solution)/shard_map/ppermute | solution.py:40
  31.6 11.5 %collective-permute-start.8 = (bf16[128,2048]{1,0:T(8,128)(2,1)}, bf16[128,2048]{1,0:T(8,128)(2,1)}, u32[]{:S(2)}, u32[]{:S(2)}) collective-permute-start(bf16[128,2048]{1,0:T(8,128)(2,1)} %collective-permute-done.2.refs_2_.refs_1_), channel_id=1, source_target_pairs={{0,1},{1,0},{2,3},{3,2},{4,6},{5,7},{6,4},{7,5},{8,10},{9,11},{10,... | collective-permute-start | bytes 1572872 | tf_op jit(solution)/shard_map/ppermute | solution.py:40
  31.7 3.7 %collective-permute-start.4 = (bf16[2,128,2048]{2,1,0:T(8,128)(2,1)}, bf16[2,128,2048]{2,1,0:T(8,128)(2,1)}, u32[]{:S(2)}, u32[]{:S(2)}) collective-permute-start(bf16[2,128,2048]{2,1,0:T(8,128)(2,1)} %collective-permute-done.3), channel_id=1, source_target_pairs={{0,1},{1,0},{2,3},{3,2},{4,5},{5,4},{6,7},{7,6},{8,9},{9,8},{10,11... | collective-permute-start | bytes 3145736 | tf_op jit(solution)/shard_map/ppermute | solution.py:30
  41.4 18.0 %collective-permute-start.13 = (bf16[160,2048]{1,0:T(8,128)(2,1)}, bf16[160,2048]{1,0:T(8,128)(2,1)}, u32[]{:S(2)}, u32[]{:S(2)}) collective-permute-start(bf16[160,2048]{1,0:T(8,128)(2,1)} %get-tuple-element.684), channel_id=1, source_target_pairs={{0,4},{4,0},{8,12},{12,8},{1,5},{5,1},{9,13},{13,9},{2,6},{6,2},{1... | collective-permute-start | bytes 1966088 | tf_op jit(solution)/shard_map/ppermute | solution.py:57
  43.2 20.8 %collective-permute-start.7 = (bf16[256,2048]{1,0:T(8,128)(2,1)}, bf16[256,2048]{1,0:T(8,128)(2,1)}, u32[]{:S(2)}, u32[]{:S(2)}) collective-permute-start(bf16[256,2048]{1,0:T(8,128)(2,1)} %collective-permute-done.5.refs_3_.refs_11_), channel_id=1, source_target_pairs={{0,1},{1,0},{2,3},{3,2},{4,8},{5,9},{6,10},{7,11},{8,4},{9,5},{10,... | collective-permute-start | bytes 3145736 | tf_op jit(solution)/shard_map/ppermute | solution.py:40
  43.2 12.6 %collective-permute-start.11 = (bf16[128,2048]{1,0:T(8,128)(2,1)}, bf16[128,2048]{1,0:T(8,128)(2,1)}, u32[]{:S(2)}, u32[]{:S(2)}) collective-permute-start(bf16[128,2048]{1,0:T(8,128)(2,1)} %collective-permute-done.8.refs_3_), channel_id=1, source_target_pairs={{0,1},{1,0},{2,3},{3,2},{4,20},{5,21},{6,22},{7,23},{8,24},{9,25},... | collective-permute-start | bytes 1572872 | tf_op jit(solution)/shard_map/ppermute | solution.py:40
  43.7 4.7 %collective-permute-start.9 = (bf16[128,2048]{1,0:T(8,128)(2,1)}, bf16[128,2048]{1,0:T(8,128)(2,1)}, u32[]{:S(2)}, u32[]{:S(2)}) collective-permute-start(bf16[128,2048]{1,0:T(8,128)(2,1)} %collective-permute-done.2.refs_2_.refs_1_), channel_id=1, source_target_pairs={{0,1},{1,0},{2,3},{3,2},{4,5},{5,4},{6,7},{7,6},{8,9},{9,8},{10,11... | collective-permute-start | bytes 1572872 | tf_op jit(solution)/shard_map/ppermute | solution.py:40
  43.8 4.7 %collective-permute-start.10 = (bf16[128,2048]{1,0:T(8,128)(2,1)}, bf16[128,2048]{1,0:T(8,128)(2,1)}, u32[]{:S(2)}, u32[]{:S(2)}) collective-permute-start(bf16[128,2048]{1,0:T(8,128)(2,1)} %collective-permute-done.6.refs_5_), channel_id=1, source_target_pairs={{0,1},{1,0},{2,3},{3,2},{4,5},{5,4},{6,7},{7,6},{8,9},{9,8},{10,11... | collective-permute-start | bytes 1572872 | tf_op jit(solution)/shard_map/ppermute | solution.py:40
  48.4 30.5 %collective-permute-start.17 = (bf16[224,2048]{1,0:T(8,128)(2,1)}, bf16[224,2048]{1,0:T(8,128)(2,1)}, u32[]{:S(2)}, u32[]{:S(2)}) collective-permute-start(bf16[224,2048]{1,0:T(8,128)(2,1)} %get-tuple-element.788), channel_id=1, source_target_pairs={{4,0},{8,12},{5,1},{9,13},{6,2},{10,14},{7,3},{11,15},{20,16},{24,... | collective-permute-start | bytes 2752520 | tf_op jit(solution)/shard_map/ppermute | solution.py:57
  49.7 6.1 %collective-permute-start.12 = (bf16[128,2048]{1,0:T(8,128)(2,1)}, bf16[128,2048]{1,0:T(8,128)(2,1)}, u32[]{:S(2)}, u32[]{:S(2)}) collective-permute-start(bf16[128,2048]{1,0:T(8,128)(2,1)} %collective-permute-done.8.refs_3_), channel_id=1, source_target_pairs={{0,1},{1,0},{2,3},{3,2},{4,5},{5,4},{6,7},{7,6},{8,9},{9,8},{10,11... | collective-permute-start | bytes 1572872 | tf_op jit(solution)/shard_map/ppermute | solution.py:40
  55.8 3.6 %collective-permute-start.14 = (bf16[128,2048]{1,0:T(8,128)(2,1)}, bf16[128,2048]{1,0:T(8,128)(2,1)}, u32[]{:S(2)}, u32[]{:S(2)}) collective-permute-start(bf16[128,2048]{1,0:T(8,128)(2,1)} %collective-permute-done.11.refs_7_), channel_id=1, source_target_pairs={{0,1},{1,0},{2,3},{3,2},{4,5},{5,4},{6,7},{7,6},{8,9},{9,8},{10,11... | collective-permute-start | bytes 1572872 | tf_op jit(solution)/shard_map/ppermute | solution.py:40
  61.4 3.6 %collective-permute-start.15 = (bf16[384,128]{1,0:T(8,128)(2,1)}, bf16[384,128]{1,0:T(8,128)(2,1)}, u32[]{:S(2)}, u32[]{:S(2)}) collective-permute-start(bf16[384,128]{1,0:T(8,128)(2,1)} %get-tuple-element.969.refs_0_), channel_id=1, source_target_pairs={{0,1},{1,0},{2,3},{3,2},{4,8},{5,9},{6,10},{7,11},{8,4},{9,5},{10,... | collective-permute-start | bytes 294920 | tf_op jit(solution)/shard_map/ppermute | solution.py:40
  61.5 17.4 %collective-permute-start.16 = (bf16[128,2048]{1,0:T(8,128)(2,1)}, bf16[128,2048]{1,0:T(8,128)(2,1)}, u32[]{:S(2)}, u32[]{:S(2)}) collective-permute-start(bf16[128,2048]{1,0:T(8,128)(2,1)} %get-tuple-element.895), channel_id=1, source_target_pairs={{0,1},{1,0},{2,3},{3,2},{4,8},{5,9},{6,10},{7,11},{8,4},{9,5},{10,... | collective-permute-start | bytes 1572872 | tf_op jit(solution)/shard_map/ppermute | solution.py:40
  62.0 16.9 %collective-permute-start.18 = (bf16[2,128,1024]{2,1,0:T(8,128)(2,1)}, bf16[2,128,1024]{2,1,0:T(8,128)(2,1)}, u32[]{:S(2)}, u32[]{:S(2)}) collective-permute-start(bf16[2,128,1024]{2,1,0:T(8,128)(2,1)} %param.13), channel_id=1, source_target_pairs={{0,2},{2,0},{1,3},{3,1},{4,6},{6,4},{5,7},{7,5},{8,10},{10,8},{9,1... | collective-permute-start | bytes 1572872 | tf_op jit(solution)/shard_map/ppermute | solution.py:30
  65.0 26.2 %collective-permute-start.21 = (bf16[256,1024]{1,0:T(8,128)(2,1)}, bf16[256,1024]{1,0:T(8,128)(2,1)}, u32[]{:S(2)}, u32[]{:S(2)}) collective-permute-start(bf16[256,1024]{1,0:T(8,128)(2,1)} %get-tuple-element.942), channel_id=1, source_target_pairs={{4,0},{8,12},{5,1},{9,13},{6,2},{10,14},{7,3},{11,15},{20,16},{24,... | collective-permute-start | bytes 1572872 | tf_op jit(solution)/shard_map/ppermute | solution.py:57
  67.9 23.3 %collective-permute-start.22 = (bf16[384,128]{1,0:T(8,128)(2,1)}, bf16[384,128]{1,0:T(8,128)(2,1)}, u32[]{:S(2)}, u32[]{:S(2)}) collective-permute-start(bf16[384,128]{1,0:T(8,128)(2,1)} %get-tuple-element.1042.refs_0_), channel_id=1, source_target_pairs={{4,0},{8,12},{5,1},{9,13},{6,2},{10,14},{7,3},{11,15},{20,16},{24,... | collective-permute-start | bytes 294920 | tf_op jit(solution)/shard_map/ppermute | solution.py:57
  78.9 2.3 %collective-permute-start.19 = (bf16[2,128,1024]{2,1,0:T(8,128)(2,1)}, bf16[2,128,1024]{2,1,0:T(8,128)(2,1)}, u32[]{:S(2)}, u32[]{:S(2)}) collective-permute-start(bf16[2,128,1024]{2,1,0:T(8,128)(2,1)} %param.13), channel_id=1, source_target_pairs={{0,1},{1,0},{2,3},{3,2},{4,5},{5,4},{6,7},{7,6},{8,9},{9,8},{10,11... | collective-permute-start | bytes 1572872 | tf_op jit(solution)/shard_map/ppermute | solution.py:30
  78.9 3.0 %collective-permute-start.20 = (bf16[2,128,1024]{2,1,0:T(8,128)(2,1)}, bf16[2,128,1024]{2,1,0:T(8,128)(2,1)}, u32[]{:S(2)}, u32[]{:S(2)}) collective-permute-start(bf16[2,128,1024]{2,1,0:T(8,128)(2,1)} %collective-permute-done.18), channel_id=1, source_target_pairs={{0,1},{1,0},{2,3},{3,2},{4,5},{5,4},{6,7},{7,6},{8,9},{9,8},{10,11... | collective-permute-start | bytes 1572872 | tf_op jit(solution)/shard_map/ppermute | solution.py:30
  81.9 14.3 %collective-permute-start.23 = (bf16[128,1024]{1,0:T(8,128)(2,1)}, bf16[128,1024]{1,0:T(8,128)(2,1)}, u32[]{:S(2)}, u32[]{:S(2)}) collective-permute-start(bf16[128,1024]{1,0:T(8,128)(2,1)} %get-tuple-element.1031), channel_id=1, source_target_pairs={{4,0},{8,12},{5,1},{9,13},{6,2},{10,14},{7,3},{11,15},{20,16},{24,... | collective-permute-start | bytes 786440 | tf_op jit(solution)/shard_map/ppermute | solution.py:57
  (12 other events, 18.3 us)
